TPU v7x, 512 devices: a whole 4x4x16 slice. The times are simulated.
512 devices in a mesh: ctx: 8 (over y, x_hi), tp: 32 (over z, core), store: 2 (over x_lo).
Axes of the slice: x: 4 (x_hi: 2, x_lo: 2; x = x_hi * 2 + x_lo), y: 4, z: 16, core: 2. Of those that a mesh axis runs over, the one named last changes fastest.
Arguments:
- query_nope: bfloat16 [4, 1024, 16384], P(None, 'ctx', ('tp', 'store')), may hold values from -4.5 to 4.5
- query_rope: bfloat16 [4, 1024, 8192], P(None, 'ctx', ('tp', 'store')), may hold values from -400 to 400
- key_up: bfloat16 [128, 128, 512], P(('tp', 'store')), may hold values from -0.5 to 0.5
- value_up: bfloat16 [128, 512, 128], P(('tp', 'store')), may hold values from -6 to 6
- new_latent: bfloat16 [4, 1024, 512], P(None, 'ctx'), may hold values from -6 to 6
- new_rope: bfloat16 [4, 1024, 64], P(None, 'ctx'), may hold values from -6 to 6
- cache_latent: bfloat16 [512, 64, 512], P(('ctx', 'store')), may hold values from -6 to 6
- cache_rope: bfloat16 [512, 64, 64], P(('ctx', 'store')), may hold values from -6 to 6
- block_owner: int32 [4, 24], replicated, may hold values from 0 to 15, as said below
- block_slot: int32 [4, 24], replicated, may hold values from 0 to 31
- cached_len: int32 [4], replicated, may hold values from 1 to 1536, as said below
Outputs:
- attended: bfloat16 [4, 1024, 16384], P(None, 'ctx', ('tp', 'store'))
Inputs may be any that keep to these rules, and one draw needn't show every extreme that they name: block_owner[s, j] is the holder (index over ctx, then store) of block j of sequence s; no two table entries name the same pool block; a holder holds at most 9 blocks named in the tables, and some holder exactly 9. `cached_len`: some sequence has exactly 1536 cached tokens.
All inputs are finite; a program needn't handle non-finite values.
Results may differ from a plain program's by a relative error of at most 0.008.
Values may be sent and summed in bfloat16 or wider, within the bound.
No kernel may reach another device: no remote copies, remote signals or barrier semaphores. Data moves between devices by JAX's collectives and lax.ppermute only.
A program may use at most 128 MiB of HBM per device.

v0:
```python
import jax
import jax.numpy as jnp
from jax import lax
from jax.sharding import PartitionSpec as P

NEG = -1e30
score_scale = 192.0 ** (-0.5)


def on_device(
    query_nope,
    query_rope,
    key_up,
    value_up,
    new_latent,
    new_rope,
    cache_latent,
    cache_rope,
    block_owner,
    block_slot,
    cached_len,
):
    head_dev = key_up.shape[0]
    nope_width = key_up.shape[1]
    latent_width = key_up.shape[2]
    seq_count = query_nope.shape[0]
    new_dev = query_nope.shape[1]
    rope_width = cache_rope.shape[2]
    block_len = cache_latent.shape[1]
    max_blocks = block_owner.shape[1]
    capacity = 3 * seq_count * (max_blocks // lax.axis_size("ctx")) // (2 * lax.axis_size("store"))
    row_count = new_dev * head_dev
    full_width = latent_width + rope_width
    split_nope = query_nope.reshape(seq_count, new_dev, head_dev, nope_width)
    query_latent = jnp.einsum(
        "sthn,hnl->sthl", split_nope, key_up, preferred_element_type=jnp.float32
    )
    query_latent = query_latent.astype(jnp.bfloat16).reshape(seq_count, row_count, latent_width)
    query_pos = query_rope.reshape(seq_count, row_count, rope_width)
    query_joint = jnp.concatenate([query_latent, query_pos], -1)
    holder = lax.axis_index(("ctx", "store"))
    owner_flat = block_owner.reshape(-1)
    slot_flat = block_slot.reshape(-1)
    entry_count = owner_flat.shape[0]
    entries = jnp.arange(entry_count)
    earlier = entries[None, :] < entries[:, None]
    same_owner = owner_flat[None, :] == owner_flat[:, None]
    owner_rank = jnp.sum((earlier & same_owner).astype(jnp.int32), 1)
    gathered_row = owner_flat * capacity + owner_rank
    owned = owner_flat == holder
    select = (owned[None, :] & (owner_rank[None, :] == jnp.arange(capacity)[:, None])).astype(
        jnp.int32
    )
    slot_pick = jnp.sum(select * slot_flat[None, :], 1)
    joint_pool = jnp.concatenate([cache_latent, cache_rope], -1)
    joint_buf = jnp.take(joint_pool, slot_pick, axis=0)
    query_index = lax.axis_index("ctx") * new_dev + jnp.arange(row_count) // head_dev
    new_joint = jnp.concatenate([new_latent, new_rope], -1)
    running = (
        jnp.full((seq_count, row_count), NEG, jnp.float32),
        jnp.zeros((seq_count, row_count), jnp.float32),
        jnp.zeros((seq_count, row_count, latent_width), jnp.float32),
    )
    blocks_all = lax.all_gather(joint_buf, ("ctx", "store"), axis=0, tiled=True)
    keys = jnp.take(blocks_all, gathered_row, axis=0).reshape(
        seq_count, max_blocks * block_len, full_width
    )
    scores = (
        jnp.einsum("srk,smk->srm", query_joint, keys, preferred_element_type=jnp.float32)
        * score_scale
    )
    positions = jnp.arange(max_blocks * block_len)
    present = positions[None, :] < cached_len[:, None]
    scores = jnp.where(present[:, None, :], scores, NEG)
    run_max, run_sum, run_total = running
    new_max = jnp.maximum(run_max, jnp.max(scores, -1))
    exp_terms = jnp.where(present[:, None, :], jnp.exp(scores - new_max[:, :, None]), 0.0)
    partial_value = jnp.einsum(
        "srm,smk->srk", exp_terms.astype(jnp.bfloat16), keys, preferred_element_type=jnp.float32
    )
    joint_piece = lax.all_gather(new_joint, "ctx", axis=1, tiled=True)
    scores = (
        jnp.einsum("srk,smk->srm", query_joint, joint_piece, preferred_element_type=jnp.float32)
        * score_scale
    )
    key_index = jnp.arange(joint_piece.shape[1])
    present = key_index[None, :] <= query_index[:, None]
    scores = jnp.where(present[None], scores, NEG)
    run_max = new_max
    run_sum = jnp.sum(exp_terms, -1)
    run_total = partial_value[:, :, :latent_width]
    add_new_max = jnp.maximum(run_max, jnp.max(scores, -1))
    add_exp_terms = jnp.where(present[None], jnp.exp(scores - add_new_max[:, :, None]), 0.0)
    add_partial_value = jnp.einsum(
        "srm,smk->srk",
        add_exp_terms.astype(jnp.bfloat16),
        joint_piece,
        preferred_element_type=jnp.float32,
    )
    factor = jnp.exp(run_max - add_new_max)
    running = (
        add_new_max,
        run_sum * factor + jnp.sum(add_exp_terms, -1),
        run_total * factor[:, :, None] + add_partial_value[:, :, :latent_width],
    )
    run_max, run_sum, run_total = running
    mixed = (
        (run_total / run_sum[:, :, None])
        .astype(jnp.bfloat16)
        .reshape(seq_count, new_dev, head_dev, latent_width)
    )
    attended = jnp.einsum(
        "sthl,hlv->sthv", mixed, value_up, preferred_element_type=jnp.float32
    ).astype(jnp.bfloat16)
    return attended.reshape(seq_count, new_dev, head_dev * value_up.shape[2])


def solution(mesh):
    return jax.shard_map(
        on_device,
        mesh=mesh,
        in_specs=(
            P(None, "ctx", ("tp", "store")),
            P(None, "ctx", ("tp", "store")),
            P(("tp", "store"), None, None),
            P(("tp", "store"), None, None),
            P(None, "ctx", None),
            P(None, "ctx", None),
            P(("ctx", "store"), None, None),
            P(("ctx", "store"), None, None),
            P(),
            P(),
            P(),
        ),
        out_specs=P(None, "ctx", ("tp", "store")),
        check_vma=False,
    )
```

profile of v0, /device:TPU:1, one launch (start us, length us, event | category | flops | bytes accessed | tf_op | source)
XLA Modules:
  0.0 265.1 jit_solution(855370665667703206)
XLA Ops:
  6.5 1.4 copy.42
  7.9 1.7 pad_maximum_fusion.4
  9.7 0.8 reshape.163
  10.5 0.8 mul.65
  11.6 2.2 pad_maximum_fusion
  13.8 1.6 gather_fusion
  15.3 2.1 broadcast_select_fusion.1
  18.5 0.8 copy.38
  19.4 0.8 copy.39
  20.8 88.5 %all-gather.5.cloned.1.call-done = bf16[4,1024,576]{1,2,0:T(8,128)(2,1)} async-done(((bf16[4,128,576]{1,2,0:T(8,128)(2,1)}), bf16[4,1024,576]{1,2,0:T(8,128)(2,1)}) %all-gather.5.cloned.1.call-update) | async-done | bytes 4718608 | tf_op jit(solution)/shard_map/all_gather | solution.py:81
  109.3 6.6 %fusion.7 = (f32[4,256]{1,0:T(4,128)S(1)}, f32[4,256,1024]{2,1,0:T(8,128)}) fusion(pred[256,1024]{1,0:T(8,128)(4,1)S(1)} %iota_compare_fusion, bf16[4,1024,576]{1,2,0:T(8,128)(2,1)} %all-gather.5.cloned.1.call-done, bf16[4,256,64]{1,2,0:T(8,128)(2,1)S(1)} %copy.40, bf16[4,256,512]{1,2,0:T(8,128)(2,1)S(1)} %copy.39), kind=kOutput, calls=%fused_computation.14 | convolution fusion | flops 1213463552 | bytes 10358784 | tf_op jit(solution)/shard_map/srk,smk->srm/dot_general | solution.py:83
  115.9 96.6 %all-gather.3.cloned.1.call-done = bf16[144,64,576]{2,1,0:T(8,128)(2,1)} async-done(((bf16[9,64,576]{2,1,0:T(8,128)(2,1)}), bf16[144,64,576]{2,1,0:T(8,128)(2,1)}) %all-gather.3.cloned.1.call-update) | async-done | bytes 10616848 | tf_op jit(solution)/shard_map/all_gather | solution.py:64
  212.5 11.4 %gather_fusion.1 = bf16[96,64,576]{2,1,0:T(8,128)(2,1)} fusion(bf16[144,64,576]{2,1,0:T(8,128)(2,1)} %all-gather.3.cloned.1.call-done, s32[1024]{0:T(1024)S(1)} %pad_clamp_fusion), kind=kCustom, calls=%fused_computation.1 | custom fusion | bytes 14156160 | tf_op jit(solution)/shard_map/jit(_take)/gather | solution.py:65
  223.9 10.2 %copy.41 = bf16[4,1536,576]{1,2,0:T(8,128)(2,1)} copy(bf16[4,1536,576]{2,1,0:T(8,128)(2,1)} %bitcast.35) | data formatting | bytes 14155776 | tf_op jit(solution)/shard_map/jit(_take)/gather | solution.py:65
  234.1 3.7 %broadcast_select_fusion = bf16[4,1536,576]{1,2,0:T(8,128)(2,1)S(1)} fusion(bf16[4,1536,576]{1,2,0:T(8,128)(2,1)} %copy.41, pred[4,1536]{1,0:T(4,128)(4,1)S(1)} %broadcast_in_dim.82), kind=kLoop, calls=%fused_computation.2 | loop fusion | flops 3538944 | bytes 14161920 | tf_op jit(solution)/shard_map/jit(_take)/select_n | solution.py:65
  237.8 4.2 %fusion.2 = (f32[4,256]{1,0:T(4,128)S(1)}, f32[4,256,1536]{2,1,0:T(8,128)S(1)}) fusion(pred[4,1536]{1,0:T(4,128)(4,1)S(1)} %iota_compare_fusion.2, bf16[4,1536,576]{1,2,0:T(8,128)(2,1)S(1)} %broadcast_select_fusion, bf16[4,256,64]{1,2,0:T(8,128)(2,1)S(1)} %copy.40, bf16[4,256,512]{1,2,0:T(8,128)(2,1)} %copy-done.3), kind=kOutput, calls=%fused_computation.7 | convolution fusion | flops 1819016192 | bytes 14559232 | tf_op jit(solution)/shard_map/srk,smk->srm/dot_general | solution.py:69
  242.0 1.7 fusion.3
  243.8 0.4 copy-done.2
  244.2 1.5 fusion.14
  245.7 5.3 %fusion.5 = f32[4,256,512]{2,1,0:T(8,128)} fusion(bf16[4,1024,576]{1,2,0:T(8,128)(2,1)} %all-gather.5.cloned.1.call-done, f32[4,256,1024]{2,1,0:T(8,128)S(1)} %copy-done.2, f32[4,256]{1,0:T(4,128)S(1)} %get-tuple-element.8, pred[256,1024]{1,0:T(8,128)(4,1)S(1)} %iota_compare_fusion), kind=kOutput, calls=%fused_computation.10 | convolution fusion | flops 1078984704 | bytes 10752000 | tf_op jit(solution)/shard_map/srm,smk->srk/dot_general | solution.py:94
  251.0 4.3 %divide_convert_fusion = bf16[4,256,512]{2,1,0:T(8,128)(2,1)} fusion(f32[4,256,512]{2,1,0:T(8,128)} %fusion.5, bf16[4,1536,576]{1,2,0:T(8,128)(2,1)S(1)} %broadcast_select_fusion, f32[4,256,1536]{2,1,0:T(8,128)S(1)} %get-tuple-element.10, f32[4,256]{1,0:T(4,128)S(1)} %get-tuple-element.7, pred[4,1536]{1,0:T(4,128)(4,1)S(1)} %iota_compare_fusion.2, ...), kind=kOutput, calls=%fused_computation.23 | convolution fusion | flops 1620574208 | bytes 15747072 | tf_op jit(solution)/shard_map/srm,smk->srk/dot_general | solution.py:78
  255.4 1.5 reshape.164
  256.8 0.5 fusion.26
  257.4 0.9 copy.46
  (46 shorter events, 2.0 us)
Async XLA Ops:
  6.5 11.4 %copy-start = (bf16[2,128,512]{2,1,0:T(8,128)(2,1)S(1)}, bf16[2,128,512]{2,1,0:T(8,128)(2,1)}, u32[]{:S(2)}) copy-start(bf16[2,128,512]{2,1,0:T(8,128)(2,1)} %param.13) | copy-start | bytes 786436
  6.5 102.8 %all-gather.5.cloned.1.call-start = ((), (), s32[]{:S(2)}) async-start(), calls=%async_computation.1 | async-start | bytes 5308416 | tf_op jit(solution)/shard_map/all_gather | solution.py:81
  9.6 202.9 %all-gather.3.cloned.1.call-start = ((), (), s32[]{:S(2)}) async-start(), calls=%async_computation | async-start | bytes 12533760 | tf_op jit(solution)/shard_map/all_gather | solution.py:64
  11.6 6.0 %copy-start.6 = (s32[4,24]{1,0:T(4,128)S(1)}, s32[4,24]{1,0:T(4,128)}, u32[]{:S(2)}) copy-start(s32[4,24]{1,0:T(4,128)} %param.19) | copy-start | bytes 1156
  11.6 6.3 %copy-start.4 = (bf16[4,128,256]{2,1,0:T(8,128)(2,1)S(1)}, bf16[4,128,256]{2,1,0:T(8,128)(2,1)}, u32[]{:S(2)}) copy-start(bf16[4,128,256]{2,1,0:T(8,128)(2,1)} %param.11) | copy-start | bytes 786436
  18.4 1.8 copy-start.5
  18.4 2.3 copy-start.7
  20.2 95.8 %copy-start.3 = (bf16[4,256,512]{1,2,0:T(8,128)(2,1)}, bf16[4,256,512]{1,2,0:T(8,128)(2,1)S(1)}, u32[]{:S(2)}) copy-start(bf16[4,256,512]{1,2,0:T(8,128)(2,1)S(1)} %copy.39) | copy-start | bytes 3145732
  242.0 2.2 copy-start.2
  251.0 5.8 %copy-start.8 = (bf16[2,512,128]{2,1,0:T(8,128)(2,1)S(1)}, bf16[2,512,128]{2,1,0:T(8,128)(2,1)}, u32[]{:S(2)}) copy-start(bf16[2,512,128]{2,1,0:T(8,128)(2,1)} %param.14) | copy-start | bytes 786436
  251.0 7.2 %copy-start.1 = (bf16[2,128,512]{2,1,0:T(8,128)(2,1)S(1)}, bf16[2,128,512]{2,1,0:T(8,128)(2,1)}, u32[]{:S(2)}) copy-start(bf16[2,128,512]{2,1,0:T(8,128)(2,1)} %param.13) | copy-start | bytes 786436
Sparse Core Ops, SparseCore 0:
  10.4 98.8 all-gather.4
  112.3 100.1 all-gather.2
where the time goes:
time: 266 us; the launch traced here: 265 us
  waiting for transfers between devices  185 us (70%)
  local copies, waits for them, and re-layouts  31.1 us (12%)
  matrix products  21.4 us (8%)
  other arithmetic  13.7 us (5%)
  between operations  13.7 us (5%)
    all_gather x1, waiting for transfers between devices, on_device(): blocks_all = lax.all_gather(joint_buf, ('ctx', 'store'), axis=0, tiled=True)  96.6 us
    all_gather x1, waiting for transfers between devices, on_device(): joint_piece = lax.all_gather(new_joint, 'ctx', axis=1, tiled=True)  88.5 us
    gather x2, local copies, waits for them, and re-layouts, on_device(): jnp.take(blocks_all, gathered_row, axis=0)  21.6 us
    dot_general x1, matrix products, on_device(): jnp.einsum('srk,smk->srm', query_joint, joint_piece, preferred_element_ty...  6.62 us
  transfers between devices with their start and end apart: 2, of which 2 were waited for; matrix products, arithmetic and copies ran while one was open for 7% of the time, Pallas kernels for 0%

commit v1 on v0

v1 whole, which is shorter than its diff:
```python
import functools

import jax
import jax.numpy as jnp
from jax import lax
from jax.experimental import pallas as pl
from jax.experimental.pallas import tpu as pltpu
from jax.sharding import Mesh
from jax.sharding import PartitionSpec as P

NEG = -1e30
LOG2E = 1.4426950408889634
EXP_SCALE = 192.0 ** (-0.5) * LOG2E
PLANE = ("y", "xh", "xl")
ROW = ("xh", "xl")
CAP = 9
PIECE = 16
HALF = 256
WIDE = 384
VMEM_LIMIT = 50 * 1024 * 1024


def pack_kernel(
    info,
    owner,
    slot,
    cache_latent,
    cache_rope,
    new_latent,
    new_rope,
    out,
    slots,
    lat,
    rope,
    nlat,
    nrope,
    sems,
):
    holder = info[0]
    core = info[1]
    xl = info[2]
    cols = pl.ds(pl.multiple_of(core * HALF, HALF), HALF)
    rows = pl.ds(pl.multiple_of(xl * 64, 64), 64)
    copies = [
        pltpu.make_async_copy(new_latent.at[:, rows, cols], nlat, sems.at[0]),
        pltpu.make_async_copy(new_rope.at[:, rows, :], nrope, sems.at[1]),
    ]
    for c in copies:
        c.start()
    for r in range(CAP):
        slots[r] = 0

    def scan(e, count):
        hit = owner[e] == holder

        @pl.when(hit & (count < CAP))
        def _():
            slots[count] = slot[e]

        return count + hit.astype(jnp.int32)

    lax.fori_loop(0, owner.shape[0], scan, jnp.int32(0))
    block_copies = []
    for r in range(CAP):
        a = pltpu.make_async_copy(cache_latent.at[slots[r], :, cols], lat.at[r], sems.at[2 + 2 * r])
        b = pltpu.make_async_copy(cache_rope.at[slots[r]], rope.at[r], sems.at[3 + 2 * r])
        a.start()
        b.start()
        block_copies.append((a, b))
    for c in copies:
        c.wait()
    pad = jnp.zeros((64, 64), jnp.bfloat16)
    for s in range(4):
        piece = jnp.concatenate([nlat[s], nrope[s], pad], axis=1)
        for x in range(4):
            out[s * 4 + x, CAP * PIECE :, :] = piece
    for r in range(CAP):
        for c in block_copies[r]:
            c.wait()
        whole = jnp.concatenate([lat[r], rope[r], pad], axis=1)
        for x in range(4):
            piece = whole[x * PIECE : (x + 1) * PIECE]
            for s in range(4):
                out[s * 4 + x, r * PIECE : (r + 1) * PIECE, :] = piece


def select_kernel(info, owner, recv, out, new_out, counts, sel, nbuf, sems):
    seq = info[3]
    per = owner.shape[0] // 4
    new_in = pltpu.make_async_copy(recv.at[:, CAP * PIECE :, :], nbuf, sems.at[per])
    new_in.start()
    for h in range(16):
        counts[h] = 0

    def scan(e, carry):
        h = owner[e]
        counts[h] = counts[h] + 1
        return carry

    lax.fori_loop(0, seq * per, scan, jnp.int32(0))
    copies = []
    for j in range(per):
        h = owner[seq * per + j]
        rank = jnp.minimum(counts[h], CAP - 1)
        counts[h] = counts[h] + 1
        c = pltpu.make_async_copy(
            recv.at[h, pl.ds(pl.multiple_of(rank * PIECE, PIECE), PIECE), :],
            sel.at[pl.ds(j * PIECE, PIECE), :],
            sems.at[j],
        )
        c.start()
        copies.append(c)
    for c in copies:
        c.wait()
    for x in range(4):
        out[x] = sel[...]
    new_in.wait()
    new_out[...] = nbuf[...]


def dot(a, b):
    return lax.dot_general(a, b, (((1,), (0,)), ((), ())), preferred_element_type=jnp.float32)


def dot_t(a, b):
    return lax.dot_general(a, b, (((1,), (1,)), ((), ())), preferred_element_type=jnp.float32)


def attend_kernel(
    info,
    cached_len,
    query,
    key_up,
    value_up,
    cache_own,
    cache_other,
    new_own,
    new_other,
    out,
    keys,
    sems,
):
    core = info[1]
    xh = info[4]
    seq = info[3]
    old = cache_own.shape[0]
    new = new_own.shape[0]
    own_cols = pl.ds(pl.multiple_of(core * HALF, HALF), HALF)
    other_cols = pl.ds(pl.multiple_of((1 - core) * HALF, HALF), HALF)
    copies = []
    for i, (own, other, start, count) in enumerate(
        ((cache_own, cache_other, 0, old), (new_own, new_other, old, new))
    ):
        rows = pl.ds(start, count)
        copies += [
            pltpu.make_async_copy(own.at[:, pl.ds(0, HALF)], keys.at[rows, own_cols], sems.at[3 * i]),
            pltpu.make_async_copy(
                other.at[:, pl.ds(0, HALF)], keys.at[rows, other_cols], sems.at[3 * i + 1]
            ),
            pltpu.make_async_copy(
                own.at[:, pl.ds(HALF, 128)], keys.at[rows, pl.ds(2 * HALF, 128)], sems.at[3 * i + 2]
            ),
        ]
    for c in copies:
        c.start()
    index = lax.broadcasted_iota(jnp.int32, (1, old), 1)
    per_x = old // 4
    rest = index % per_x
    position = (rest // PIECE) * (4 * PIECE) + (index // per_x) * PIECE + rest % PIECE
    bias = jnp.where(position < cached_len[seq], 0.0, NEG).astype(jnp.float32)
    tok = query.shape[1]
    row_tok = lax.broadcasted_iota(jnp.int32, (2 * tok, 2 * tok), 0) % tok + xh * tok
    col = lax.broadcasted_iota(jnp.int32, (2 * tok, 2 * tok), 1)
    causal = jnp.where(col <= row_tok, 0.0, NEG).astype(jnp.float32)
    pad = jnp.zeros((tok, 64), jnp.bfloat16)
    joint = []
    for chunk in range(4):
        parts = []
        for h in range(2):
            latent = dot(query[chunk, :, h * 128 : (h + 1) * 128], key_up[h]).astype(jnp.bfloat16)
            pos = query[chunk, :, 256 + h * 64 : 256 + (h + 1) * 64]
            parts.append(jnp.concatenate([latent, pos, pad], axis=1))
        joint.append(jnp.concatenate(parts, axis=0))
    for c in copies:
        c.wait()
    for chunk in range(4):
        q = joint[chunk]
        full = old + chunk * 2 * tok
        pieces = [dot_t(q, keys[0:old, :]) + bias]
        if chunk:
            pieces.append(dot_t(q, keys[old:full, :]))
        pieces.append(dot_t(q, keys[full : full + 2 * tok, :]) + causal)
        top = functools.reduce(jnp.maximum, [jnp.max(p, -1, keepdims=True) for p in pieces])
        expo = [jnp.exp2((p - top) * EXP_SCALE) for p in pieces]
        denom = functools.reduce(jnp.add, [jnp.sum(e, -1, keepdims=True) for e in expo])
        weights = [e.astype(jnp.bfloat16) for e in expo]
        total = dot(weights[0], keys[0:old, 0:512])
        if chunk:
            total += dot(weights[1], keys[old:full, 0:512])
        total += dot(weights[-1], keys[full : full + 2 * tok, 0:512])
        mixed = (total / denom).astype(jnp.bfloat16)
        for h in range(2):
            out[chunk, :, h * 128 : (h + 1) * 128] = dot(
                mixed[h * tok : (h + 1) * tok], value_up[h]
            ).astype(jnp.bfloat16)


def smem():
    return pl.BlockSpec(memory_space=pltpu.SMEM)


def vmem():
    return pl.BlockSpec(memory_space=pltpu.VMEM)


def hbm():
    return pl.BlockSpec(memory_space=pl.ANY)


def params():
    return pltpu.CompilerParams(vmem_limit_bytes=VMEM_LIMIT)


def on_device(
    query_nope,
    query_rope,
    key_up,
    value_up,
    new_latent,
    new_rope,
    cache_latent,
    cache_rope,
    block_owner,
    block_slot,
    cached_len,
):
    y = lax.axis_index("y")
    x = lax.axis_index(ROW)
    info = jnp.stack(
        [y * 4 + x, lax.axis_index("core"), lax.axis_index("xl"), y, lax.axis_index("xh")]
    ).astype(jnp.int32)
    owner = block_owner.reshape(-1)
    slot = block_slot.reshape(-1)
    entries = owner.shape[0] // 4
    chunk_rows = CAP * PIECE + 64
    bf16 = jnp.bfloat16

    send = pl.pallas_call(
        pack_kernel,
        out_shape=jax.ShapeDtypeStruct((16, chunk_rows, WIDE), bf16),
        in_specs=[smem(), smem(), smem(), hbm(), hbm(), hbm(), hbm()],
        out_specs=vmem(),
        scratch_shapes=[
            pltpu.SMEM((16,), jnp.int32),
            pltpu.VMEM((CAP, 64, HALF), bf16),
            pltpu.VMEM((CAP, 64, 64), bf16),
            pltpu.VMEM((4, 64, HALF), bf16),
            pltpu.VMEM((4, 64, 64), bf16),
            pltpu.SemaphoreType.DMA((2 + 2 * CAP,)),
        ],
        compiler_params=params(),
        name="pack",
    )(info, owner, slot, cache_latent, cache_rope, new_latent, new_rope)
    recv = lax.all_to_all(send, PLANE, 0, 0)

    query = jnp.concatenate([query_nope, query_rope], -1)
    query = lax.all_to_all(query, "y", 0, 0)

    picked, new_own = pl.pallas_call(
        select_kernel,
        out_shape=(
            jax.ShapeDtypeStruct((4, entries * PIECE, WIDE), bf16),
            jax.ShapeDtypeStruct((16, 64, WIDE), bf16),
        ),
        in_specs=[smem(), smem(), hbm()],
        out_specs=(vmem(), vmem()),
        scratch_shapes=[
            pltpu.SMEM((16,), jnp.int32),
            pltpu.VMEM((entries * PIECE, WIDE), bf16),
            pltpu.VMEM((16, 64, WIDE), bf16),
            pltpu.SemaphoreType.DMA((entries + 1,)),
        ],
        compiler_params=params(),
        name="select",
    )(info, owner, recv)
    swap = [(0, 1), (1, 0)]
    new_own = new_own.reshape(16 * 64, WIDE)
    new_other = lax.ppermute(new_own, "core", swap)
    cache_own = lax.all_to_all(picked, ROW, 0, 0).reshape(4 * entries * PIECE, WIDE)
    cache_other = lax.ppermute(cache_own, "core", swap)

    mixed = pl.pallas_call(
        attend_kernel,
        out_shape=jax.ShapeDtypeStruct((4, 128, 256), bf16),
        in_specs=[smem(), smem(), vmem(), vmem(), vmem(), hbm(), hbm(), hbm(), hbm()],
        out_specs=vmem(),
        scratch_shapes=[
            pltpu.VMEM((4 * entries * PIECE + 16 * 64, 640), bf16),
            pltpu.SemaphoreType.DMA((6,)),
        ],
        compiler_params=params(),
        name="attend",
    )(info, cached_len, query, key_up, value_up, cache_own, cache_other, new_own, new_other)
    return lax.all_to_all(mixed, "y", 0, 0)


def solution(mesh):
    fine = Mesh(mesh.devices.reshape(4, 2, 16, 2, 2), ("y", "xh", "z", "core", "xl"))
    ctx = ("y", "xh")
    heads = ("z", "core", "xl")
    holders = ("y", "xh", "xl")
    return jax.shard_map(
        on_device,
        mesh=fine,
        in_specs=(
            P(None, ctx, heads),
            P(None, ctx, heads),
            P(heads, None, None),
            P(heads, None, None),
            P(None, ctx, None),
            P(None, ctx, None),
            P(holders, None, None),
            P(holders, None, None),
            P(),
            P(),
            P(),
        ),
        out_specs=P(None, ctx, heads),
        check_vma=False,
    )
```

time: 266 us -> 109 us (0.41)
  the two profiles are of different devices: /device:TPU:1 before, /device:TPU:288 now
where the time goes in v1:
time: 109 us
  blocking collectives  78.6 us (72%)
  Pallas kernels  17.6 us (16%)
  local copies, waits for them, and re-layouts  7.99 us (7%)
  starting transfers between devices  4.32 us (4%)
    all_to_all x1, blocking collectives, on_device(): recv = lax.all_to_all(send, PLANE, 0, 0)  40.5 us
    all_to_all x1, blocking collectives, on_device(): lax.all_to_all(picked, ROW, 0, 0).reshape(4 * entries * PIECE, WIDE)  18.2 us
    pallas_call x1, Pallas kernels, on_device(): pl.pallas_call(attend_kernel, out_shape=jax.ShapeDtypeStruct((4, 128, 256...  11.6 us
    all_to_all x1, blocking collectives, on_device(): query = lax.all_to_all(query, 'y', 0, 0)  10.9 us
    all_to_all x1, blocking collectives, on_device(): return lax.all_to_all(mixed, 'y', 0, 0)  9.07 us
    unnamed x20, local copies, waits for them, and re-layouts  6.38 us
    pallas_call x1, Pallas kernels, on_device(): pl.pallas_call(pack_kernel, out_shape=jax.ShapeDtypeStruct((16, chunk_row...  3.92 us
    ppermute x1, starting transfers between devices, on_device(): new_other = lax.ppermute(new_own, 'core', swap)  2.41 us
  transfers between devices with their start and end apart: 2, of which 0 were waited for; matrix products, arithmetic and copies ran while one was open for 0% of the time, Pallas kernels for 0%

profile of v1, /device:TPU:288, one launch (start us, length us, event | category | flops | bytes accessed | tf_op | source)
XLA Modules:
  0.0 108.7 jit_solution(9555894288106726447)
XLA Ops:
  0.0 0.8 reshape.12.owner
  0.8 1.0 copy.12.new_rope
  1.7 0.8 reshape.13.slot
  2.5 0.1 stack.23.info
  2.6 1.6 %copy-done = bf16[32,64,512]{2,1,0:T(8,128)(2,1)S(1)} copy-done((bf16[32,64,512]{2,1,0:T(8,128)(2,1)S(1)}, bf16[32,64,512]{2,1,0:T(8,128)(2,1)}, u32[]{:S(2)}) %copy-start) | copy-done | bytes 2097176
  4.2 1.0 copy-done.1
  5.2 1.0 copy-done.2
  6.3 3.9 %pack.1 = bf16[16,208,384]{2,1,0:T(8,128)(2,1)} custom-call(s32[5]{0:T(128)S(1)} %stack.23.info, s32[96]{0:T(128)S(1)} %reshape.12.owner, s32[96]{0:T(128)S(1)} %reshape.13.slot, bf16[32,64,512]{2,1,0:T(8,128)(2,1)S(1)} %copy-done, bf16[32,64,64]{2,1,0:T(8,128)(2,1)S(1)} %copy-done.1, bf16[4,128,512]{2,1,0:T(8,128)(2,1)S(1)} %copy-done.2, ...), custom_call_target="tpu_custom_call" | custom-call | tf_op jit(solution)/shard_map/pack/pallas_call | solution.py:248
  10.2 40.5 %all_to_all.20.recv = bf16[16,208,384]{2,1,0:T(8,128)(2,1)} all-to-all(bf16[16,208,384]{2,1,0:T(8,128)(2,1)} %pack.1), channel_id=1, replica_groups=mesh['y'=4,'xh'=2,'z'=16,'core'=2,'xl'=2] {'y','xh','xl'}, dimensions={0} | all-to-all | bytes 5111808 | tf_op jit(solution)/shard_map/all_to_all | solution.py:264
  50.6 2.1 %select.1 = (bf16[4,384,384]{2,1,0:T(8,128)(2,1)S(1)}, bf16[16,64,384]{2,1,0:T(8,128)(2,1)S(1)}) custom-call(s32[5]{0:T(128)S(1)} %stack.23.info, s32[96]{0:T(128)S(1)} %reshape.12.owner, bf16[16,208,384]{2,1,0:T(8,128)(2,1)} %all_to_all.20.recv), custom_call_target="tpu_custom_call" | custom-call | tf_op jit(solution)/shard_map/select/pallas_call | solution.py:269
  52.7 0.0 copy-start.3
  52.7 0.0 copy-start.4
  52.7 0.0 copy-start.5
  52.8 18.2 %all_to_all.21 = bf16[4,384,384]{2,1,0:T(8,128)(2,1)S(1)} all-to-all(bf16[4,384,384]{2,1,0:T(8,128)(2,1)S(1)} %get-tuple-element.7), channel_id=1, replica_groups=mesh['y'=4,'xh'=2,'z'=16,'core'=2,'xl'=2] {'xh','xl'}, dimensions={0} | all-to-all | bytes 2359296 | tf_op jit(solution)/shard_map/all_to_all | solution.py:289
  70.9 1.9 %collective-permute-start = (bf16[1536,384]{1,0:T(8,128)(2,1)S(1)}, bf16[1536,384]{1,0:T(8,128)(2,1)S(1)}, u32[]{:S(2)}, u32[]{:S(2)}) collective-permute-start(bf16[1536,384]{1,0:T(8,128)(2,1)S(1)} %bitcast.7), channel_id=1, source_target_pairs={{0,2},{2,0},{1,3},{3,1},{4,6},{6,4},{5,7},{7,5},{8,10},{10,8},{9,1... | collective-permute-start | bytes 3538952 | tf_op jit(solution)/shard_map/ppermute | solution.py:290
  72.9 2.4 %collective-permute-start.1 = (bf16[1024,384]{1,0:T(8,128)(2,1)S(1)}, bf16[1024,384]{1,0:T(8,128)(2,1)S(1)}, u32[]{:S(2)}, u32[]{:S(2)}) collective-permute-start(bf16[1024,384]{1,0:T(8,128)(2,1)S(1)} %bitcast.9), channel_id=1, source_target_pairs={{0,2},{2,0},{1,3},{3,1},{4,6},{6,4},{5,7},{7,5},{8,10},{10,8},{9,1... | collective-permute-start | bytes 2359304 | tf_op jit(solution)/shard_map/ppermute | solution.py:288
  75.3 10.9 %all_to_all.22.query = bf16[4,128,384]{2,1,0:T(8,128)(2,1)S(1)} all-to-all(bf16[4,128,384]{2,1,0:T(8,128)(2,1)S(1)} %pad_maximum_fusion), channel_id=1, replica_groups=mesh['y'=4,'xh'=2,'z'=16,'core'=2,'xl'=2] {'y'}, dimensions={0} | all-to-all | bytes 786432 | tf_op jit(solution)/shard_map/all_to_all | solution.py:267
  86.3 0.0 collective-permute-done.1.new_other
  86.3 0.0 collective-permute-done.cache_other
  86.3 1.0 copy-done.6
  87.3 0.0 copy-done.4
  87.3 11.6 %attend.1 = bf16[4,128,256]{2,1,0:T(8,128)(2,1)S(1)} custom-call(s32[5]{0:T(128)S(1)} %stack.23.info, s32[4]{0:T(128)S(1)} %copy-done.5, bf16[4,128,384]{2,1,0:T(8,128)(2,1)S(1)} %all_to_all.22.query, bf16[2,128,512]{2,1,0:T(8,128)(2,1)S(1)} %copy-done.3, bf16[2,512,128]{2,1,0:T(8,128)(2,1)S(1)} %copy-done.4, bf16[1536,384]{1,0:T(8,128)(2,1)S(1)} %bitcast.8, ...), custom_call_target="tpu_custom_call" | custom-call | tf_op jit(solution)/shard_map/attend/pallas_call | solution.py:292
  98.9 9.1 %all_to_all.23 = bf16[4,128,256]{2,1,0:T(8,128)(2,1)S(1)} all-to-all(bf16[4,128,256]{2,1,0:T(8,128)(2,1)S(1)} %attend.1), channel_id=1, replica_groups=mesh['y'=4,'xh'=2,'z'=16,'core'=2,'xl'=2] {'y'}, dimensions={0} | all-to-all | bytes 524288 | tf_op jit(solution)/shard_map/all_to_all | solution.py:304
  108.0 0.7 copy.14
  (11 shorter events, 0.1 us)
Async XLA Ops:
  2.6 1.6 %copy-start = (bf16[32,64,512]{2,1,0:T(8,128)(2,1)S(1)}, bf16[32,64,512]{2,1,0:T(8,128)(2,1)}, u32[]{:S(2)}) copy-start(bf16[32,64,512]{2,1,0:T(8,128)(2,1)} %cache_latent.1) | copy-start | bytes 6291460
  4.2 1.0 copy-start.1
  5.2 1.0 copy-start.2
  50.6 24.6 %copy-start.7 = (bf16[4,128,256]{2,1,0:T(8,128)(2,1)S(1)}, bf16[4,128,256]{2,1,0:T(8,128)(2,1)}, u32[]{:S(2)}) copy-start(bf16[4,128,256]{2,1,0:T(8,128)(2,1)} %param.11) | copy-start | bytes 786436
  50.6 24.6 %copy-start.8 = (bf16[4,128,128]{2,1,0:T(8,128)(2,1)S(1)}, bf16[4,128,128]{2,1,0:T(8,128)(2,1)}, u32[]{:S(2)}) copy-start(bf16[4,128,128]{2,1,0:T(8,128)(2,1)} %param.12) | copy-start | bytes 393220
  52.7 34.6 %copy-start.3 = (bf16[2,128,512]{2,1,0:T(8,128)(2,1)S(1)}, bf16[2,128,512]{2,1,0:T(8,128)(2,1)}, u32[]{:S(2)}) copy-start(bf16[2,128,512]{2,1,0:T(8,128)(2,1)} %key_up.1) | copy-start | bytes 786436
  52.7 34.6 %copy-start.4 = (bf16[2,512,128]{2,1,0:T(8,128)(2,1)S(1)}, bf16[2,512,128]{2,1,0:T(8,128)(2,1)}, u32[]{:S(2)}) copy-start(bf16[2,512,128]{2,1,0:T(8,128)(2,1)} %value_up.1) | copy-start | bytes 786436
  52.7 34.6 %copy-start.5 = (s32[4]{0:T(128)S(1)}, s32[4]{0:T(128)}, u32[]{:S(2)}) copy-start(s32[4]{0:T(128)} %cached_len.1) | copy-start | bytes 52
  70.9 15.3 %collective-permute-start = (bf16[1536,384]{1,0:T(8,128)(2,1)S(1)}, bf16[1536,384]{1,0:T(8,128)(2,1)S(1)}, u32[]{:S(2)}, u32[]{:S(2)}) collective-permute-start(bf16[1536,384]{1,0:T(8,128)(2,1)S(1)} %bitcast.7), channel_id=1, source_target_pairs={{0,2},{2,0},{1,3},{3,1},{4,6},{6,4},{5,7},{7,5},{8,10},{10,8},{9,1... | collective-permute-start | bytes 3538952 | tf_op jit(solution)/shard_map/ppermute | solution.py:290
  72.9 13.4 %collective-permute-start.1 = (bf16[1024,384]{1,0:T(8,128)(2,1)S(1)}, bf16[1024,384]{1,0:T(8,128)(2,1)S(1)}, u32[]{:S(2)}, u32[]{:S(2)}) collective-permute-start(bf16[1024,384]{1,0:T(8,128)(2,1)S(1)} %bitcast.9), channel_id=1, source_target_pairs={{0,2},{2,0},{1,3},{3,1},{4,6},{6,4},{5,7},{7,5},{8,10},{10,8},{9,1... | collective-permute-start | bytes 2359304 | tf_op jit(solution)/shard_map/ppermute | solution.py:288
  86.3 1.0 copy-start.6

commit v2 on v1

v2 whole, which is shorter than its diff:
```python
import functools

import jax
import jax.numpy as jnp
from jax import lax
from jax.experimental import pallas as pl
from jax.experimental.pallas import tpu as pltpu
from jax.sharding import Mesh
from jax.sharding import PartitionSpec as P

NEG = -1e30
LOG2E = 1.4426950408889634
EXP_SCALE = 192.0 ** (-0.5) * LOG2E
PLANE = ("y", "xh", "xl")
SPREAD = ("xh", "zp", "xl")
CAP = 9
PIECE = 16
LANES = 128
SEQS = 4
BLOCKS = 24
TOK = 128
LAT_ROWS = CAP * PIECE
ROPE_ROWS = (CAP + 1) // 2 * PIECE
NEW_AT = LAT_ROWS + ROPE_ROWS
NEW_ROWS = 2 * 64 + 16
MSG_ROWS = NEW_AT + NEW_ROWS
PICK_LAT = BLOCKS * PIECE
PICK_PART = BLOCKS // 2 * PIECE // 4
PICK_ROWS = PICK_LAT + PICK_PART
MIB = 1024 * 1024
bf16 = jnp.bfloat16
f32 = jnp.float32


def coords(*names):
    return [lax.axis_index(n) for n in names]


def pack_kernel(
    owner,
    slot,
    cache_latent,
    cache_rope,
    new_latent,
    new_rope,
    out,
    owners,
    places,
    slots,
    lat,
    rope,
    nlat,
    nrope_t,
    nrope,
    cached_part,
    new_part,
    sems,
    out_sems,
):
    holder, core, xl, zp = coords(PLANE, "core", "xl", "zp")
    table_copies = [
        pltpu.make_async_copy(owner, owners, sems.at[2 + 2 * CAP]),
        pltpu.make_async_copy(slot, places, sems.at[3 + 2 * CAP]),
    ]
    for c in table_copies:
        c.start()
    cols = pl.ds(pl.multiple_of((core * 2 + zp) * LANES, LANES), LANES)
    half = pl.ds(pl.multiple_of(core * 2 * LANES, 2 * LANES), 2 * LANES)
    rows = pl.ds(pl.multiple_of(xl * 64, 64), 64)
    new_copies = [
        pltpu.make_async_copy(new_latent.at[:, rows, half], nlat, sems.at[0]),
        pltpu.make_async_copy(new_rope, nrope_t, sems.at[1]),
    ]
    for c in new_copies:
        c.start()
    for r in range(CAP):
        slots[r] = 0
    for c in table_copies:
        c.wait()
    count = jnp.int32(0)
    for s in range(SEQS):
        for j in range(BLOCKS):
            hit = owners[s, j] == holder
            slots[jnp.where(hit, jnp.minimum(count, CAP), CAP)] = places[s, j]
            count = count + hit.astype(jnp.int32)
    lat_copies, rope_copies = [], []
    for r in range(CAP):
        at = slots[r]
        lat_copies.append(pltpu.make_async_copy(cache_latent.at[at, :, cols], lat.at[r], sems.at[2 + 2 * r]))
        rope_copies.append(pltpu.make_async_copy(cache_rope.at[at], rope.at[r], sems.at[3 + 2 * r]))
        lat_copies[-1].start()
        rope_copies[-1].start()
    for c in new_copies:
        c.wait()
    low = pl.ds(pl.multiple_of(xl * 64 + core * 16, 16), 16)
    high = pl.ds(pl.multiple_of(xl * 64 + 32 + core * 16, 16), 16)
    for s in range(SEQS):
        nrope[s] = nrope_t[s].T
        new_part[s, 0:64, :] = nlat[s, :, 0:LANES]
        new_part[s, 64:128, :] = nlat[s, :, LANES : 2 * LANES]
        new_part[s, 128:144, :] = jnp.concatenate([nrope[s, low, :], nrope[s, high, :]], axis=1)
    out_copies = [
        pltpu.make_async_copy(new_part, out.at[:, x, pl.ds(NEW_AT, NEW_ROWS), :], out_sems.at[x])
        for x in range(4)
    ]
    for c in out_copies:
        c.start()
    for r in range(CAP):
        lat_copies[r].wait()
        for x in range(4):
            cached_part[x, r * PIECE : (r + 1) * PIECE, :] = lat[r, x * PIECE : (x + 1) * PIECE, :]
    for c in rope_copies:
        c.wait()
    for m in range((CAP + 1) // 2):
        first = rope[2 * m]
        second = rope[2 * m + 1] if 2 * m + 1 < CAP else first
        both = jnp.concatenate([first, second], axis=1)
        for x in range(4):
            cached_part[x, LAT_ROWS + m * PIECE : LAT_ROWS + (m + 1) * PIECE, :] = both[
                x * PIECE : (x + 1) * PIECE, :
            ]
    for s in range(SEQS):
        c = pltpu.make_async_copy(cached_part, out.at[s, :, pl.ds(0, NEW_AT), :], out_sems.at[4 + s])
        c.start()
        out_copies.append(c)
    for c in out_copies:
        c.wait()


def plan_kernel(owner, plan, counts):
    (seq,) = coords("y")
    for h in range(16):
        counts[h] = 0

    def scan(e, carry):
        h = owner[e // BLOCKS, e % BLOCKS]
        counts[h] = counts[h] + 1
        return carry

    lax.fori_loop(0, seq * BLOCKS, scan, jnp.int32(0))
    for j in range(BLOCKS):
        h = owner[seq, j]
        rank = jnp.minimum(counts[h], CAP - 1)
        counts[h] = counts[h] + 1
        plan[0, j] = h
        plan[1, j] = rank


def select_kernel(plan, recv, out, new_out, lat, tiles, pairs, nbuf, sems):
    core, zp = coords("core", "zp")
    copies = []
    for j in range(BLOCKS):
        h, rank = plan[0, j], plan[1, j]
        b = pltpu.make_async_copy(
            recv.at[h, pl.ds(pl.multiple_of(LAT_ROWS + rank // 2 * PIECE, PIECE), PIECE), :],
            tiles.at[j],
            sems.at[2 * j + 1],
        )
        b.start()
        copies.append(b)
    for j in range(BLOCKS):
        h, rank = plan[0, j], plan[1, j]
        a = pltpu.make_async_copy(
            recv.at[h, pl.ds(pl.multiple_of(rank * PIECE, PIECE), PIECE), :],
            lat.at[pl.ds(j * PIECE, PIECE), :],
            sems.at[2 * j],
        )
        a.start()
        copies.append(a)
    new_in = pltpu.make_async_copy(recv.at[:, pl.ds(NEW_AT, NEW_ROWS), :], nbuf, sems.at[2 * BLOCKS])
    new_in.start()
    for c in copies[:BLOCKS]:
        c.wait()
    for j in range(BLOCKS // 2):
        k = j + BLOCKS // 2
        first = jnp.where(plan[1, j] % 2 == 1, tiles[j, :, 64:128], tiles[j, :, 0:64])
        second = jnp.where(plan[1, k] % 2 == 1, tiles[k, :, 64:128], tiles[k, :, 0:64])
        pairs[j * PIECE : (j + 1) * PIECE, :] = jnp.concatenate([first, second], axis=1)
    part = pairs[pl.ds(pl.multiple_of((core * 2 + zp) * PICK_PART, 16), PICK_PART), :]
    for d in range(8):
        out[d, PICK_LAT:PICK_ROWS, :] = part
    for c in copies[BLOCKS:]:
        c.wait()
    for d in range(8):
        out[d, 0:PICK_LAT, :] = lat[...]
    new_in.wait()
    new_out[...] = nbuf[...]


def dot(a, b):
    return lax.dot_general(a, b, (((1,), (0,)), ((), ())), preferred_element_type=f32)


def dot_t(a, b):
    return lax.dot_general(a, b, (((1,), (1,)), ((), ())), preferred_element_type=f32)


def gather_query(refs, query, sems):
    (y,) = coords("y")
    copies = []
    for k in range(4):
        at = lax.rem(y + 4 - k, 4)
        copies.append(pltpu.make_async_copy(refs[k], query.at[at], sems.at[k]))
    for c in copies:
        c.start()
    return copies


def joint_query(query, key_up, chunk):
    pad = jnp.zeros((TOK, 64), bf16)
    low, high = [], []
    for h in range(2):
        latent = dot(query[chunk, :, h * 128 : (h + 1) * 128], key_up[h]).astype(bf16)
        pos = query[chunk, :, 256 + h * 64 : 256 + (h + 1) * 64]
        low.append(jnp.concatenate([latent, pos, pad], axis=1))
        high.append(jnp.concatenate([latent, pad, pos], axis=1))
    return jnp.concatenate(low, axis=0), jnp.concatenate(high, axis=0)


def project(mixed, value_up):
    return [dot(mixed[h * TOK : (h + 1) * TOK], value_up[h]) for h in range(2)]


def new_kernel(q0, q1, q2, q3, key_up, value_up, own, other, stats_out, part_out, query, keys, sems):
    core, xh = coords("core", "xh")
    query_copies = gather_query((q0, q1, q2, q3), query, sems)
    copies = []
    n = 4
    for which, ref in ((core, own), (1 - core, other)):
        for half in range(2):
            for tile in range(2):
                col = pl.ds(pl.multiple_of((which * 2 + tile) * LANES, LANES), LANES)
                copies.append(
                    pltpu.make_async_copy(
                        ref.at[:, :, pl.ds(tile * 64 + half * 32, 32), :],
                        keys.at[:, half, :, :, col],
                        sems.at[n],
                    )
                )
                n += 1
            copies.append(
                pltpu.make_async_copy(
                    ref.at[:, :, pl.ds(128, 16), :],
                    keys.at[:, half, :, pl.ds(pl.multiple_of(which * 16, 16), 16), pl.ds(512, LANES)],
                    sems.at[n],
                )
            )
            n += 1
    for c in copies:
        c.start()
    for c in query_copies:
        c.wait()
    joint = [joint_query(query, key_up, chunk) for chunk in range(4)]
    rows = 2 * TOK
    row_tok = lax.broadcasted_iota(jnp.int32, (rows, TOK), 0) % TOK + xh * TOK
    col = lax.broadcasted_iota(jnp.int32, (rows, TOK), 1)
    col_tok = col // 32 * 64 + col % 32
    causal = [jnp.where(col_tok + 32 * half <= row_tok, 0.0, NEG).astype(f32) for half in range(2)]
    for c in copies:
        c.wait()
    for chunk in range(4):
        scores = []
        for part in range(chunk + 1):
            for half in range(2):
                k = keys[part, half].reshape(TOK, 640)
                s = dot_t(joint[chunk][half], k)
                if part == chunk:
                    s = s + causal[half]
                scores.append(s)
        top = functools.reduce(jnp.maximum, [jnp.max(s, -1, keepdims=True) for s in scores])
        expo = [jnp.exp2((s - top) * EXP_SCALE) for s in scores]
        denom = functools.reduce(jnp.add, [jnp.sum(e, -1, keepdims=True) for e in expo])
        weights = jnp.concatenate([e.astype(bf16) for e in expo], axis=1)
        total = dot(weights, keys[0 : chunk + 1, :, :, :, 0:512].reshape((chunk + 1) * rows, 512))
        stats_out[chunk] = jnp.concatenate(
            [jnp.broadcast_to(top, (rows, 64)), jnp.broadcast_to(denom, (rows, 64))], axis=1
        )
        for h, part in enumerate(project((total / denom).astype(bf16), value_up)):
            part_out[chunk, :, h * 128 : (h + 1) * 128] = part


def cached_kernel(
    cached_len,
    q0,
    q1,
    q2,
    q3,
    key_up,
    value_up,
    own,
    other,
    stats_hbm,
    part_hbm,
    out,
    query,
    keys,
    stats,
    new_part,
    sems,
):
    core, seq = coords("core", "y")
    query_copies = gather_query((q0, q1, q2, q3), query, sems)
    state_copies = [
        pltpu.make_async_copy(stats_hbm, stats, sems.at[20]),
        pltpu.make_async_copy(part_hbm, new_part, sems.at[21]),
    ]
    copies = []
    n = 4
    for which, ref in ((core, own), (1 - core, other)):
        for zp in range(2):
            group = which * 2 + zp
            col = pl.ds(pl.multiple_of(group * LANES, LANES), LANES)
            for half in range(2):
                copies.append(
                    pltpu.make_async_copy(
                        ref.at[:, zp, :, pl.ds(half * PICK_LAT // 2, PICK_LAT // 2), :],
                        keys.at[half, :, :, :, col],
                        sems.at[n],
                    )
                )
                copies.append(
                    pltpu.make_async_copy(
                        ref.at[:, zp, :, pl.ds(PICK_LAT, PICK_PART), :],
                        keys.at[
                            half,
                            :,
                            :,
                            pl.ds(pl.multiple_of(group * PICK_PART, 16), PICK_PART),
                            pl.ds(512, LANES),
                        ],
                        sems.at[n + 1],
                    )
                )
                n += 2
    for c in copies + state_copies:
        c.start()
    for c in query_copies:
        c.wait()
    joint = [joint_query(query, key_up, chunk) for chunk in range(4)]
    count = 4 * PICK_LAT // 2
    index = lax.broadcasted_iota(jnp.int32, (1, count), 1)
    rest = index % (PICK_LAT // 2)
    position = rest // PIECE * 64 + index // (PICK_LAT // 2) * PIECE + rest % PIECE
    length = cached_len[seq]
    bias = [
        jnp.where(position + half * (BLOCKS // 2 * 64) < length, 0.0, NEG).astype(f32)
        for half in range(2)
    ]
    for c in copies + state_copies:
        c.wait()
    for chunk in range(4):
        scores = [
            dot_t(joint[chunk][half], keys[half].reshape(count, 640)) + bias[half]
            for half in range(2)
        ]
        before, denom_before = stats[chunk, :, 0:1], stats[chunk, :, 64:65]
        top = functools.reduce(jnp.maximum, [before] + [jnp.max(s, -1, keepdims=True) for s in scores])
        factor = jnp.exp2((before - top) * EXP_SCALE) * denom_before
        expo = [jnp.exp2((s - top) * EXP_SCALE) for s in scores]
        denom = functools.reduce(jnp.add, [factor] + [jnp.sum(e, -1, keepdims=True) for e in expo])
        weights = jnp.concatenate([e.astype(bf16) for e in expo], axis=1)
        total = dot(weights, keys[:, :, :, :, 0:512].reshape(2 * count, 512))
        share = factor / denom
        for h, part in enumerate(project((total / denom).astype(bf16), value_up)):
            tok = slice(h * TOK, (h + 1) * TOK)
            cols = slice(h * 128, (h + 1) * 128)
            out[chunk, :, cols] = (part + new_part[chunk, :, cols] * share[tok]).astype(bf16)


def smem():
    return pl.BlockSpec(memory_space=pltpu.SMEM)


def vmem():
    return pl.BlockSpec(memory_space=pltpu.VMEM)


def anywhere():
    return pl.BlockSpec(memory_space=pl.ANY)


def params(mib):
    return pltpu.CompilerParams(vmem_limit_bytes=mib * MIB)


def shape(dims, kind=bf16):
    return jax.ShapeDtypeStruct(dims, kind)


def on_device(
    query_nope,
    query_rope,
    key_up,
    value_up,
    new_latent,
    new_rope,
    cache_latent,
    cache_rope,
    block_owner,
    block_slot,
    cached_len,
):
    y = lax.axis_index("y")
    send = pl.pallas_call(
        pack_kernel,
        out_shape=shape((SEQS, 4, MSG_ROWS, LANES)),
        in_specs=[anywhere()] * 6,
        out_specs=anywhere(),
        scratch_shapes=[
            pltpu.SMEM((SEQS, BLOCKS), jnp.int32),
            pltpu.SMEM((SEQS, BLOCKS), jnp.int32),
            pltpu.SMEM((16,), jnp.int32),
            pltpu.VMEM((CAP, 64, LANES), bf16),
            pltpu.VMEM((CAP, 64, 64), bf16),
            pltpu.VMEM((SEQS, 64, 2 * LANES), bf16),
            pltpu.VMEM((SEQS, 64, TOK), bf16),
            pltpu.VMEM((SEQS, TOK, 64), bf16),
            pltpu.VMEM((4, NEW_AT, LANES), bf16),
            pltpu.VMEM((SEQS, NEW_ROWS, LANES), bf16),
            pltpu.SemaphoreType.DMA((4 + 2 * CAP,)),
            pltpu.SemaphoreType.DMA((8,)),
        ],
        compiler_params=params(63),
        name="pack",
    )(block_owner, block_slot, cache_latent, cache_rope, new_latent, jnp.swapaxes(new_rope, 1, 2))
    send, query_nope, query_rope, owner = lax.optimization_barrier(
        (send, query_nope, query_rope, block_owner)
    )
    recv = lax.all_to_all(send.reshape(16, MSG_ROWS, LANES), PLANE, 0, 0)
    query = jnp.concatenate([query_nope, query_rope], -1)
    queries = []
    for k in range(4):
        part = lax.dynamic_index_in_dim(query, lax.rem(y + k, 4), 0, keepdims=False)
        if k:
            part = lax.ppermute(part, "y", [(i, (i + k) % 4) for i in range(4)])
        queries.append(part)
    plan = pl.pallas_call(
        plan_kernel,
        out_shape=shape((2, BLOCKS), jnp.int32),
        in_specs=[smem()],
        out_specs=smem(),
        scratch_shapes=[pltpu.SMEM((16,), jnp.int32)],
        name="plan",
    )(owner)
    recv, plan = lax.optimization_barrier((recv, plan))

    picked, new_own = pl.pallas_call(
        select_kernel,
        out_shape=(shape((8, PICK_ROWS, LANES)), shape((16, NEW_ROWS, LANES))),
        in_specs=[smem(), anywhere()],
        out_specs=(vmem(), vmem()),
        scratch_shapes=[
            pltpu.VMEM((PICK_LAT, LANES), bf16),
            pltpu.VMEM((BLOCKS, PIECE, LANES), bf16),
            pltpu.VMEM((BLOCKS // 2 * PIECE, LANES), bf16),
            pltpu.VMEM((16, NEW_ROWS, LANES), bf16),
            pltpu.SemaphoreType.DMA((2 * BLOCKS + 1,)),
        ],
        compiler_params=params(16),
        name="select",
    )(plan, recv)
    picked, new_own, *queries = lax.optimization_barrier((picked, new_own, *queries))
    swap = [(0, 1), (1, 0)]
    new_own = new_own.reshape(4, 4, NEW_ROWS, LANES)
    new_other = lax.ppermute(new_own, "core", swap)
    cache_own = lax.all_to_all(picked, SPREAD, 0, 0).reshape(2, 2, 2, PICK_ROWS, LANES)

    rows = 2 * TOK
    stats, part = pl.pallas_call(
        new_kernel,
        out_shape=(shape((4, rows, LANES), f32), shape((4, TOK, 256), f32)),
        in_specs=[anywhere()] * 4 + [vmem()] * 2 + [anywhere()] * 2,
        out_specs=(vmem(), vmem()),
        scratch_shapes=[
            pltpu.VMEM((4, TOK, 384), bf16),
            pltpu.VMEM((4, 2, 4, 32, 640), bf16),
            pltpu.SemaphoreType.DMA((16,)),
        ],
        compiler_params=params(32),
        cost_estimate=pl.CostEstimate(flops=3 * 10**9, bytes_accessed=5 * 10**6, transcendentals=700000),
        name="attend_new",
    )(*queries, key_up, value_up, new_own, new_other)
    cache_own, stats, part = lax.optimization_barrier((cache_own, stats, part))
    cache_other = lax.ppermute(cache_own, "core", swap)
    mixed = pl.pallas_call(
        cached_kernel,
        out_shape=shape((4, TOK, 256)),
        in_specs=[smem()] + [anywhere()] * 4 + [vmem()] * 2 + [anywhere()] * 4,
        out_specs=vmem(),
        scratch_shapes=[
            pltpu.VMEM((4, TOK, 384), bf16),
            pltpu.VMEM((2, 2, 2, PICK_LAT // 2, 640), bf16),
            pltpu.VMEM((4, rows, LANES), f32),
            pltpu.VMEM((4, TOK, 256), f32),
            pltpu.SemaphoreType.DMA((22,)),
        ],
        compiler_params=params(32),
        cost_estimate=pl.CostEstimate(flops=4 * 10**9, bytes_accessed=5 * 10**6, transcendentals=1600000),
        name="attend_cached",
    )(cached_len, *queries, key_up, value_up, cache_own, cache_other, stats, part)
    return lax.all_to_all(mixed, "y", 0, 0)


def solution(mesh):
    fine = Mesh(
        mesh.devices.reshape(4, 2, 8, 2, 2, 2), ("y", "xh", "zh", "zp", "core", "xl")
    )
    ctx = ("y", "xh")
    heads = ("zh", "zp", "core", "xl")
    holders = ("y", "xh", "xl")
    return jax.shard_map(
        on_device,
        mesh=fine,
        in_specs=(
            P(None, ctx, heads),
            P(None, ctx, heads),
            P(heads, None, None),
            P(heads, None, None),
            P(None, ctx, None),
            P(None, ctx, None),
            P(holders, None, None),
            P(holders, None, None),
            P(),
            P(),
            P(),
        ),
        out_specs=P(None, ctx, heads),
        check_vma=False,
    )
```

time: 109 us -> 81.8 us (0.75)
  the two profiles are of different devices: /device:TPU:288 before, /device:TPU:1 now
where the time goes in v2:
time: 81.8 us; the launch traced here: 81 us
  starting transfers between devices  31.7 us (39%)
  Pallas kernels  21.5 us (26%)
  waiting for transfers between devices  15.2 us (19%)
  blocking collectives  8.96 us (11%)
  local copies, waits for them, and re-layouts  3.37 us (4%)
    ppermute x3, starting transfers between devices, on_device(): part = lax.ppermute(part, 'y', [(i, (i + k) % 4) for i in range(4)])  9.43 us
    all_to_all x1, blocking collectives, on_device(): return lax.all_to_all(mixed, 'y', 0, 0)  8.96 us
    pallas_call x1, Pallas kernels, on_device(): pl.pallas_call(cached_kernel, out_shape=shape((4, TOK, 256)), in_specs=[s...  8.63 us
    all_to_all x1, waiting for transfers between devices, on_device(): recv = lax.all_to_all(send.reshape(16, MSG_ROWS, LANES), PLANE, 0, 0)  8.2 us
    all_to_all x1, starting transfers between devices, on_device(): recv = lax.all_to_all(send.reshape(16, MSG_ROWS, LANES), PLANE, 0, 0)  7.85 us
    ppermute x1, starting transfers between devices, on_device(): cache_other = lax.ppermute(cache_own, 'core', swap)  5.6 us
    all_to_all x1, starting transfers between devices, on_device(): lax.all_to_all(picked, SPREAD, 0, 0).reshape(2, 2, 2, PICK_ROWS, LANES)  5.3 us
    pallas_call x1, Pallas kernels, on_device(): pl.pallas_call(new_kernel, out_shape=(shape((4, rows, LANES), f32), shape...  5.25 us
  transfers between devices with their start and end apart: 7, of which 5 were waited for; matrix products, arithmetic and copies ran while one was open for 0% of the time, Pallas kernels for 12%

profile of v2, /device:TPU:1, one launch (start us, length us, event | category | flops | bytes accessed | tf_op | source)
XLA Modules:
  0.0 81.0 jit_solution(9908733799198088056)
XLA Ops:
  0.0 3.3 %pack.1 = bf16[4,4,368,128]{3,2,1,0:T(8,128)(2,1)} custom-call(s32[4,24]{1,0:T(4,128)} %owner.2, s32[4,24]{1,0:T(4,128)} %slot.1, bf16[32,64,512]{2,1,0:T(8,128)(2,1)} %cache_latent.1, bf16[32,64,64]{2,1,0:T(8,128)(2,1)} %cache_rope.1, bf16[4,128,512]{2,1,0:T(8,128)(2,1)} %new_latent.1, bf16[4,64,128]{2,1,0:T(8,128)(2,1)} %bitcast.17), custom_call_target="tpu_custom_call" | custom-call | tf_op jit(solution)/shard_map/pack/pallas_call | solution.py:404
  3.3 0.0 copy-start.6
  3.3 7.9 %all-to-all-start = ((bf16[16,368,128]{2,1,0:T(8,128)(2,1)}), bf16[16,368,128]{2,1,0:T(8,128)(2,1)S(1)}, u32[]{:S(2)}, u32[]{:S(2)}) async-start(bf16[16,368,128]{2,1,0:T(8,128)(2,1)} %bitcast.16), calls=%async_computation | async-start | bytes 3014656 | tf_op jit(solution)/shard_map/all_to_all | solution.py:429
  11.3 0.1 dynamic-slice_bitcast_fusion
  11.3 4.5 %collective-permute-start.2 = (bf16[128,384]{1,0:T(8,128)(2,1)S(1)}, bf16[128,384]{1,0:T(8,128)(2,1)S(1)}, u32[]{:S(2)}, u32[]{:S(2)}) collective-permute-start(bf16[128,384]{1,0:T(8,128)(2,1)S(1)} %get-tuple-element.43), channel_id=1, source_target_pairs={{0,384},{128,0},{256,128},{384,256},{1,385},{129,1},{257,129},{385... | collective-permute-start | bytes 294920 | tf_op jit(solution)/shard_map/ppermute | solution.py:435
  15.8 2.5 %collective-permute-start.1 = (bf16[128,384]{1,0:T(8,128)(2,1)S(1)}, bf16[128,384]{1,0:T(8,128)(2,1)S(1)}, u32[]{:S(2)}, u32[]{:S(2)}) collective-permute-start(bf16[128,384]{1,0:T(8,128)(2,1)S(1)} %get-tuple-element.44), channel_id=1, source_target_pairs={{0,256},{128,384},{256,0},{384,128},{1,257},{129,385},{257,1},{385... | collective-permute-start | bytes 294920 | tf_op jit(solution)/shard_map/ppermute | solution.py:435
  18.3 2.5 %collective-permute-start = (bf16[128,384]{1,0:T(8,128)(2,1)S(1)}, bf16[128,384]{1,0:T(8,128)(2,1)S(1)}, u32[]{:S(2)}, u32[]{:S(2)}) collective-permute-start(bf16[128,384]{1,0:T(8,128)(2,1)S(1)} %get-tuple-element.45), channel_id=1, source_target_pairs={{0,128},{128,256},{256,384},{384,0},{1,129},{129,257},{257,385},{3... | collective-permute-start | bytes 294920 | tf_op jit(solution)/shard_map/ppermute | solution.py:435
  20.8 1.4 %plan.1 = s32[2,24]{1,0:T(2,128)} custom-call(s32[4,24]{1,0:T(4,128)} %owner.2), custom_call_target="tpu_custom_call" | custom-call | tf_op jit(solution)/shard_map/plan/pallas_call | solution.py:437
  22.2 8.2 %all-to-all-done.recv = bf16[16,368,128]{2,1,0:T(8,128)(2,1)S(1)} async-done(((bf16[16,368,128]{2,1,0:T(8,128)(2,1)}), bf16[16,368,128]{2,1,0:T(8,128)(2,1)S(1)}, u32[]{:S(2)}, u32[]{:S(2)}) %all-to-all-start) | async-done | bytes 1507360 | tf_op jit(solution)/shard_map/all_to_all | solution.py:429
  30.4 0.7 copy-done
  31.1 3.0 %select.9 = (bf16[8,432,128]{2,1,0:T(8,128)(2,1)}, bf16[16,144,128]{2,1,0:T(8,128)(2,1)S(1)}) custom-call(s32[2,24]{1,0:T(2,128)S(1)} %copy-done, bf16[16,368,128]{2,1,0:T(8,128)(2,1)S(1)} %all-to-all-done.recv), custom_call_target="tpu_custom_call" | custom-call | tf_op jit(solution)/shard_map/select/pallas_call | solution.py:447
  34.1 1.8 %collective-permute-done.q1 = bf16[128,384]{1,0:T(8,128)(2,1)S(1)} collective-permute-done((bf16[128,384]{1,0:T(8,128)(2,1)S(1)}, bf16[128,384]{1,0:T(8,128)(2,1)S(1)}, u32[]{:S(2)}, u32[]{:S(2)}) %collective-permute-start) | collective-permute-done | bytes 98336 | tf_op jit(solution)/shard_map/ppermute | solution.py:435
  35.8 5.3 %all-to-all-start.1 = ((bf16[8,432,128]{2,1,0:T(8,128)(2,1)}), bf16[8,432,128]{2,1,0:T(8,128)(2,1)S(1)}, u32[]{:S(2)}, u32[]{:S(2)}) async-start(bf16[8,432,128]{2,1,0:T(8,128)(2,1)} %get-tuple-element.36), calls=%async_computation.1 | async-start | bytes 1769472 | tf_op jit(solution)/shard_map/all_to_all | solution.py:466
  41.1 3.5 %collective-permute-start.3 = (bf16[4,4,144,128]{3,2,1,0:T(8,128)(2,1)S(1)}, bf16[4,4,144,128]{3,2,1,0:T(8,128)(2,1)S(1)}, u32[]{:S(2)}, u32[]{:S(2)}) collective-permute-start(bf16[4,4,144,128]{3,2,1,0:T(8,128)(2,1)S(1)} %bitcast.14), channel_id=1, source_target_pairs={{0,2},{2,0},{1,3},{3,1},{4,6},{6,4},{5,7},{7,5},{8,10},{10,8},{9,1... | collective-permute-start | bytes 1769480 | tf_op jit(solution)/shard_map/ppermute | solution.py:465
  44.7 1.6 %collective-permute-done.3.other = bf16[4,4,144,128]{3,2,1,0:T(8,128)(2,1)S(1)} collective-permute-done((bf16[4,4,144,128]{3,2,1,0:T(8,128)(2,1)S(1)}, bf16[4,4,144,128]{3,2,1,0:T(8,128)(2,1)S(1)}, u32[]{:S(2)}, u32[]{:S(2)}) %collective-permute-start.3) | collective-permute-done | bytes 589856 | tf_op jit(solution)/shard_map/ppermute | solution.py:465
  46.3 5.2 %attend_new.1 = (f32[4,256,128]{2,1,0:T(8,128)S(1)}, f32[4,128,256]{2,1,0:T(8,128)S(1)}) custom-call(bf16[128,384]{1,0:T(8,128)(2,1)S(1)} %get-tuple-element.32.q0, bf16[128,384]{1,0:T(8,128)(2,1)S(1)} %collective-permute-done.q1, bf16[128,384]{1,0:T(8,128)(2,1)S(1)} %collective-permute-done.1.q2, bf16[128,384]{1,0:T(8,128)(2,1)S(1)} %collective-permute-done.2.q3, ...), custom_call_target="tpu_custom_call" | custom-call | flops 3000000000 | bytes 5000000 | tf_op jit(solution)/shard_map/attend_new/pallas_call | solution.py:469
  51.5 0.8 %copy-done.4 = f32[4,128,256]{2,1,0:T(8,128)} copy-done((f32[4,128,256]{2,1,0:T(8,128)}, f32[4,128,256]{2,1,0:T(8,128)S(1)}, u32[]{:S(2)}) %copy-start.4) | copy-done | bytes 524312
  52.4 1.8 %all-to-all-done.1 = bf16[8,432,128]{2,1,0:T(8,128)(2,1)S(1)} async-done(((bf16[8,432,128]{2,1,0:T(8,128)(2,1)}), bf16[8,432,128]{2,1,0:T(8,128)(2,1)S(1)}, u32[]{:S(2)}, u32[]{:S(2)}) %all-to-all-start.1) | async-done | bytes 884768 | tf_op jit(solution)/shard_map/all_to_all | solution.py:466
  54.2 5.6 %collective-permute-start.4 = (bf16[2,2,2,432,128]{4,3,2,1,0:T(8,128)(2,1)S(1)}, bf16[2,2,2,432,128]{4,3,2,1,0:T(8,128)(2,1)S(1)}, u32[]{:S(2)}, u32[]{:S(2)}) collective-permute-start(bf16[2,2,2,432,128]{4,3,2,1,0:T(8,128)(2,1)S(1)} %bitcast.12), channel_id=1, source_target_pairs={{0,2},{2,0},{1,3},{3,1},{4,6},{6,4},{5,7},{7,5},{8,10},{10,8},{9,1... | collective-permute-start | bytes 2654216 | tf_op jit(solution)/shard_map/ppermute | solution.py:484
  59.8 1.9 %collective-permute-done.4.other = bf16[2,2,2,432,128]{4,3,2,1,0:T(8,128)(2,1)S(1)} collective-permute-done((bf16[2,2,2,432,128]{4,3,2,1,0:T(8,128)(2,1)S(1)}, bf16[2,2,2,432,128]{4,3,2,1,0:T(8,128)(2,1)S(1)}, u32[]{:S(2)}, u32[]{:S(2)}) %collective-permute-start.4) | collective-permute-done | bytes 884768 | tf_op jit(solution)/shard_map/ppermute | solution.py:484
  61.6 1.0 %copy-done.5 = f32[4,128,256]{2,1,0:T(8,128)S(1)} copy-done((f32[4,128,256]{2,1,0:T(8,128)S(1)}, f32[4,128,256]{2,1,0:T(8,128)}, u32[]{:S(2)}) %copy-start.5) | copy-done | bytes 524312
  62.7 8.6 %attend_cached.1 = bf16[4,128,256]{2,1,0:T(8,128)(2,1)S(1)} custom-call(s32[4]{0:T(128)S(1)} %copy-done.3, bf16[128,384]{1,0:T(8,128)(2,1)S(1)} %get-tuple-element.32.q0, bf16[128,384]{1,0:T(8,128)(2,1)S(1)} %collective-permute-done.q1, bf16[128,384]{1,0:T(8,128)(2,1)S(1)} %collective-permute-done.1.q2, bf16[128,384]{1,0:T(8,128)(2,1)S(1)} %collective-permute-done.2.q3, ...), custom_call_target="tpu_custom_call" | custom-call | flops 4000000000 | bytes 5000000 | tf_op jit(solution)/shard_map/attend_cached/pallas_call | solution.py:485
  71.3 9.0 %all_to_all.15 = bf16[4,128,256]{2,1,0:T(8,128)(2,1)S(1)} all-to-all(bf16[4,128,256]{2,1,0:T(8,128)(2,1)S(1)} %attend_cached.1), channel_id=1, replica_groups=mesh['y'=4,'xh'=2,'zh'=8,'zp'=2,'core'=2,'xl'=2] {'y'}, dimensions={0} | all-to-all | bytes 524288 | tf_op jit(solution)/shard_map/all_to_all | solution.py:501
  80.3 0.7 copy.14
  (16 shorter events, 0.1 us)
Async XLA Ops:
  3.3 7.9 %copy-start.6 = (bf16[4,128,256]{2,1,0:T(8,128)(2,1)S(1)}, bf16[4,128,256]{2,1,0:T(8,128)(2,1)}, u32[]{:S(2)}) copy-start(bf16[4,128,256]{2,1,0:T(8,128)(2,1)} %param.11) | copy-start | bytes 786436
  3.3 7.9 %copy-start.7 = (bf16[4,128,128]{2,1,0:T(8,128)(2,1)S(1)}, bf16[4,128,128]{2,1,0:T(8,128)(2,1)}, u32[]{:S(2)}) copy-start(bf16[4,128,128]{2,1,0:T(8,128)(2,1)} %param.12) | copy-start | bytes 393220
  3.3 27.1 %all-to-all-start = ((bf16[16,368,128]{2,1,0:T(8,128)(2,1)}), bf16[16,368,128]{2,1,0:T(8,128)(2,1)S(1)}, u32[]{:S(2)}, u32[]{:S(2)}) async-start(bf16[16,368,128]{2,1,0:T(8,128)(2,1)} %bitcast.16), calls=%async_computation | async-start | bytes 3014656 | tf_op jit(solution)/shard_map/all_to_all | solution.py:429
  11.3 22.7 %collective-permute-start.2 = (bf16[128,384]{1,0:T(8,128)(2,1)S(1)}, bf16[128,384]{1,0:T(8,128)(2,1)S(1)}, u32[]{:S(2)}, u32[]{:S(2)}) collective-permute-start(bf16[128,384]{1,0:T(8,128)(2,1)S(1)} %get-tuple-element.43), channel_id=1, source_target_pairs={{0,384},{128,0},{256,128},{384,256},{1,385},{129,1},{257,129},{385... | collective-permute-start | bytes 294920 | tf_op jit(solution)/shard_map/ppermute | solution.py:435
  15.8 18.3 %collective-permute-start.1 = (bf16[128,384]{1,0:T(8,128)(2,1)S(1)}, bf16[128,384]{1,0:T(8,128)(2,1)S(1)}, u32[]{:S(2)}, u32[]{:S(2)}) collective-permute-start(bf16[128,384]{1,0:T(8,128)(2,1)S(1)} %get-tuple-element.44), channel_id=1, source_target_pairs={{0,256},{128,384},{256,0},{384,128},{1,257},{129,385},{257,1},{385... | collective-permute-start | bytes 294920 | tf_op jit(solution)/shard_map/ppermute | solution.py:435
  18.3 17.5 %collective-permute-start = (bf16[128,384]{1,0:T(8,128)(2,1)S(1)}, bf16[128,384]{1,0:T(8,128)(2,1)S(1)}, u32[]{:S(2)}, u32[]{:S(2)}) collective-permute-start(bf16[128,384]{1,0:T(8,128)(2,1)S(1)} %get-tuple-element.45), channel_id=1, source_target_pairs={{0,128},{128,256},{256,384},{384,0},{1,129},{129,257},{257,385},{3... | collective-permute-start | bytes 294920 | tf_op jit(solution)/shard_map/ppermute | solution.py:435
  30.4 0.7 copy-start
  31.1 15.2 %copy-start.1 = (bf16[2,128,512]{2,1,0:T(8,128)(2,1)S(1)}, bf16[2,128,512]{2,1,0:T(8,128)(2,1)}, u32[]{:S(2)}) copy-start(bf16[2,128,512]{2,1,0:T(8,128)(2,1)} %key_up.3) | copy-start | bytes 786436
  31.1 15.2 %copy-start.2 = (bf16[2,512,128]{2,1,0:T(8,128)(2,1)S(1)}, bf16[2,512,128]{2,1,0:T(8,128)(2,1)}, u32[]{:S(2)}) copy-start(bf16[2,512,128]{2,1,0:T(8,128)(2,1)} %value_up.3) | copy-start | bytes 786436
  35.8 18.3 %all-to-all-start.1 = ((bf16[8,432,128]{2,1,0:T(8,128)(2,1)}), bf16[8,432,128]{2,1,0:T(8,128)(2,1)S(1)}, u32[]{:S(2)}, u32[]{:S(2)}) async-start(bf16[8,432,128]{2,1,0:T(8,128)(2,1)} %get-tuple-element.36), calls=%async_computation.1 | async-start | bytes 1769472 | tf_op jit(solution)/shard_map/all_to_all | solution.py:466
  41.1 20.5 %copy-start.3 = (s32[4]{0:T(128)S(1)}, s32[4]{0:T(128)}, u32[]{:S(2)}) copy-start(s32[4]{0:T(128)} %cached_len.1) | copy-start | bytes 52
  41.1 5.2 %collective-permute-start.3 = (bf16[4,4,144,128]{3,2,1,0:T(8,128)(2,1)S(1)}, bf16[4,4,144,128]{3,2,1,0:T(8,128)(2,1)S(1)}, u32[]{:S(2)}, u32[]{:S(2)}) collective-permute-start(bf16[4,4,144,128]{3,2,1,0:T(8,128)(2,1)S(1)} %bitcast.14), channel_id=1, source_target_pairs={{0,2},{2,0},{1,3},{3,1},{4,6},{6,4},{5,7},{7,5},{8,10},{10,8},{9,1... | collective-permute-start | bytes 1769480 | tf_op jit(solution)/shard_map/ppermute | solution.py:465
  51.5 0.8 %copy-start.4 = (f32[4,128,256]{2,1,0:T(8,128)}, f32[4,128,256]{2,1,0:T(8,128)S(1)}, u32[]{:S(2)}) copy-start(f32[4,128,256]{2,1,0:T(8,128)S(1)} %get-tuple-element.42.part_hbm) | copy-start | bytes 1572868
  54.2 7.5 %collective-permute-start.4 = (bf16[2,2,2,432,128]{4,3,2,1,0:T(8,128)(2,1)S(1)}, bf16[2,2,2,432,128]{4,3,2,1,0:T(8,128)(2,1)S(1)}, u32[]{:S(2)}, u32[]{:S(2)}) collective-permute-start(bf16[2,2,2,432,128]{4,3,2,1,0:T(8,128)(2,1)S(1)} %bitcast.12), channel_id=1, source_target_pairs={{0,2},{2,0},{1,3},{3,1},{4,6},{6,4},{5,7},{7,5},{8,10},{10,8},{9,1... | collective-permute-start | bytes 2654216 | tf_op jit(solution)/shard_map/ppermute | solution.py:484
  61.6 1.0 %copy-start.5 = (f32[4,128,256]{2,1,0:T(8,128)S(1)}, f32[4,128,256]{2,1,0:T(8,128)}, u32[]{:S(2)}) copy-start(f32[4,128,256]{2,1,0:T(8,128)} %copy-done.4) | copy-start | bytes 1572868

commit v3 on v2

v3 whole, which is shorter than its diff:
```python
import functools

import jax
import jax.numpy as jnp
from jax import lax
from jax.experimental import pallas as pl
from jax.experimental.pallas import tpu as pltpu
from jax.sharding import Mesh
from jax.sharding import PartitionSpec as P

NEG = -1e30
LOG2E = 1.4426950408889634
EXP_SCALE = 192.0 ** (-0.5) * LOG2E
HOLDER = ("y", "xh", "xl")
PLANE = ("xl", "xh", "y")
SPREAD = ("xl", "xh", "zp")
CAP = 9
PIECE = 16
LANES = 128
SEQS = 4
BLOCKS = 24
TOK = 128
LAT_ROWS = CAP * PIECE
ROPE_ROWS = (CAP + 1) // 2 * PIECE
NEW_AT = LAT_ROWS + ROPE_ROWS
NEW_ROWS = 2 * 64 + 16
MSG_ROWS = NEW_AT + NEW_ROWS
PICK_LAT = BLOCKS * PIECE
PICK_PART = BLOCKS // 2 * PIECE // 4
PICK_ROWS = PICK_LAT + PICK_PART
MIB = 1024 * 1024
bf16 = jnp.bfloat16
f32 = jnp.float32


def coords(*names):
    return [lax.axis_index(n) for n in names]


def pack_kernel(
    owner,
    slot,
    cache_latent,
    cache_rope,
    new_latent,
    new_rope,
    out,
    owners,
    places,
    slots,
    lat,
    rope,
    nlat,
    nrope_t,
    nrope,
    cached_part,
    new_part,
    sems,
    out_sems,
):
    holder, core, xl, zp = coords(HOLDER, "core", "xl", "zp")
    table_copies = [
        pltpu.make_async_copy(owner, owners, sems.at[4]),
        pltpu.make_async_copy(slot, places, sems.at[5]),
    ]
    for c in table_copies:
        c.start()
    cols = pl.ds(pl.multiple_of((core * 2 + zp) * LANES, LANES), LANES)
    half = pl.ds(pl.multiple_of(core * 2 * LANES, 2 * LANES), 2 * LANES)
    rows = pl.ds(pl.multiple_of(xl * 64, 64), 64)
    new_copies = [
        pltpu.make_async_copy(new_latent.at[:, rows, half], nlat, sems.at[0]),
        pltpu.make_async_copy(new_rope, nrope_t, sems.at[1]),
    ]
    pool_copies = [
        pltpu.make_async_copy(cache_latent.at[:, :, cols], lat, sems.at[2]),
        pltpu.make_async_copy(cache_rope, rope, sems.at[3]),
    ]
    for c in new_copies + pool_copies:
        c.start()
    for r in range(CAP):
        slots[r] = 0
    for c in table_copies:
        c.wait()
    count = jnp.int32(0)
    for s in range(SEQS):
        for j in range(BLOCKS):
            hit = owners[s, j] == holder
            slots[jnp.where(hit, jnp.minimum(count, CAP), CAP)] = places[s, j]
            count = count + hit.astype(jnp.int32)
    for c in new_copies:
        c.wait()
    low = pl.ds(pl.multiple_of(xl * 64 + core * 16, 16), 16)
    high = pl.ds(pl.multiple_of(xl * 64 + 32 + core * 16, 16), 16)
    for s in range(SEQS):
        nrope[s] = nrope_t[s].T
        new_part[s, 0:64, :] = nlat[s, :, 0:LANES]
        new_part[s, 64:128, :] = nlat[s, :, LANES : 2 * LANES]
        new_part[s, 128:144, :] = jnp.concatenate([nrope[s, low, :], nrope[s, high, :]], axis=1)
    out_copies = [
        pltpu.make_async_copy(new_part, out.at[x, :, pl.ds(NEW_AT, NEW_ROWS), :], out_sems.at[x])
        for x in range(4)
    ]
    for c in out_copies:
        c.start()
    flipped = (0, 2, 1, 3)
    for c in pool_copies:
        c.wait()
    blocks = [slots[r] for r in range(CAP)]
    for r in range(CAP):
        for i, x in enumerate(flipped):
            cached_part[i, r * PIECE : (r + 1) * PIECE, :] = lat[blocks[r], x * PIECE : (x + 1) * PIECE, :]
    for m in range((CAP + 1) // 2):
        first = rope[blocks[2 * m]]
        second = rope[blocks[2 * m + 1]] if 2 * m + 1 < CAP else first
        both = jnp.concatenate([first, second], axis=1)
        for i, x in enumerate(flipped):
            cached_part[i, LAT_ROWS + m * PIECE : LAT_ROWS + (m + 1) * PIECE, :] = both[
                x * PIECE : (x + 1) * PIECE, :
            ]
    for s in range(SEQS):
        c = pltpu.make_async_copy(cached_part, out.at[:, s, pl.ds(0, NEW_AT), :], out_sems.at[4 + s])
        c.start()
        out_copies.append(c)
    for c in out_copies:
        c.wait()


def plan_kernel(owner, plan, counts):
    for h in range(16):
        counts[h] = 0
    for s in range(SEQS):
        for j in range(BLOCKS):
            h = owner[s, j]
            rank = counts[h]
            counts[h] = rank + 1
            source = (h % 2 * 2 + h // 2 % 2) * 4 + h // 4
            plan[s, j] = source * 16 + jnp.minimum(rank, CAP - 1)


def select_kernel(plan, recv, out, new_out, picked, tiles, pairs, sems, out_sems):
    core, zp, seq = coords("core", "zp", "y")
    entries = [plan[seq, j] for j in range(BLOCKS)]
    ranks = [e % 16 for e in entries]
    sources = [e // 16 for e in entries]
    rope_copies, lat_copies = [], []
    for j in range(BLOCKS):
        c = pltpu.make_async_copy(
            recv.at[sources[j], pl.ds(pl.multiple_of(LAT_ROWS + ranks[j] // 2 * PIECE, PIECE), PIECE), :],
            tiles.at[j],
            sems.at[2 * j + 1],
        )
        c.start()
        rope_copies.append(c)
    for j in range(BLOCKS):
        c = pltpu.make_async_copy(
            recv.at[sources[j], pl.ds(pl.multiple_of(ranks[j] * PIECE, PIECE), PIECE), :],
            picked.at[pl.ds(j * PIECE, PIECE), :],
            sems.at[2 * j],
        )
        c.start()
        lat_copies.append(c)
    new_copy = pltpu.make_async_copy(
        recv.at[:, pl.ds(NEW_AT, NEW_ROWS), :], new_out, sems.at[2 * BLOCKS]
    )
    new_copy.start()
    for c in rope_copies:
        c.wait()
    for j in range(BLOCKS // 2):
        k = j + BLOCKS // 2
        first = jnp.where(ranks[j] % 2 == 1, tiles[j, :, 64:128], tiles[j, :, 0:64])
        second = jnp.where(ranks[k] % 2 == 1, tiles[k, :, 64:128], tiles[k, :, 0:64])
        pairs[j * PIECE : (j + 1) * PIECE, :] = jnp.concatenate([first, second], axis=1)
    part = pl.ds(pl.multiple_of((core * 2 + zp) * PICK_PART, 16), PICK_PART)
    picked[PICK_LAT:PICK_ROWS, :] = pairs[part, :]
    for c in lat_copies:
        c.wait()
    out_copies = [pltpu.make_async_copy(picked, out.at[d], out_sems.at[d]) for d in range(8)]
    for c in out_copies:
        c.start()
    for c in out_copies + [new_copy]:
        c.wait()


def dot(a, b):
    return lax.dot_general(a, b, (((1,), (0,)), ((), ())), preferred_element_type=f32)


def dot_t(a, b):
    return lax.dot_general(a, b, (((1,), (1,)), ((), ())), preferred_element_type=f32)


def gather_query(refs, query, sems):
    (y,) = coords("y")
    copies = []
    for k in range(4):
        at = lax.rem(y + 4 - k, 4)
        copies.append(pltpu.make_async_copy(refs[k], query.at[at], sems.at[k]))
    for c in copies:
        c.start()
    return copies


def halves(core):
    return [pl.ds(pl.multiple_of(c * 256, 256), 256) for c in (core, 1 - core)]


def joint_query(query, key_up, core, chunk, joint):
    pad = jnp.zeros((TOK, 64), bf16)
    for h in range(2):
        rows = pl.ds((2 * chunk + h) * TOK, TOK)
        nope = query[chunk, :, h * 128 : (h + 1) * 128]
        pos = query[chunk, :, 256 + h * 64 : 256 + (h + 1) * 64]
        for i, cols in enumerate(halves(core)):
            joint[rows, i * 256 : (i + 1) * 256] = dot(nope, key_up[h, :, cols]).astype(bf16)
        joint[rows, 512:640] = jnp.concatenate([pos, pad], axis=1)
        joint[rows, 640:768] = jnp.concatenate([pad, pos], axis=1)


def load_query(joint, start, count):
    low = joint[start : start + count, 0:640]
    high = jnp.concatenate([joint[start : start + count, 0:512], joint[start : start + count, 640:768]], axis=1)
    return low, high


def project(mixed, value_up, core, h):
    own, other = halves(core)
    return dot(mixed[:, 0:256], value_up[h, own, :]) + dot(mixed[:, 256:512], value_up[h, other, :])


def new_kernel(
    q0, q1, q2, q3, key_up, value_up, own, other, stats_out, part_out, token, query, joint, keys, sems
):
    core, xh = coords("core", "xh")
    query_copies = gather_query((q0, q1, q2, q3), query, sems)
    token[...] = jnp.zeros_like(token)
    for i, (which, ref) in enumerate(((core, own), (1 - core, other))):
        rope_rows = pl.ds(pl.multiple_of(which * 16, 16), 16)
        for y in range(4):
            for part in range(4):
                for half in range(2):
                    for tile in range(2):
                        at = tile * 64 + half * 32
                        col = (2 * i + tile) * LANES
                        keys[y, half, part, :, col : col + LANES] = ref[part % 2, part // 2, y, at : at + 32, :]
                    keys[y, half, part, rope_rows, 512:640] = ref[part % 2, part // 2, y, 128:144, :]
    for c in query_copies:
        c.wait()
    for chunk in range(4):
        joint_query(query, key_up, core, chunk, joint)
    rows = 2 * TOK
    row_tok = lax.broadcasted_iota(jnp.int32, (rows, TOK), 0) % TOK + xh * TOK
    col = lax.broadcasted_iota(jnp.int32, (rows, TOK), 1)
    col_tok = col // 32 * 64 + col % 32
    lane = lax.broadcasted_iota(jnp.int32, (rows, LANES), 1)
    causal = [jnp.where(col_tok + 32 * half <= row_tok, 0.0, NEG).astype(f32) for half in range(2)]
    for chunk in range(4):
        q = load_query(joint, chunk * rows, rows)
        scores = []
        for part in range(chunk + 1):
            for half in range(2):
                s = dot_t(q[half], keys[part, half].reshape(TOK, 640))
                if part == chunk:
                    s = s + causal[half]
                scores.append(s)
        top = functools.reduce(jnp.maximum, [jnp.max(s, -1, keepdims=True) for s in scores])
        expo = [jnp.exp2((s - top) * EXP_SCALE) for s in scores]
        denom = functools.reduce(jnp.add, [jnp.sum(e, -1, keepdims=True) for e in expo])
        weights = jnp.concatenate([e.astype(bf16) for e in expo], axis=1)
        total = dot(weights, keys[0 : chunk + 1, :, :, :, 0:512].reshape((chunk + 1) * rows, 512))
        stats_out[:, chunk * rows : (chunk + 1) * rows] = jnp.where(lane == 0, top, denom).T[0:8]
        mixed = (total / denom).astype(bf16)
        for h in range(2):
            part_out[chunk, :, h * 128 : (h + 1) * 128] = project(
                mixed[h * TOK : (h + 1) * TOK], value_up, core, h
            )


def cached_kernel(
    cached_len,
    q0,
    q1,
    q2,
    q3,
    key_up,
    value_up,
    own,
    other,
    stats,
    new_part,
    token,
    out,
    query,
    joint,
    keys,
    sems,
):
    core, seq = coords("core", "y")
    query_copies = gather_query((q0, q1, q2, q3), query, sems)
    span = PICK_LAT // 2
    for i, (which, ref) in enumerate(((core, own), (1 - core, other))):
        for zp in range(2):
            rope_at = (which * 2 + zp) * PICK_PART
            for x in range(4):
                for half in range(2):
                    keys[half, x * span : (x + 1) * span, (2 * i + zp) * LANES : (2 * i + zp + 1) * LANES] = ref[
                        x % 2, x // 2, zp, half * span : (half + 1) * span, :
                    ]
                    keys[half, pl.ds(pl.multiple_of(x * span + rope_at, 16), PICK_PART), 512:640] = ref[
                        x % 2, x // 2, zp, PICK_LAT:PICK_ROWS, :
                    ]
    count = 4 * span
    index = lax.broadcasted_iota(jnp.int32, (1, count), 1)
    rest = index % span
    position = rest // PIECE * 64 + index // span * PIECE + rest % PIECE
    length = cached_len[seq]
    bias = [
        jnp.where(position + half * (BLOCKS // 2 * 64) < length, 0.0, NEG).astype(f32)
        for half in range(2)
    ]
    for c in query_copies:
        c.wait()
    for chunk in range(4):
        joint_query(query, key_up, core, chunk, joint)
    rows = 4 * TOK
    for group in range(2):
        at = slice(group * rows, (group + 1) * rows)
        q = load_query(joint, group * rows, rows)
        scores = [dot_t(q[half], keys[half]) + bias[half] for half in range(2)]
        state = jnp.concatenate([stats[:, at]] * 16, axis=0).T
        before, denom_before = state[:, 0:1], state[:, 1:2]
        top = functools.reduce(jnp.maximum, [before] + [jnp.max(s, -1, keepdims=True) for s in scores])
        factor = jnp.exp2((before - top) * EXP_SCALE) * denom_before
        expo = [jnp.exp2((s - top) * EXP_SCALE) for s in scores]
        denom = functools.reduce(jnp.add, [factor] + [jnp.sum(e, -1, keepdims=True) for e in expo])
        weights = jnp.concatenate([e.astype(bf16) for e in expo], axis=1)
        total = dot(weights, keys[:, :, 0:512].reshape(2 * count, 512))
        share = factor / denom
        mixed = (total / denom).astype(bf16)
        for c in range(2):
            chunk = group * 2 + c
            for h in range(2):
                tok = slice((2 * c + h) * TOK, (2 * c + h + 1) * TOK)
                cols = slice(h * 128, (h + 1) * 128)
                fresh = project(mixed[tok], value_up, core, h)
                out[chunk, :, cols] = (fresh + new_part[chunk, :, cols] * share[tok]).astype(bf16)


def smem():
    return pl.BlockSpec(memory_space=pltpu.SMEM)


def vmem():
    return pl.BlockSpec(memory_space=pltpu.VMEM)


def anywhere():
    return pl.BlockSpec(memory_space=pl.ANY)


def params(mib):
    return pltpu.CompilerParams(vmem_limit_bytes=mib * MIB)


def shape(dims, kind=bf16):
    return jax.ShapeDtypeStruct(dims, kind)


def on_device(
    query_nope,
    query_rope,
    key_up,
    value_up,
    new_latent,
    new_rope,
    cache_latent,
    cache_rope,
    block_owner,
    block_slot,
    cached_len,
):
    y = lax.axis_index("y")
    send = pl.pallas_call(
        pack_kernel,
        out_shape=shape((4, SEQS, MSG_ROWS, LANES)),
        in_specs=[anywhere()] * 6,
        out_specs=anywhere(),
        scratch_shapes=[
            pltpu.SMEM((SEQS, BLOCKS), jnp.int32),
            pltpu.SMEM((SEQS, BLOCKS), jnp.int32),
            pltpu.SMEM((16,), jnp.int32),
            pltpu.VMEM((32, 64, LANES), bf16),
            pltpu.VMEM((32, 64, 64), bf16),
            pltpu.VMEM((SEQS, 64, 2 * LANES), bf16),
            pltpu.VMEM((SEQS, 64, TOK), bf16),
            pltpu.VMEM((SEQS, TOK, 64), bf16),
            pltpu.VMEM((4, NEW_AT, LANES), bf16),
            pltpu.VMEM((SEQS, NEW_ROWS, LANES), bf16),
            pltpu.SemaphoreType.DMA((6,)),
            pltpu.SemaphoreType.DMA((8,)),
        ],
        compiler_params=params(63),
        name="pack",
    )(block_owner, block_slot, cache_latent, cache_rope, new_latent, jnp.swapaxes(new_rope, 1, 2))
    send, query_nope, query_rope, owner = lax.optimization_barrier(
        (send, query_nope, query_rope, block_owner)
    )
    plan = pl.pallas_call(
        plan_kernel,
        out_shape=shape((SEQS, BLOCKS), jnp.int32),
        in_specs=[smem()],
        out_specs=smem(),
        scratch_shapes=[pltpu.SMEM((16,), jnp.int32)],
        name="plan",
    )(owner)
    recv = lax.all_to_all(send.reshape(16, MSG_ROWS, LANES), PLANE, 0, 0)
    query = jnp.concatenate([query_nope, query_rope], -1)
    queries = []
    for k in range(4):
        part = lax.dynamic_index_in_dim(query, lax.rem(y + k, 4), 0, keepdims=False)
        if k == 3:
            part, plan = lax.optimization_barrier((part, plan))
        if k:
            part = lax.ppermute(part, "y", [(i, (i + k) % 4) for i in range(4)])
        queries.append(part)
    picked, new_own = pl.pallas_call(
        select_kernel,
        out_shape=(shape((8, PICK_ROWS, LANES)), shape((16, NEW_ROWS, LANES))),
        in_specs=[smem(), anywhere()],
        out_specs=(anywhere(), anywhere()),
        scratch_shapes=[
            pltpu.VMEM((PICK_ROWS, LANES), bf16),
            pltpu.VMEM((BLOCKS, PIECE, LANES), bf16),
            pltpu.VMEM((BLOCKS // 2 * PIECE, LANES), bf16),
            pltpu.SemaphoreType.DMA((2 * BLOCKS + 1,)),
            pltpu.SemaphoreType.DMA((8,)),
        ],
        compiler_params=params(16),
        name="select",
    )(plan, recv)
    picked, new_own, *queries = lax.optimization_barrier((picked, new_own, *queries))
    swap = [(0, 1), (1, 0)]
    new_own = new_own.reshape(2, 2, 4, NEW_ROWS, LANES)
    new_other = lax.ppermute(new_own, "core", swap)
    cache_own = lax.all_to_all(picked, SPREAD, 0, 0).reshape(2, 2, 2, PICK_ROWS, LANES)

    rows = 8 * TOK
    stats, part, token = pl.pallas_call(
        new_kernel,
        out_shape=(
            shape((8, rows), f32),
            shape((4, TOK, 256), f32),
            shape((8, LANES), f32),
        ),
        in_specs=[anywhere()] * 4 + [vmem()] * 4,
        out_specs=(vmem(),) * 3,
        scratch_shapes=[
            pltpu.VMEM((4, TOK, 384), bf16),
            pltpu.VMEM((rows, 768), bf16),
            pltpu.VMEM((4, 2, 4, 32, 640), bf16),
            pltpu.SemaphoreType.DMA((4,)),
        ],
        compiler_params=params(24),
        cost_estimate=pl.CostEstimate(flops=3 * 10**9, bytes_accessed=5 * 10**6, transcendentals=700000),
        name="attend_new",
    )(*queries, key_up, value_up, new_own, new_other)
    cache_own, token = lax.optimization_barrier((cache_own, token))
    cache_other = lax.ppermute(cache_own, "core", swap)
    mixed = pl.pallas_call(
        cached_kernel,
        out_shape=shape((4, TOK, 256)),
        in_specs=[smem()] + [anywhere()] * 4 + [vmem()] * 7,
        out_specs=vmem(),
        scratch_shapes=[
            pltpu.VMEM((4, TOK, 384), bf16),
            pltpu.VMEM((rows, 768), bf16),
            pltpu.VMEM((2, 4 * PICK_LAT // 2, 640), bf16),
            pltpu.SemaphoreType.DMA((4,)),
        ],
        compiler_params=params(24),
        cost_estimate=pl.CostEstimate(flops=4 * 10**9, bytes_accessed=5 * 10**6, transcendentals=1600000),
        name="attend_cached",
    )(cached_len, *queries, key_up, value_up, cache_own, cache_other, stats, part, token)
    return lax.all_to_all(mixed, "y", 0, 0)


def solution(mesh):
    fine = Mesh(
        mesh.devices.reshape(4, 2, 8, 2, 2, 2), ("y", "xh", "zh", "zp", "core", "xl")
    )
    ctx = ("y", "xh")
    heads = ("zh", "zp", "core", "xl")
    holders = ("y", "xh", "xl")
    return jax.shard_map(
        on_device,
        mesh=fine,
        in_specs=(
            P(None, ctx, heads),
            P(None, ctx, heads),
            P(heads, None, None),
            P(heads, None, None),
            P(None, ctx, None),
            P(None, ctx, None),
            P(holders, None, None),
            P(holders, None, None),
            P(),
            P(),
            P(),
        ),
        out_specs=P(None, ctx, heads),
        check_vma=False,
    )
```

time: 81.8 us -> 77.2 us (0.944)
  local copies, waits for them, and re-layouts: 3.37 us -> 0.84 us
  waiting for transfers between devices: 15.2 us -> 13.3 us
    all_to_all x1, waiting for transfers between devices: 8.2 us -> 5.47 us  [on_device(): recv = lax.all_to_all(send.reshape(16, MSG_ROWS, LANES), PLANE, 0, 0)]
    unnamed x18 -> x14, local copies, waits for them, and re-layouts: 3.28 us -> 0.76 us
    ppermute x3, waiting for transfers between devices: 1.77 us -> 3.64 us  [on_device(): part = lax.ppermute(part, 'y', [(i, (i + k) % 4) for i in range(4)])]
    all_to_all x1, waiting for transfers between devices: 1.79 us -> 0.79 us  [on_device(): lax.all_to_all(picked, SPREAD, 0, 0).reshape(2, 2, 2, PICK_ROWS, LANES)]
  transfers between devices with their start and end apart: 7 -> 7, of which waited for: 5 -> 6; matrix products, arithmetic and copies ran while one was open for 0% -> 0% of each run, Pallas kernels for 12% -> 14%
where the time goes in v3:
time: 77.2 us; the launch traced here: 76.4 us
  starting transfers between devices  31.9 us (41%)
  Pallas kernels  21.2 us (27%)
  waiting for transfers between devices  13.3 us (17%)
  blocking collectives  8.94 us (12%)
  local copies, waits for them, and re-layouts  0.84 us (1%)
    ppermute x3, starting transfers between devices, on_device(): part = lax.ppermute(part, 'y', [(i, (i + k) % 4) for i in range(4)])  9.56 us
    all_to_all x1, blocking collectives, on_device(): return lax.all_to_all(mixed, 'y', 0, 0)  8.94 us
    pallas_call x1, Pallas kernels, on_device(): pl.pallas_call(cached_kernel, out_shape=shape((4, TOK, 256)), in_specs=[s...  7.95 us
    all_to_all x1, starting transfers between devices, on_device(): recv = lax.all_to_all(send.reshape(16, MSG_ROWS, LANES), PLANE, 0, 0)  7.73 us
    ppermute x1, starting transfers between devices, on_device(): cache_other = lax.ppermute(cache_own, 'core', swap)  5.85 us
    all_to_all x1, waiting for transfers between devices, on_device(): recv = lax.all_to_all(send.reshape(16, MSG_ROWS, LANES), PLANE, 0, 0)  5.47 us
    pallas_call x1, Pallas kernels, on_device(): pl.pallas_call(new_kernel, out_shape=(shape((8, rows), f32), shape((4, TO...  5.01 us
    all_to_all x1, starting transfers between devices, on_device(): lax.all_to_all(picked, SPREAD, 0, 0).reshape(2, 2, 2, PICK_ROWS, LANES)  4.6 us
  transfers between devices with their start and end apart: 7, of which 6 were waited for; matrix products, arithmetic and copies ran while one was open for 0% of the time, Pallas kernels for 14%

profile of v3, /device:TPU:1, one launch (start us, length us, event | category | flops | bytes accessed | tf_op | source)
XLA Modules:
  0.0 76.4 jit_solution(14636651086224293314)
XLA Ops:
  0.0 2.5 %pack.1 = bf16[4,4,368,128]{3,2,1,0:T(8,128)(2,1)} custom-call(s32[4,24]{1,0:T(4,128)} %owner.2, s32[4,24]{1,0:T(4,128)} %slot.1, bf16[32,64,512]{2,1,0:T(8,128)(2,1)} %cache_latent.1, bf16[32,64,64]{2,1,0:T(8,128)(2,1)} %cache_rope.1, bf16[4,128,512]{2,1,0:T(8,128)(2,1)} %new_latent.1, bf16[4,64,128]{2,1,0:T(8,128)(2,1)} %bitcast.17), custom_call_target="tpu_custom_call" | custom-call | tf_op jit(solution)/shard_map/pack/pallas_call | solution.py:383
  2.5 0.0 copy-start.4
  2.5 0.0 copy-start.5
  2.5 7.7 %all-to-all-start = ((bf16[16,368,128]{2,1,0:T(8,128)(2,1)}), bf16[16,368,128]{2,1,0:T(8,128)(2,1)S(1)}, u32[]{:S(2)}, u32[]{:S(2)}) async-start(bf16[16,368,128]{2,1,0:T(8,128)(2,1)} %bitcast.16), calls=%async_computation | async-start | bytes 3014656 | tf_op jit(solution)/shard_map/all_to_all | solution.py:416
  10.3 2.6 %plan.1 = s32[4,24]{1,0:T(4,128)} custom-call(s32[4,24]{1,0:T(4,128)} %owner.2), custom_call_target="tpu_custom_call" | custom-call | tf_op jit(solution)/shard_map/plan/pallas_call | solution.py:408
  12.9 0.0 copy-start
  13.0 0.1 dynamic-slice_bitcast_fusion
  13.0 4.5 %collective-permute-start.2 = (bf16[128,384]{1,0:T(8,128)(2,1)S(1)}, bf16[128,384]{1,0:T(8,128)(2,1)S(1)}, u32[]{:S(2)}, u32[]{:S(2)}) collective-permute-start(bf16[128,384]{1,0:T(8,128)(2,1)S(1)} %get-tuple-element.31), channel_id=1, source_target_pairs={{0,384},{128,0},{256,128},{384,256},{1,385},{129,1},{257,129},{385... | collective-permute-start | bytes 294920 | tf_op jit(solution)/shard_map/ppermute | solution.py:424
  17.5 2.5 %collective-permute-start.1 = (bf16[128,384]{1,0:T(8,128)(2,1)S(1)}, bf16[128,384]{1,0:T(8,128)(2,1)S(1)}, u32[]{:S(2)}, u32[]{:S(2)}) collective-permute-start(bf16[128,384]{1,0:T(8,128)(2,1)S(1)} %get-tuple-element.43), channel_id=1, source_target_pairs={{0,256},{128,384},{256,0},{384,128},{1,257},{129,385},{257,1},{385... | collective-permute-start | bytes 294920 | tf_op jit(solution)/shard_map/ppermute | solution.py:424
  20.0 2.6 %collective-permute-start = (bf16[128,384]{1,0:T(8,128)(2,1)S(1)}, bf16[128,384]{1,0:T(8,128)(2,1)S(1)}, u32[]{:S(2)}, u32[]{:S(2)}) collective-permute-start(bf16[128,384]{1,0:T(8,128)(2,1)S(1)} %get-tuple-element.44), channel_id=1, source_target_pairs={{0,128},{128,256},{256,384},{384,0},{1,129},{129,257},{257,385},{3... | collective-permute-start | bytes 294920 | tf_op jit(solution)/shard_map/ppermute | solution.py:424
  22.7 5.5 %all-to-all-done.recv = bf16[16,368,128]{2,1,0:T(8,128)(2,1)S(1)} async-done(((bf16[16,368,128]{2,1,0:T(8,128)(2,1)}), bf16[16,368,128]{2,1,0:T(8,128)(2,1)S(1)}, u32[]{:S(2)}, u32[]{:S(2)}) %all-to-all-start) | async-done | bytes 1507360 | tf_op jit(solution)/shard_map/all_to_all | solution.py:416
  28.1 3.1 %select.9 = (bf16[8,432,128]{2,1,0:T(8,128)(2,1)}, bf16[16,144,128]{2,1,0:T(8,128)(2,1)S(1)}) custom-call(s32[4,24]{1,0:T(4,128)S(1)} %copy-done, bf16[16,368,128]{2,1,0:T(8,128)(2,1)S(1)} %all-to-all-done.recv), custom_call_target="tpu_custom_call" | custom-call | tf_op jit(solution)/shard_map/select/pallas_call | solution.py:426
  31.3 0.3 collective-permute-done.1.q2
  31.6 3.3 %collective-permute-done.q1 = bf16[128,384]{1,0:T(8,128)(2,1)S(1)} collective-permute-done((bf16[128,384]{1,0:T(8,128)(2,1)S(1)}, bf16[128,384]{1,0:T(8,128)(2,1)S(1)}, u32[]{:S(2)}, u32[]{:S(2)}) %collective-permute-start) | collective-permute-done | bytes 98336 | tf_op jit(solution)/shard_map/ppermute | solution.py:424
  34.9 4.6 %all-to-all-start.1 = ((bf16[8,432,128]{2,1,0:T(8,128)(2,1)}), bf16[8,432,128]{2,1,0:T(8,128)(2,1)S(1)}, u32[]{:S(2)}, u32[]{:S(2)}) async-start(bf16[8,432,128]{2,1,0:T(8,128)(2,1)} %get-tuple-element.36), calls=%async_computation.1 | async-start | bytes 1769472 | tf_op jit(solution)/shard_map/all_to_all | solution.py:445
  39.5 4.1 %collective-permute-start.3 = (bf16[2,2,4,144,128]{4,3,2,1,0:T(8,128)(2,1)S(1)}, bf16[2,2,4,144,128]{4,3,2,1,0:T(8,128)(2,1)S(1)}, u32[]{:S(2)}, u32[]{:S(2)}) collective-permute-start(bf16[2,2,4,144,128]{4,3,2,1,0:T(8,128)(2,1)S(1)} %bitcast.14), channel_id=1, source_target_pairs={{0,2},{2,0},{1,3},{3,1},{4,6},{6,4},{5,7},{7,5},{8,10},{10,8},{9,1... | collective-permute-start | bytes 1769480 | tf_op jit(solution)/shard_map/ppermute | solution.py:444
  43.6 1.6 %collective-permute-done.3.other = bf16[2,2,4,144,128]{4,3,2,1,0:T(8,128)(2,1)S(1)} collective-permute-done((bf16[2,2,4,144,128]{4,3,2,1,0:T(8,128)(2,1)S(1)}, bf16[2,2,4,144,128]{4,3,2,1,0:T(8,128)(2,1)S(1)}, u32[]{:S(2)}, u32[]{:S(2)}) %collective-permute-start.3) | collective-permute-done | bytes 589856 | tf_op jit(solution)/shard_map/ppermute | solution.py:444
  45.3 5.0 %attend_new.1 = (f32[8,1024]{1,0:T(8,128)S(1)}, f32[4,128,256]{2,1,0:T(8,128)S(1)}, f32[8,128]{1,0:T(8,128)S(1)}) custom-call(bf16[128,384]{1,0:T(8,128)(2,1)S(1)} %get-tuple-element.32.q0, bf16[128,384]{1,0:T(8,128)(2,1)S(1)} %collective-permute-done.q1, bf16[128,384]{1,0:T(8,128)(2,1)S(1)} %collective-permute-done.1.q2, ...), custom_call_target="tpu_custom_call" | custom-call | flops 3000000000 | bytes 5000000 | tf_op jit(solution)/shard_map/attend_new/pallas_call | solution.py:448
  50.3 0.8 %all-to-all-done.1 = bf16[8,432,128]{2,1,0:T(8,128)(2,1)S(1)} async-done(((bf16[8,432,128]{2,1,0:T(8,128)(2,1)}), bf16[8,432,128]{2,1,0:T(8,128)(2,1)S(1)}, u32[]{:S(2)}, u32[]{:S(2)}) %all-to-all-start.1) | async-done | bytes 884768 | tf_op jit(solution)/shard_map/all_to_all | solution.py:445
  51.1 5.9 %collective-permute-start.4 = (bf16[2,2,2,432,128]{4,3,2,1,0:T(8,128)(2,1)S(1)}, bf16[2,2,2,432,128]{4,3,2,1,0:T(8,128)(2,1)S(1)}, u32[]{:S(2)}, u32[]{:S(2)}) collective-permute-start(bf16[2,2,2,432,128]{4,3,2,1,0:T(8,128)(2,1)S(1)} %bitcast.12), channel_id=1, source_target_pairs={{0,2},{2,0},{1,3},{3,1},{4,6},{6,4},{5,7},{7,5},{8,10},{10,8},{9,1... | collective-permute-start | bytes 2654216 | tf_op jit(solution)/shard_map/ppermute | solution.py:468
  56.9 1.9 %collective-permute-done.4.other = bf16[2,2,2,432,128]{4,3,2,1,0:T(8,128)(2,1)S(1)} collective-permute-done((bf16[2,2,2,432,128]{4,3,2,1,0:T(8,128)(2,1)S(1)}, bf16[2,2,2,432,128]{4,3,2,1,0:T(8,128)(2,1)S(1)}, u32[]{:S(2)}, u32[]{:S(2)}) %collective-permute-start.4) | collective-permute-done | bytes 884768 | tf_op jit(solution)/shard_map/ppermute | solution.py:468
  58.8 8.0 %attend_cached.1 = bf16[4,128,256]{2,1,0:T(8,128)(2,1)S(1)} custom-call(s32[4]{0:T(128)S(1)} %copy-done.3, bf16[128,384]{1,0:T(8,128)(2,1)S(1)} %get-tuple-element.32.q0, bf16[128,384]{1,0:T(8,128)(2,1)S(1)} %collective-permute-done.q1, bf16[128,384]{1,0:T(8,128)(2,1)S(1)} %collective-permute-done.1.q2, bf16[128,384]{1,0:T(8,128)(2,1)S(1)} %collective-permute-done.2.q3, ...), custom_call_target="tpu_custom_call" | custom-call | flops 4000000000 | bytes 5000000 | tf_op jit(solution)/shard_map/attend_cached/pallas_call | solution.py:469
  66.7 8.9 %all_to_all.15 = bf16[4,128,256]{2,1,0:T(8,128)(2,1)S(1)} all-to-all(bf16[4,128,256]{2,1,0:T(8,128)(2,1)S(1)} %attend_cached.1), channel_id=1, replica_groups=mesh['y'=4,'xh'=2,'zh'=8,'zp'=2,'core'=2,'xl'=2] {'y'}, dimensions={0} | all-to-all | bytes 524288 | tf_op jit(solution)/shard_map/all_to_all | solution.py:484
  75.7 0.7 copy.14
  (12 shorter events, 0.1 us)
Async XLA Ops:
  2.5 10.4 %copy-start.4 = (bf16[4,128,256]{2,1,0:T(8,128)(2,1)S(1)}, bf16[4,128,256]{2,1,0:T(8,128)(2,1)}, u32[]{:S(2)}) copy-start(bf16[4,128,256]{2,1,0:T(8,128)(2,1)} %param.11) | copy-start | bytes 786436
  2.5 10.4 %copy-start.5 = (bf16[4,128,128]{2,1,0:T(8,128)(2,1)S(1)}, bf16[4,128,128]{2,1,0:T(8,128)(2,1)}, u32[]{:S(2)}) copy-start(bf16[4,128,128]{2,1,0:T(8,128)(2,1)} %param.12) | copy-start | bytes 393220
  2.5 25.6 %all-to-all-start = ((bf16[16,368,128]{2,1,0:T(8,128)(2,1)}), bf16[16,368,128]{2,1,0:T(8,128)(2,1)S(1)}, u32[]{:S(2)}, u32[]{:S(2)}) async-start(bf16[16,368,128]{2,1,0:T(8,128)(2,1)} %bitcast.16), calls=%async_computation | async-start | bytes 3014656 | tf_op jit(solution)/shard_map/all_to_all | solution.py:416
  12.9 15.3 %copy-start = (s32[4,24]{1,0:T(4,128)S(1)}, s32[4,24]{1,0:T(4,128)}, u32[]{:S(2)}) copy-start(s32[4,24]{1,0:T(4,128)} %plan.1) | copy-start | bytes 1156
  13.0 18.2 %collective-permute-start.2 = (bf16[128,384]{1,0:T(8,128)(2,1)S(1)}, bf16[128,384]{1,0:T(8,128)(2,1)S(1)}, u32[]{:S(2)}, u32[]{:S(2)}) collective-permute-start(bf16[128,384]{1,0:T(8,128)(2,1)S(1)} %get-tuple-element.31), channel_id=1, source_target_pairs={{0,384},{128,0},{256,128},{384,256},{1,385},{129,1},{257,129},{385... | collective-permute-start | bytes 294920 | tf_op jit(solution)/shard_map/ppermute | solution.py:424
  17.5 14.1 %collective-permute-start.1 = (bf16[128,384]{1,0:T(8,128)(2,1)S(1)}, bf16[128,384]{1,0:T(8,128)(2,1)S(1)}, u32[]{:S(2)}, u32[]{:S(2)}) collective-permute-start(bf16[128,384]{1,0:T(8,128)(2,1)S(1)} %get-tuple-element.43), channel_id=1, source_target_pairs={{0,256},{128,384},{256,0},{384,128},{1,257},{129,385},{257,1},{385... | collective-permute-start | bytes 294920 | tf_op jit(solution)/shard_map/ppermute | solution.py:424
  20.0 25.3 %copy-start.1 = (bf16[2,128,512]{2,1,0:T(8,128)(2,1)S(1)}, bf16[2,128,512]{2,1,0:T(8,128)(2,1)}, u32[]{:S(2)}) copy-start(bf16[2,128,512]{2,1,0:T(8,128)(2,1)} %key_up.3) | copy-start | bytes 786436
  20.0 25.2 %copy-start.2 = (bf16[2,512,128]{2,1,0:T(8,128)(2,1)S(1)}, bf16[2,512,128]{2,1,0:T(8,128)(2,1)}, u32[]{:S(2)}) copy-start(bf16[2,512,128]{2,1,0:T(8,128)(2,1)} %value_up.3) | copy-start | bytes 786436
  20.0 14.9 %collective-permute-start = (bf16[128,384]{1,0:T(8,128)(2,1)S(1)}, bf16[128,384]{1,0:T(8,128)(2,1)S(1)}, u32[]{:S(2)}, u32[]{:S(2)}) collective-permute-start(bf16[128,384]{1,0:T(8,128)(2,1)S(1)} %get-tuple-element.44), channel_id=1, source_target_pairs={{0,128},{128,256},{256,384},{384,0},{1,129},{129,257},{257,385},{3... | collective-permute-start | bytes 294920 | tf_op jit(solution)/shard_map/ppermute | solution.py:424
  34.9 16.2 %all-to-all-start.1 = ((bf16[8,432,128]{2,1,0:T(8,128)(2,1)}), bf16[8,432,128]{2,1,0:T(8,128)(2,1)S(1)}, u32[]{:S(2)}, u32[]{:S(2)}) async-start(bf16[8,432,128]{2,1,0:T(8,128)(2,1)} %get-tuple-element.36), calls=%async_computation.1 | async-start | bytes 1769472 | tf_op jit(solution)/shard_map/all_to_all | solution.py:445
  39.5 19.3 %copy-start.3 = (s32[4]{0:T(128)S(1)}, s32[4]{0:T(128)}, u32[]{:S(2)}) copy-start(s32[4]{0:T(128)} %cached_len.1) | copy-start | bytes 52
  39.5 5.7 %collective-permute-start.3 = (bf16[2,2,4,144,128]{4,3,2,1,0:T(8,128)(2,1)S(1)}, bf16[2,2,4,144,128]{4,3,2,1,0:T(8,128)(2,1)S(1)}, u32[]{:S(2)}, u32[]{:S(2)}) collective-permute-start(bf16[2,2,4,144,128]{4,3,2,1,0:T(8,128)(2,1)S(1)} %bitcast.14), channel_id=1, source_target_pairs={{0,2},{2,0},{1,3},{3,1},{4,6},{6,4},{5,7},{7,5},{8,10},{10,8},{9,1... | collective-permute-start | bytes 1769480 | tf_op jit(solution)/shard_map/ppermute | solution.py:444
  51.1 7.7 %collective-permute-start.4 = (bf16[2,2,2,432,128]{4,3,2,1,0:T(8,128)(2,1)S(1)}, bf16[2,2,2,432,128]{4,3,2,1,0:T(8,128)(2,1)S(1)}, u32[]{:S(2)}, u32[]{:S(2)}) collective-permute-start(bf16[2,2,2,432,128]{4,3,2,1,0:T(8,128)(2,1)S(1)} %bitcast.12), channel_id=1, source_target_pairs={{0,2},{2,0},{1,3},{3,1},{4,6},{6,4},{5,7},{7,5},{8,10},{10,8},{9,1... | collective-permute-start | bytes 2654216 | tf_op jit(solution)/shard_map/ppermute | solution.py:468

commit v4 on v3

--- a/solution.py
+++ b/solution.py
@@ -21,12 +21,12 @@
 BLOCKS = 24
 TOK = 128
 LAT_ROWS = CAP * PIECE
-ROPE_ROWS = (CAP + 1) // 2 * PIECE
+ROPE_ROWS = (CAP + 3) // 4 * PIECE
 NEW_AT = LAT_ROWS + ROPE_ROWS
 NEW_ROWS = 2 * 64 + 16
 MSG_ROWS = NEW_AT + NEW_ROWS
 PICK_LAT = BLOCKS * PIECE
-PICK_PART = BLOCKS // 2 * PIECE // 4
+PICK_PART = BLOCKS // 4 * PIECE // 2
 PICK_ROWS = PICK_LAT + PICK_PART
 MIB = 1024 * 1024
 bf16 = jnp.bfloat16
@@ -110,10 +110,12 @@
     for r in range(CAP):
         for i, x in enumerate(flipped):
             cached_part[i, r * PIECE : (r + 1) * PIECE, :] = lat[blocks[r], x * PIECE : (x + 1) * PIECE, :]
-    for m in range((CAP + 1) // 2):
-        first = rope[blocks[2 * m]]
-        second = rope[blocks[2 * m + 1]] if 2 * m + 1 < CAP else first
-        both = jnp.concatenate([first, second], axis=1)
+    for m in range((CAP + 3) // 4):
+        quarter = []
+        for r in range(4 * m, 4 * m + 4):
+            whole = rope[blocks[min(r, CAP - 1)]]
+            quarter.append(jnp.where(core == 0, whole[:, 0:32], whole[:, 32:64]))
+        both = jnp.concatenate(quarter, axis=1)
         for i, x in enumerate(flipped):
             cached_part[i, LAT_ROWS + m * PIECE : LAT_ROWS + (m + 1) * PIECE, :] = both[
                 x * PIECE : (x + 1) * PIECE, :
@@ -126,55 +128,50 @@
         c.wait()
 
 
-def plan_kernel(owner, plan, counts):
-    for h in range(16):
-        counts[h] = 0
+def plan_kernel(owner, plan):
+    low, high = jnp.int32(0), jnp.int32(0)
     for s in range(SEQS):
         for j in range(BLOCKS):
             h = owner[s, j]
-            rank = counts[h]
-            counts[h] = rank + 1
-            source = (h % 2 * 2 + h // 2 % 2) * 4 + h // 4
+            shift = (h & 7) * 4
+            first = h < 8
+            rank = (jnp.where(first, low, high) >> shift) & 15
+            one = jnp.int32(1) << shift
+            low = low + jnp.where(first, one, 0)
+            high = high + jnp.where(first, 0, one)
+            source = ((h & 1) * 2 + ((h >> 1) & 1)) * 4 + (h >> 2)
             plan[s, j] = source * 16 + jnp.minimum(rank, CAP - 1)
 
 
-def select_kernel(plan, recv, out, new_out, picked, tiles, pairs, sems, out_sems):
-    core, zp, seq = coords("core", "zp", "y")
+def select_kernel(plan, recv, out, new_out, cached, picked, packed, sems, out_sems):
+    zp, seq = coords("zp", "y")
+    arrive = pltpu.make_async_copy(recv.at[:, pl.ds(0, NEW_AT), :], cached, sems.at[0])
+    arrive.start()
     entries = [plan[seq, j] for j in range(BLOCKS)]
-    ranks = [e % 16 for e in entries]
-    sources = [e // 16 for e in entries]
-    rope_copies, lat_copies = [], []
-    for j in range(BLOCKS):
-        c = pltpu.make_async_copy(
-            recv.at[sources[j], pl.ds(pl.multiple_of(LAT_ROWS + ranks[j] // 2 * PIECE, PIECE), PIECE), :],
-            tiles.at[j],
-            sems.at[2 * j + 1],
-        )
-        c.start()
-        rope_copies.append(c)
-    for j in range(BLOCKS):
-        c = pltpu.make_async_copy(
-            recv.at[sources[j], pl.ds(pl.multiple_of(ranks[j] * PIECE, PIECE), PIECE), :],
-            picked.at[pl.ds(j * PIECE, PIECE), :],
-            sems.at[2 * j],
-        )
-        c.start()
-        lat_copies.append(c)
+    ranks = [e & 15 for e in entries]
+    sources = [e >> 4 for e in entries]
     new_copy = pltpu.make_async_copy(
-        recv.at[:, pl.ds(NEW_AT, NEW_ROWS), :], new_out, sems.at[2 * BLOCKS]
+        recv.at[:, pl.ds(NEW_AT, NEW_ROWS), :], new_out, sems.at[1]
     )
     new_copy.start()
-    for c in rope_copies:
-        c.wait()
-    for j in range(BLOCKS // 2):
-        k = j + BLOCKS // 2
-        first = jnp.where(ranks[j] % 2 == 1, tiles[j, :, 64:128], tiles[j, :, 0:64])
-        second = jnp.where(ranks[k] % 2 == 1, tiles[k, :, 64:128], tiles[k, :, 0:64])
-        pairs[j * PIECE : (j + 1) * PIECE, :] = jnp.concatenate([first, second], axis=1)
-    part = pl.ds(pl.multiple_of((core * 2 + zp) * PICK_PART, 16), PICK_PART)
-    picked[PICK_LAT:PICK_ROWS, :] = pairs[part, :]
-    for c in lat_copies:
-        c.wait()
+    arrive.wait()
+    for j in range(BLOCKS):
+        rows = pl.ds(pl.multiple_of(ranks[j] * PIECE, PIECE), PIECE)
+        picked[j * PIECE : (j + 1) * PIECE, :] = cached[sources[j], rows, :]
+
+    def rotary(j):
+        rows = pl.ds(pl.multiple_of(LAT_ROWS + (ranks[j] >> 2) * PIECE, PIECE), PIECE)
+        tile = cached[sources[j], rows, :]
+        odd = (ranks[j] & 1) == 1
+        left = jnp.where(odd, tile[:, 32:64], tile[:, 0:32])
+        right = jnp.where(odd, tile[:, 96:128], tile[:, 64:96])
+        return jnp.where((ranks[j] & 2) == 2, right, left)
+
+    for j in range(BLOCKS // 4):
+        packed[j * PIECE : (j + 1) * PIECE, :] = jnp.concatenate(
+            [rotary(j + e * BLOCKS // 4) for e in range(4)], axis=1
+        )
+    picked[PICK_LAT:PICK_ROWS, :] = packed[pl.ds(pl.multiple_of(zp * PICK_PART, 16), PICK_PART), :]
     out_copies = [pltpu.make_async_copy(picked, out.at[d], out_sems.at[d]) for d in range(8)]
     for c in out_copies:
         c.start()
@@ -276,65 +273,62 @@
             )
 
 
-def cached_kernel(
-    cached_len,
-    q0,
-    q1,
-    q2,
-    q3,
-    key_up,
-    value_up,
-    own,
-    other,
-    stats,
-    new_part,
-    token,
-    out,
-    query,
-    joint,
-    keys,
-    sems,
-):
+def prepare_kernel(q0, q1, q2, q3, key_up, joint, query, sems):
+    (core,) = coords("core")
+    for c in gather_query((q0, q1, q2, q3), query, sems):
+        c.wait()
+    pad = jnp.zeros((TOK, 64), bf16)
+    for chunk in range(4):
+        for h in range(2):
+            rows = pl.ds((2 * chunk + h) * TOK, TOK)
+            nope = query[chunk, :, h * 128 : (h + 1) * 128]
+            pos = query[chunk, :, 256 + h * 64 : 256 + (h + 1) * 64]
+            for i, cols in enumerate(halves(core)):
+                joint[rows, i * 256 : (i + 1) * 256] = dot(nope, key_up[h, :, cols]).astype(bf16)
+            pos = jnp.where(core == 0, pos, jnp.concatenate([pos[:, 32:64], pos[:, 0:32]], axis=1))
+            joint[rows, 512:640] = jnp.concatenate([pos, pad], axis=1)
+
+
+def cached_kernel(cached_len, joint, value_up, own, other, stats, new_part, token, out, keys):
     core, seq = coords("core", "y")
-    query_copies = gather_query((q0, q1, q2, q3), query, sems)
-    span = PICK_LAT // 2
-    for i, (which, ref) in enumerate(((core, own), (1 - core, other))):
-        for zp in range(2):
-            rope_at = (which * 2 + zp) * PICK_PART
-            for x in range(4):
-                for half in range(2):
-                    keys[half, x * span : (x + 1) * span, (2 * i + zp) * LANES : (2 * i + zp + 1) * LANES] = ref[
-                        x % 2, x // 2, zp, half * span : (half + 1) * span, :
+    span = PICK_LAT // 4
+    pad = jnp.zeros((span, 64), bf16)
+    for x in range(4):
+        for i, ref in enumerate((own, other)):
+            for zp in range(2):
+                for e in range(4):
+                    start = (e * 4 + x) * span
+                    keys[start : start + span, (2 * i + zp) * LANES : (2 * i + zp + 1) * LANES] = ref[
+                        x % 2, x // 2, zp, e * span : (e + 1) * span, :
                     ]
-                    keys[half, pl.ds(pl.multiple_of(x * span + rope_at, 16), PICK_PART), 512:640] = ref[
-                        x % 2, x // 2, zp, PICK_LAT:PICK_ROWS, :
-                    ]
-    count = 4 * span
+        packed = [
+            jnp.concatenate([ref[x % 2, x // 2, zp, PICK_LAT:PICK_ROWS, :] for zp in range(2)], axis=0)
+            for ref in (own, other)
+        ]
+        for e in range(4):
+            start = (e * 4 + x) * span
+            lanes = slice(32 * e, 32 * e + 32)
+            keys[start : start + span, 512:640] = jnp.concatenate(
+                [packed[0][:, lanes], packed[1][:, lanes], pad], axis=1
+            )
+    count = 16 * span
     index = lax.broadcasted_iota(jnp.int32, (1, count), 1)
     rest = index % span
-    position = rest // PIECE * 64 + index // span * PIECE + rest % PIECE
+    position = (index // (4 * span) * (BLOCKS // 4) + rest // PIECE) * 64
+    position = position + index // span % 4 * PIECE + rest % PIECE
     length = cached_len[seq]
-    bias = [
-        jnp.where(position + half * (BLOCKS // 2 * 64) < length, 0.0, NEG).astype(f32)
-        for half in range(2)
-    ]
-    for c in query_copies:
-        c.wait()
-    for chunk in range(4):
-        joint_query(query, key_up, core, chunk, joint)
+    bias = jnp.where(position < length, 0.0, NEG).astype(f32)
     rows = 4 * TOK
     for group in range(2):
         at = slice(group * rows, (group + 1) * rows)
-        q = load_query(joint, group * rows, rows)
-        scores = [dot_t(q[half], keys[half]) + bias[half] for half in range(2)]
+        scores = dot_t(joint[at, :], keys[...]) + bias
         state = jnp.concatenate([stats[:, at]] * 16, axis=0).T
         before, denom_before = state[:, 0:1], state[:, 1:2]
-        top = functools.reduce(jnp.maximum, [before] + [jnp.max(s, -1, keepdims=True) for s in scores])
+        top = jnp.maximum(before, jnp.max(scores, -1, keepdims=True))
         factor = jnp.exp2((before - top) * EXP_SCALE) * denom_before
-        expo = [jnp.exp2((s - top) * EXP_SCALE) for s in scores]
-        denom = functools.reduce(jnp.add, [factor] + [jnp.sum(e, -1, keepdims=True) for e in expo])
-        weights = jnp.concatenate([e.astype(bf16) for e in expo], axis=1)
-        total = dot(weights, keys[:, :, 0:512].reshape(2 * count, 512))
+        expo = jnp.exp2((scores - top) * EXP_SCALE)
+        denom = factor + jnp.sum(expo, -1, keepdims=True)
+        total = dot(expo.astype(bf16), keys[:, 0:512])
         share = factor / denom
         mixed = (total / denom).astype(bf16)
         for c in range(2):
@@ -410,7 +404,6 @@
         out_shape=shape((SEQS, BLOCKS), jnp.int32),
         in_specs=[smem()],
         out_specs=smem(),
-        scratch_shapes=[pltpu.SMEM((16,), jnp.int32)],
         name="plan",
     )(owner)
     recv = lax.all_to_all(send.reshape(16, MSG_ROWS, LANES), PLANE, 0, 0)
@@ -429,10 +422,10 @@
         in_specs=[smem(), anywhere()],
         out_specs=(anywhere(), anywhere()),
         scratch_shapes=[
+            pltpu.VMEM((16, NEW_AT, LANES), bf16),
             pltpu.VMEM((PICK_ROWS, LANES), bf16),
-            pltpu.VMEM((BLOCKS, PIECE, LANES), bf16),
-            pltpu.VMEM((BLOCKS // 2 * PIECE, LANES), bf16),
-            pltpu.SemaphoreType.DMA((2 * BLOCKS + 1,)),
+            pltpu.VMEM((BLOCKS // 4 * PIECE, LANES), bf16),
+            pltpu.SemaphoreType.DMA((2,)),
             pltpu.SemaphoreType.DMA((8,)),
         ],
         compiler_params=params(16),
@@ -464,23 +457,30 @@
         cost_estimate=pl.CostEstimate(flops=3 * 10**9, bytes_accessed=5 * 10**6, transcendentals=700000),
         name="attend_new",
     )(*queries, key_up, value_up, new_own, new_other)
-    cache_own, token = lax.optimization_barrier((cache_own, token))
+    cache_own, token, *queries = lax.optimization_barrier((cache_own, token, *queries))
     cache_other = lax.ppermute(cache_own, "core", swap)
+    joint = pl.pallas_call(
+        prepare_kernel,
+        out_shape=shape((rows, 640)),
+        in_specs=[anywhere()] * 4 + [vmem()],
+        out_specs=vmem(),
+        scratch_shapes=[pltpu.VMEM((4, TOK, 384), bf16), pltpu.SemaphoreType.DMA((4,))],
+        compiler_params=params(16),
+        cost_estimate=pl.CostEstimate(flops=2 * 10**8, bytes_accessed=2 * 10**6, transcendentals=0),
+        name="prepare",
+    )(*queries, key_up)
     mixed = pl.pallas_call(
         cached_kernel,
         out_shape=shape((4, TOK, 256)),
-        in_specs=[smem()] + [anywhere()] * 4 + [vmem()] * 7,
+        in_specs=[smem()] + [vmem()] * 7,
         out_specs=vmem(),
         scratch_shapes=[
-            pltpu.VMEM((4, TOK, 384), bf16),
-            pltpu.VMEM((rows, 768), bf16),
-            pltpu.VMEM((2, 4 * PICK_LAT // 2, 640), bf16),
-            pltpu.SemaphoreType.DMA((4,)),
+            pltpu.VMEM((4 * PICK_LAT, 640), bf16),
         ],
         compiler_params=params(24),
         cost_estimate=pl.CostEstimate(flops=4 * 10**9, bytes_accessed=5 * 10**6, transcendentals=1600000),
         name="attend_cached",
-    )(cached_len, *queries, key_up, value_up, cache_own, cache_other, stats, part, token)
+    )(cached_len, joint, value_up, cache_own, cache_other, stats, part, token)
     return lax.all_to_all(mixed, "y", 0, 0)
 
 

time: 77.2 us -> 74.3 us (0.962)
  starting transfers between devices: 31.9 us -> 29.6 us
  Pallas kernels: 21.2 us -> 19.1 us
  waiting for transfers between devices: 13.3 us -> 15.3 us
    all_to_all x1, waiting for transfers between devices: 0.79 us -> 3.68 us  [on_device(): lax.all_to_all(picked, SPREAD, 0, 0).reshape(2, 2, 2, PICK_ROWS, LANES)]
    ppermute x3, waiting for transfers between devices: 3.64 us -> 5.67 us  [on_device(): part = lax.ppermute(part, 'y', [(i, (i + k) % 4) for i in range(4)])]
    all_to_all x1, waiting for transfers between devices: 5.47 us -> 3.58 us  [on_device(): recv = lax.all_to_all(send.reshape(16, MSG_ROWS, LANES), PLANE, 0, 0)]
    ppermute x1, starting transfers between devices: 5.85 us -> 4.14 us  [on_device(): cache_other = lax.ppermute(cache_own, 'core', swap)]
    pallas_call x1, Pallas kernels: 7.95 us -> 6.46 us  [on_device(): pl.pallas_call(cached_kernel, out_shape=shape((4, TOK, 256)), in_specs=[s...]
    ppermute x1, starting transfers between devices: 4.13 us -> 2.79 us  [on_device(): new_other = lax.ppermute(new_own, 'core', swap)]
    ppermute x1, waiting for transfers between devices: 1.85 us -> 0.73 us  [on_device(): cache_other = lax.ppermute(cache_own, 'core', swap)]
    pallas_call x1, Pallas kernels: 3.13 us -> 2.02 us  [on_device(): pl.pallas_call(select_kernel, out_shape=(shape((8, PICK_ROWS, LANES)), sh...]
  transfers between devices with their start and end apart: 7 -> 7, of which waited for: 6 -> 7; matrix products, arithmetic and copies ran while one was open for 0% -> 0% of each run, Pallas kernels for 14% -> 14%
where the time goes in v4:
time: 74.3 us; the launch traced here: 73.8 us
  starting transfers between devices  29.6 us (40%)
  Pallas kernels  19.1 us (26%)
  waiting for transfers between devices  15.3 us (21%)
  blocking collectives  8.81 us (12%)
  local copies, waits for them, and re-layouts  0.85 us (1%)
    ppermute x3, starting transfers between devices, on_device(): part = lax.ppermute(part, 'y', [(i, (i + k) % 4) for i in range(4)])  10.2 us
    all_to_all x1, blocking collectives, on_device(): return lax.all_to_all(mixed, 'y', 0, 0)  8.81 us
    all_to_all x1, starting transfers between devices, on_device(): recv = lax.all_to_all(send.reshape(16, MSG_ROWS, LANES), PLANE, 0, 0)  7.73 us
    pallas_call x1, Pallas kernels, on_device(): pl.pallas_call(cached_kernel, out_shape=shape((4, TOK, 256)), in_specs=[s...  6.46 us
    ppermute x3, waiting for transfers between devices, on_device(): part = lax.ppermute(part, 'y', [(i, (i + k) % 4) for i in range(4)])  5.67 us
    pallas_call x1, Pallas kernels, on_device(): pl.pallas_call(new_kernel, out_shape=(shape((8, rows), f32), shape((4, TO...  4.97 us
    all_to_all x1, starting transfers between devices, on_device(): lax.all_to_all(picked, SPREAD, 0, 0).reshape(2, 2, 2, PICK_ROWS, LANES)  4.75 us
    ppermute x1, starting transfers between devices, on_device(): cache_other = lax.ppermute(cache_own, 'core', swap)  4.14 us
  transfers between devices with their start and end apart: 7, of which 7 were waited for; matrix products, arithmetic and copies ran while one was open for 0% of the time, Pallas kernels for 14%

profile of v4, /device:TPU:1, one launch (start us, length us, event | category | flops | bytes accessed | tf_op | source)
XLA Modules:
  0.0 73.8 jit_solution(8260631458075170197)
XLA Ops:
  0.0 2.6 %pack.1 = bf16[4,4,336,128]{3,2,1,0:T(8,128)(2,1)} custom-call(s32[4,24]{1,0:T(4,128)} %owner.2, s32[4,24]{1,0:T(4,128)} %slot.1, bf16[32,64,512]{2,1,0:T(8,128)(2,1)} %cache_latent.1, bf16[32,64,64]{2,1,0:T(8,128)(2,1)} %cache_rope.1, bf16[4,128,512]{2,1,0:T(8,128)(2,1)} %new_latent.1, bf16[4,64,128]{2,1,0:T(8,128)(2,1)} %bitcast.17), custom_call_target="tpu_custom_call" | custom-call | tf_op jit(solution)/shard_map/pack/pallas_call | solution.py:377
  2.6 0.0 copy-start.4
  2.6 7.7 %all-to-all-start = ((bf16[16,336,128]{2,1,0:T(8,128)(2,1)}), bf16[16,336,128]{2,1,0:T(8,128)(2,1)S(1)}, u32[]{:S(2)}, u32[]{:S(2)}) async-start(bf16[16,336,128]{2,1,0:T(8,128)(2,1)} %bitcast.16), calls=%async_computation | async-start | bytes 2752512 | tf_op jit(solution)/shard_map/all_to_all | solution.py:409
  10.4 2.0 %plan.1 = s32[4,24]{1,0:T(4,128)} custom-call(s32[4,24]{1,0:T(4,128)} %owner.2), custom_call_target="tpu_custom_call" | custom-call | tf_op jit(solution)/shard_map/plan/pallas_call | solution.py:402
  12.5 0.1 dynamic-slice_bitcast_fusion
  12.5 4.5 %collective-permute-start.2 = (bf16[128,384]{1,0:T(8,128)(2,1)S(1)}, bf16[128,384]{1,0:T(8,128)(2,1)S(1)}, u32[]{:S(2)}, u32[]{:S(2)}) collective-permute-start(bf16[128,384]{1,0:T(8,128)(2,1)S(1)} %get-tuple-element.35), channel_id=1, source_target_pairs={{0,384},{128,0},{256,128},{384,256},{1,385},{129,1},{257,129},{385... | collective-permute-start | bytes 294920 | tf_op jit(solution)/shard_map/ppermute | solution.py:417
  17.0 1.9 %collective-permute-start = (bf16[128,384]{1,0:T(8,128)(2,1)S(1)}, bf16[128,384]{1,0:T(8,128)(2,1)S(1)}, u32[]{:S(2)}, u32[]{:S(2)}) collective-permute-start(bf16[128,384]{1,0:T(8,128)(2,1)S(1)} %get-tuple-element.52), channel_id=1, source_target_pairs={{0,128},{128,256},{256,384},{384,0},{1,129},{129,257},{257,385},{3... | collective-permute-start | bytes 294920 | tf_op jit(solution)/shard_map/ppermute | solution.py:417
  18.9 3.8 %collective-permute-start.1 = (bf16[128,384]{1,0:T(8,128)(2,1)S(1)}, bf16[128,384]{1,0:T(8,128)(2,1)S(1)}, u32[]{:S(2)}, u32[]{:S(2)}) collective-permute-start(bf16[128,384]{1,0:T(8,128)(2,1)S(1)} %get-tuple-element.51), channel_id=1, source_target_pairs={{0,256},{128,384},{256,0},{384,128},{1,257},{129,385},{257,1},{385... | collective-permute-start | bytes 294920 | tf_op jit(solution)/shard_map/ppermute | solution.py:417
  22.7 3.6 %all-to-all-done.recv = bf16[16,336,128]{2,1,0:T(8,128)(2,1)S(1)} async-done(((bf16[16,336,128]{2,1,0:T(8,128)(2,1)}), bf16[16,336,128]{2,1,0:T(8,128)(2,1)S(1)}, u32[]{:S(2)}, u32[]{:S(2)}) %all-to-all-start) | async-done | bytes 1376288 | tf_op jit(solution)/shard_map/all_to_all | solution.py:409
  26.3 2.0 %select.9 = (bf16[8,432,128]{2,1,0:T(8,128)(2,1)}, bf16[16,144,128]{2,1,0:T(8,128)(2,1)S(1)}) custom-call(s32[4,24]{1,0:T(4,128)S(1)} %copy-done.1, bf16[16,336,128]{2,1,0:T(8,128)(2,1)S(1)} %all-to-all-done.recv), custom_call_target="tpu_custom_call" | custom-call | tf_op jit(solution)/shard_map/select/pallas_call | solution.py:419
  28.3 0.2 collective-permute-done.2.q3
  28.5 3.0 %collective-permute-done.q1 = bf16[128,384]{1,0:T(8,128)(2,1)S(1)} collective-permute-done((bf16[128,384]{1,0:T(8,128)(2,1)S(1)}, bf16[128,384]{1,0:T(8,128)(2,1)S(1)}, u32[]{:S(2)}, u32[]{:S(2)}) %collective-permute-start) | collective-permute-done | bytes 98336 | tf_op jit(solution)/shard_map/ppermute | solution.py:417
  31.5 2.6 %collective-permute-done.1.q2 = bf16[128,384]{1,0:T(8,128)(2,1)S(1)} collective-permute-done((bf16[128,384]{1,0:T(8,128)(2,1)S(1)}, bf16[128,384]{1,0:T(8,128)(2,1)S(1)}, u32[]{:S(2)}, u32[]{:S(2)}) %collective-permute-start.1) | collective-permute-done | bytes 98336 | tf_op jit(solution)/shard_map/ppermute | solution.py:417
  34.0 4.8 %all-to-all-start.1 = ((bf16[8,432,128]{2,1,0:T(8,128)(2,1)}), bf16[8,432,128]{2,1,0:T(8,128)(2,1)S(1)}, u32[]{:S(2)}, u32[]{:S(2)}) async-start(bf16[8,432,128]{2,1,0:T(8,128)(2,1)} %get-tuple-element.36), calls=%async_computation.1 | async-start | bytes 1769472 | tf_op jit(solution)/shard_map/all_to_all | solution.py:438
  38.8 2.8 %collective-permute-start.3 = (bf16[2,2,4,144,128]{4,3,2,1,0:T(8,128)(2,1)S(1)}, bf16[2,2,4,144,128]{4,3,2,1,0:T(8,128)(2,1)S(1)}, u32[]{:S(2)}, u32[]{:S(2)}) collective-permute-start(bf16[2,2,4,144,128]{4,3,2,1,0:T(8,128)(2,1)S(1)} %bitcast.14), channel_id=1, source_target_pairs={{0,2},{2,0},{1,3},{3,1},{4,6},{6,4},{5,7},{7,5},{8,10},{10,8},{9,1... | collective-permute-start | bytes 1769480 | tf_op jit(solution)/shard_map/ppermute | solution.py:437
  41.6 1.6 %collective-permute-done.3.other = bf16[2,2,4,144,128]{4,3,2,1,0:T(8,128)(2,1)S(1)} collective-permute-done((bf16[2,2,4,144,128]{4,3,2,1,0:T(8,128)(2,1)S(1)}, bf16[2,2,4,144,128]{4,3,2,1,0:T(8,128)(2,1)S(1)}, u32[]{:S(2)}, u32[]{:S(2)}) %collective-permute-start.3) | collective-permute-done | bytes 589856 | tf_op jit(solution)/shard_map/ppermute | solution.py:437
  43.2 5.0 %attend_new.1 = (f32[8,1024]{1,0:T(8,128)S(1)}, f32[4,128,256]{2,1,0:T(8,128)S(1)}, f32[8,128]{1,0:T(8,128)S(1)}) custom-call(bf16[128,384]{1,0:T(8,128)(2,1)S(1)} %get-tuple-element.43.q0, bf16[128,384]{1,0:T(8,128)(2,1)S(1)} %collective-permute-done.q1, bf16[128,384]{1,0:T(8,128)(2,1)S(1)} %collective-permute-done.1.q2, ...), custom_call_target="tpu_custom_call" | custom-call | flops 3000000000 | bytes 5000000 | tf_op jit(solution)/shard_map/attend_new/pallas_call | solution.py:441
  48.2 3.7 %all-to-all-done.1 = bf16[8,432,128]{2,1,0:T(8,128)(2,1)S(1)} async-done(((bf16[8,432,128]{2,1,0:T(8,128)(2,1)}), bf16[8,432,128]{2,1,0:T(8,128)(2,1)S(1)}, u32[]{:S(2)}, u32[]{:S(2)}) %all-to-all-start.1) | async-done | bytes 884768 | tf_op jit(solution)/shard_map/all_to_all | solution.py:438
  51.9 4.1 %collective-permute-start.4 = (bf16[2,2,2,432,128]{4,3,2,1,0:T(8,128)(2,1)S(1)}, bf16[2,2,2,432,128]{4,3,2,1,0:T(8,128)(2,1)S(1)}, u32[]{:S(2)}, u32[]{:S(2)}) collective-permute-start(bf16[2,2,2,432,128]{4,3,2,1,0:T(8,128)(2,1)S(1)} %bitcast.12), channel_id=1, source_target_pairs={{0,2},{2,0},{1,3},{3,1},{4,6},{6,4},{5,7},{7,5},{8,10},{10,8},{9,1... | collective-permute-start | bytes 2654216 | tf_op jit(solution)/shard_map/ppermute | solution.py:461
  56.0 1.1 %prepare.1.joint = bf16[1024,640]{1,0:T(8,128)(2,1)S(1)} custom-call(bf16[128,384]{1,0:T(8,128)(2,1)S(1)} %get-tuple-element.43.q0, bf16[128,384]{1,0:T(8,128)(2,1)S(1)} %collective-permute-done.q1, bf16[128,384]{1,0:T(8,128)(2,1)S(1)} %collective-permute-done.1.q2, bf16[128,384]{1,0:T(8,128)(2,1)S(1)} %collective-permute-done.2.q3, ...), custom_call_target="tpu_custom_call" | custom-call | flops 200000000 | bytes 2000000 | tf_op jit(solution)/shard_map/prepare/pallas_call | solution.py:462
  57.1 0.7 collective-permute-done.4.other
  57.9 6.5 %attend_cached.1 = bf16[4,128,256]{2,1,0:T(8,128)(2,1)S(1)} custom-call(s32[4]{0:T(128)S(1)} %copy-done.3, bf16[1024,640]{1,0:T(8,128)(2,1)S(1)} %prepare.1.joint, bf16[2,512,128]{2,1,0:T(8,128)(2,1)S(1)} %copy-done.2, bf16[2,2,2,432,128]{4,3,2,1,0:T(8,128)(2,1)S(1)} %bitcast.13, bf16[2,2,2,432,128]{4,3,2,1,0:T(8,128)(2,1)S(1)} %collective-permute-done.4.other, ...), custom_call_target="tpu_custom_call" | custom-call | flops 4000000000 | bytes 5000000 | tf_op jit(solution)/shard_map/attend_cached/pallas_call | solution.py:472
  64.3 8.8 %all_to_all.15 = bf16[4,128,256]{2,1,0:T(8,128)(2,1)S(1)} all-to-all(bf16[4,128,256]{2,1,0:T(8,128)(2,1)S(1)} %attend_cached.1), channel_id=1, replica_groups=mesh['y'=4,'xh'=2,'zh'=8,'zp'=2,'core'=2,'xl'=2] {'y'}, dimensions={0} | all-to-all | bytes 524288 | tf_op jit(solution)/shard_map/all_to_all | solution.py:484
  73.1 0.7 copy.14
  (13 shorter events, 0.1 us)
Async XLA Ops:
  2.6 9.8 %copy-start.4 = (bf16[4,128,256]{2,1,0:T(8,128)(2,1)S(1)}, bf16[4,128,256]{2,1,0:T(8,128)(2,1)}, u32[]{:S(2)}) copy-start(bf16[4,128,256]{2,1,0:T(8,128)(2,1)} %param.11) | copy-start | bytes 786436
  2.6 9.8 %copy-start.5 = (bf16[4,128,128]{2,1,0:T(8,128)(2,1)S(1)}, bf16[4,128,128]{2,1,0:T(8,128)(2,1)}, u32[]{:S(2)}) copy-start(bf16[4,128,128]{2,1,0:T(8,128)(2,1)} %param.12) | copy-start | bytes 393220
  2.6 23.7 %all-to-all-start = ((bf16[16,336,128]{2,1,0:T(8,128)(2,1)}), bf16[16,336,128]{2,1,0:T(8,128)(2,1)S(1)}, u32[]{:S(2)}, u32[]{:S(2)}) async-start(bf16[16,336,128]{2,1,0:T(8,128)(2,1)} %bitcast.16), calls=%async_computation | async-start | bytes 2752512 | tf_op jit(solution)/shard_map/all_to_all | solution.py:409
  12.3 14.0 %copy-start.1 = (s32[4,24]{1,0:T(4,128)S(1)}, s32[4,24]{1,0:T(4,128)}, u32[]{:S(2)}) copy-start(s32[4,24]{1,0:T(4,128)} %plan.1) | copy-start | bytes 1156
  12.5 16.0 %collective-permute-start.2 = (bf16[128,384]{1,0:T(8,128)(2,1)S(1)}, bf16[128,384]{1,0:T(8,128)(2,1)S(1)}, u32[]{:S(2)}, u32[]{:S(2)}) collective-permute-start(bf16[128,384]{1,0:T(8,128)(2,1)S(1)} %get-tuple-element.35), channel_id=1, source_target_pairs={{0,384},{128,0},{256,128},{384,256},{1,385},{129,1},{257,129},{385... | collective-permute-start | bytes 294920 | tf_op jit(solution)/shard_map/ppermute | solution.py:417
  17.0 14.5 %collective-permute-start = (bf16[128,384]{1,0:T(8,128)(2,1)S(1)}, bf16[128,384]{1,0:T(8,128)(2,1)S(1)}, u32[]{:S(2)}, u32[]{:S(2)}) collective-permute-start(bf16[128,384]{1,0:T(8,128)(2,1)S(1)} %get-tuple-element.52), channel_id=1, source_target_pairs={{0,128},{128,256},{256,384},{384,0},{1,129},{129,257},{257,385},{3... | collective-permute-start | bytes 294920 | tf_op jit(solution)/shard_map/ppermute | solution.py:417
  18.9 24.3 %copy-start = (bf16[2,128,512]{2,1,0:T(8,128)(2,1)S(1)}, bf16[2,128,512]{2,1,0:T(8,128)(2,1)}, u32[]{:S(2)}) copy-start(bf16[2,128,512]{2,1,0:T(8,128)(2,1)} %key_up.3) | copy-start | bytes 786436
  18.9 24.3 %copy-start.2 = (bf16[2,512,128]{2,1,0:T(8,128)(2,1)S(1)}, bf16[2,512,128]{2,1,0:T(8,128)(2,1)}, u32[]{:S(2)}) copy-start(bf16[2,512,128]{2,1,0:T(8,128)(2,1)} %value_up.3) | copy-start | bytes 786436
  18.9 15.1 %collective-permute-start.1 = (bf16[128,384]{1,0:T(8,128)(2,1)S(1)}, bf16[128,384]{1,0:T(8,128)(2,1)S(1)}, u32[]{:S(2)}, u32[]{:S(2)}) collective-permute-start(bf16[128,384]{1,0:T(8,128)(2,1)S(1)} %get-tuple-element.51), channel_id=1, source_target_pairs={{0,256},{128,384},{256,0},{384,128},{1,257},{129,385},{257,1},{385... | collective-permute-start | bytes 294920 | tf_op jit(solution)/shard_map/ppermute | solution.py:417
  34.0 17.8 %all-to-all-start.1 = ((bf16[8,432,128]{2,1,0:T(8,128)(2,1)}), bf16[8,432,128]{2,1,0:T(8,128)(2,1)S(1)}, u32[]{:S(2)}, u32[]{:S(2)}) async-start(bf16[8,432,128]{2,1,0:T(8,128)(2,1)} %get-tuple-element.36), calls=%async_computation.1 | async-start | bytes 1769472 | tf_op jit(solution)/shard_map/all_to_all | solution.py:438
  38.8 4.4 %collective-permute-start.3 = (bf16[2,2,4,144,128]{4,3,2,1,0:T(8,128)(2,1)S(1)}, bf16[2,2,4,144,128]{4,3,2,1,0:T(8,128)(2,1)S(1)}, u32[]{:S(2)}, u32[]{:S(2)}) collective-permute-start(bf16[2,2,4,144,128]{4,3,2,1,0:T(8,128)(2,1)S(1)} %bitcast.14), channel_id=1, source_target_pairs={{0,2},{2,0},{1,3},{3,1},{4,6},{6,4},{5,7},{7,5},{8,10},{10,8},{9,1... | collective-permute-start | bytes 1769480 | tf_op jit(solution)/shard_map/ppermute | solution.py:437
  48.2 9.7 %copy-start.3 = (s32[4]{0:T(128)S(1)}, s32[4]{0:T(128)}, u32[]{:S(2)}) copy-start(s32[4]{0:T(128)} %cached_len.1) | copy-start | bytes 52
  51.9 6.0 %collective-permute-start.4 = (bf16[2,2,2,432,128]{4,3,2,1,0:T(8,128)(2,1)S(1)}, bf16[2,2,2,432,128]{4,3,2,1,0:T(8,128)(2,1)S(1)}, u32[]{:S(2)}, u32[]{:S(2)}) collective-permute-start(bf16[2,2,2,432,128]{4,3,2,1,0:T(8,128)(2,1)S(1)} %bitcast.12), channel_id=1, source_target_pairs={{0,2},{2,0},{1,3},{3,1},{4,6},{6,4},{5,7},{7,5},{8,10},{10,8},{9,1... | collective-permute-start | bytes 2654216 | tf_op jit(solution)/shard_map/ppermute | solution.py:461

commit v5 on v4

--- a/solution.py
+++ b/solution.py
@@ -12,8 +12,8 @@
 LOG2E = 1.4426950408889634
 EXP_SCALE = 192.0 ** (-0.5) * LOG2E
 HOLDER = ("y", "xh", "xl")
-PLANE = ("xl", "xh", "y")
-SPREAD = ("xl", "xh", "zp")
+PLANE = ("xh", "xl", "y")
+SPREAD = ("zp", "xl", "xh")
 CAP = 9
 PIECE = 16
 LANES = 128
@@ -103,21 +103,20 @@
     ]
     for c in out_copies:
         c.start()
-    flipped = (0, 2, 1, 3)
     for c in pool_copies:
         c.wait()
     blocks = [slots[r] for r in range(CAP)]
     for r in range(CAP):
-        for i, x in enumerate(flipped):
-            cached_part[i, r * PIECE : (r + 1) * PIECE, :] = lat[blocks[r], x * PIECE : (x + 1) * PIECE, :]
+        for x in range(4):
+            cached_part[x, r * PIECE : (r + 1) * PIECE, :] = lat[blocks[r], x * PIECE : (x + 1) * PIECE, :]
     for m in range((CAP + 3) // 4):
         quarter = []
         for r in range(4 * m, 4 * m + 4):
             whole = rope[blocks[min(r, CAP - 1)]]
             quarter.append(jnp.where(core == 0, whole[:, 0:32], whole[:, 32:64]))
         both = jnp.concatenate(quarter, axis=1)
-        for i, x in enumerate(flipped):
-            cached_part[i, LAT_ROWS + m * PIECE : LAT_ROWS + (m + 1) * PIECE, :] = both[
+        for x in range(4):
+            cached_part[x, LAT_ROWS + m * PIECE : LAT_ROWS + (m + 1) * PIECE, :] = both[
                 x * PIECE : (x + 1) * PIECE, :
             ]
     for s in range(SEQS):
@@ -128,32 +127,31 @@
         c.wait()
 
 
-def plan_kernel(owner, plan):
-    low, high = jnp.int32(0), jnp.int32(0)
-    for s in range(SEQS):
-        for j in range(BLOCKS):
-            h = owner[s, j]
-            shift = (h & 7) * 4
-            first = h < 8
-            rank = (jnp.where(first, low, high) >> shift) & 15
-            one = jnp.int32(1) << shift
-            low = low + jnp.where(first, one, 0)
-            high = high + jnp.where(first, 0, one)
-            source = ((h & 1) * 2 + ((h >> 1) & 1)) * 4 + (h >> 2)
-            plan[s, j] = source * 16 + jnp.minimum(rank, CAP - 1)
-
-
-def select_kernel(plan, recv, out, new_out, cached, picked, packed, sems, out_sems):
+def select_kernel(owner, recv, out, new_out, counts, cached, picked, packed, sems, out_sems):
     zp, seq = coords("zp", "y")
     arrive = pltpu.make_async_copy(recv.at[:, pl.ds(0, NEW_AT), :], cached, sems.at[0])
     arrive.start()
-    entries = [plan[seq, j] for j in range(BLOCKS)]
-    ranks = [e & 15 for e in entries]
-    sources = [e >> 4 for e in entries]
     new_copy = pltpu.make_async_copy(
         recv.at[:, pl.ds(NEW_AT, NEW_ROWS), :], new_out, sems.at[1]
     )
     new_copy.start()
+    for h in range(16):
+        counts[h] = 0
+
+    def scan(s, carry):
+        for j in range(BLOCKS):
+            h = owner[s, j]
+            counts[h] = counts[h] + 1
+        return carry
+
+    lax.fori_loop(0, seq, scan, jnp.int32(0))
+    ranks, sources = [], []
+    for j in range(BLOCKS):
+        h = owner[seq, j]
+        rank = counts[h]
+        counts[h] = rank + 1
+        ranks.append(jnp.minimum(rank, CAP - 1))
+        sources.append((h & 3) * 4 + (h >> 2))
     arrive.wait()
     for j in range(BLOCKS):
         rows = pl.ds(pl.multiple_of(ranks[j] * PIECE, PIECE), PIECE)
@@ -239,8 +237,8 @@
                     for tile in range(2):
                         at = tile * 64 + half * 32
                         col = (2 * i + tile) * LANES
-                        keys[y, half, part, :, col : col + LANES] = ref[part % 2, part // 2, y, at : at + 32, :]
-                    keys[y, half, part, rope_rows, 512:640] = ref[part % 2, part // 2, y, 128:144, :]
+                        keys[y, half, part, :, col : col + LANES] = ref[part // 2, part % 2, y, at : at + 32, :]
+                    keys[y, half, part, rope_rows, 512:640] = ref[part // 2, part % 2, y, 128:144, :]
     for c in query_copies:
         c.wait()
     for chunk in range(4):
@@ -299,10 +297,10 @@
                 for e in range(4):
                     start = (e * 4 + x) * span
                     keys[start : start + span, (2 * i + zp) * LANES : (2 * i + zp + 1) * LANES] = ref[
-                        x % 2, x // 2, zp, e * span : (e + 1) * span, :
+                        zp, x % 2, x // 2, e * span : (e + 1) * span, :
                     ]
         packed = [
-            jnp.concatenate([ref[x % 2, x // 2, zp, PICK_LAT:PICK_ROWS, :] for zp in range(2)], axis=0)
+            jnp.concatenate([ref[zp, x % 2, x // 2, PICK_LAT:PICK_ROWS, :] for zp in range(2)], axis=0)
             for ref in (own, other)
         ]
         for e in range(4):
@@ -396,23 +394,12 @@
         compiler_params=params(63),
         name="pack",
     )(block_owner, block_slot, cache_latent, cache_rope, new_latent, jnp.swapaxes(new_rope, 1, 2))
-    send, query_nope, query_rope, owner = lax.optimization_barrier(
-        (send, query_nope, query_rope, block_owner)
-    )
-    plan = pl.pallas_call(
-        plan_kernel,
-        out_shape=shape((SEQS, BLOCKS), jnp.int32),
-        in_specs=[smem()],
-        out_specs=smem(),
-        name="plan",
-    )(owner)
+    send, query_nope, query_rope = lax.optimization_barrier((send, query_nope, query_rope))
     recv = lax.all_to_all(send.reshape(16, MSG_ROWS, LANES), PLANE, 0, 0)
     query = jnp.concatenate([query_nope, query_rope], -1)
     queries = []
     for k in range(4):
         part = lax.dynamic_index_in_dim(query, lax.rem(y + k, 4), 0, keepdims=False)
-        if k == 3:
-            part, plan = lax.optimization_barrier((part, plan))
         if k:
             part = lax.ppermute(part, "y", [(i, (i + k) % 4) for i in range(4)])
         queries.append(part)
@@ -422,6 +409,7 @@
         in_specs=[smem(), anywhere()],
         out_specs=(anywhere(), anywhere()),
         scratch_shapes=[
+            pltpu.SMEM((16,), jnp.int32),
             pltpu.VMEM((16, NEW_AT, LANES), bf16),
             pltpu.VMEM((PICK_ROWS, LANES), bf16),
             pltpu.VMEM((BLOCKS // 4 * PIECE, LANES), bf16),
@@ -430,7 +418,7 @@
         ],
         compiler_params=params(16),
         name="select",
-    )(plan, recv)
+    )(block_owner, recv)
     picked, new_own, *queries = lax.optimization_barrier((picked, new_own, *queries))
     swap = [(0, 1), (1, 0)]
     new_own = new_own.reshape(2, 2, 4, NEW_ROWS, LANES)

time: 74.3 us -> 73.4 us (0.988)
  Pallas kernels: 19.1 us -> 17.2 us
  starting transfers between devices: 29.6 us -> 31.4 us
  waiting for transfers between devices: 15.3 us -> 14 us
    all_to_all x1, waiting for transfers between devices: 3.58 us -> 6.37 us  [on_device(): recv = lax.all_to_all(send.reshape(16, MSG_ROWS, LANES), PLANE, 0, 0)]
    ppermute x3, waiting for transfers between devices: 5.67 us -> 3.2 us  [on_device(): part = lax.ppermute(part, 'y', [(i, (i + k) % 4) for i in range(4)])]
    pallas_call x1 -> x0, Pallas kernels: 1.95 us -> none  [on_device(): pl.pallas_call(plan_kernel, out_shape=shape((SEQS, BLOCKS), jnp.int32), i...]
    all_to_all x1, waiting for transfers between devices: 3.68 us -> 1.94 us  [on_device(): lax.all_to_all(picked, SPREAD, 0, 0).reshape(2, 2, 2, PICK_ROWS, LANES)]
    all_to_all x1, starting transfers between devices: 4.75 us -> 5.54 us  [on_device(): lax.all_to_all(picked, SPREAD, 0, 0).reshape(2, 2, 2, PICK_ROWS, LANES)]
  transfers between devices with their start and end apart: 7 -> 7, of which waited for: 7 -> 5; matrix products, arithmetic and copies ran while one was open for 0% -> 0% of each run, Pallas kernels for 14% -> 11%
where the time goes in v5:
time: 73.4 us; the launch traced here: 72.6 us
  starting transfers between devices  31.4 us (43%)
  Pallas kernels  17.2 us (23%)
  waiting for transfers between devices  14 us (19%)
  blocking collectives  8.89 us (12%)
  local copies, waits for them, and re-layouts  0.85 us (1%)
    ppermute x3, starting transfers between devices, on_device(): part = lax.ppermute(part, 'y', [(i, (i + k) % 4) for i in range(4)])  10.8 us
    all_to_all x1, blocking collectives, on_device(): return lax.all_to_all(mixed, 'y', 0, 0)  8.89 us
    all_to_all x1, starting transfers between devices, on_device(): recv = lax.all_to_all(send.reshape(16, MSG_ROWS, LANES), PLANE, 0, 0)  7.73 us
    pallas_call x1, Pallas kernels, on_device(): pl.pallas_call(cached_kernel, out_shape=shape((4, TOK, 256)), in_specs=[s...  6.46 us
    all_to_all x1, waiting for transfers between devices, on_device(): recv = lax.all_to_all(send.reshape(16, MSG_ROWS, LANES), PLANE, 0, 0)  6.37 us
    all_to_all x1, starting transfers between devices, on_device(): lax.all_to_all(picked, SPREAD, 0, 0).reshape(2, 2, 2, PICK_ROWS, LANES)  5.54 us
    pallas_call x1, Pallas kernels, on_device(): pl.pallas_call(new_kernel, out_shape=(shape((8, rows), f32), shape((4, TO...  4.97 us
    ppermute x1, starting transfers between devices, on_device(): cache_other = lax.ppermute(cache_own, 'core', swap)  4.39 us
  transfers between devices with their start and end apart: 7, of which 5 were waited for; matrix products, arithmetic and copies ran while one was open for 0% of the time, Pallas kernels for 11%

profile of v5, /device:TPU:1, one launch (start us, length us, event | category | flops | bytes accessed | tf_op | source)
XLA Modules:
  0.0 72.6 jit_solution(14727116525269365648)
XLA Ops:
  0.0 2.6 %pack.1 = bf16[4,4,336,128]{3,2,1,0:T(8,128)(2,1)} custom-call(s32[4,24]{1,0:T(4,128)} %owner.3, s32[4,24]{1,0:T(4,128)} %slot.1, bf16[32,64,512]{2,1,0:T(8,128)(2,1)} %cache_latent.1, bf16[32,64,64]{2,1,0:T(8,128)(2,1)} %cache_rope.1, bf16[4,128,512]{2,1,0:T(8,128)(2,1)} %new_latent.1, bf16[4,64,128]{2,1,0:T(8,128)(2,1)} %bitcast.17), custom_call_target="tpu_custom_call" | custom-call | tf_op jit(solution)/shard_map/pack/pallas_call | solution.py:375
  2.6 0.0 copy-start.4
  2.6 0.0 copy-start.5
  2.6 7.7 %all-to-all-start = ((bf16[16,336,128]{2,1,0:T(8,128)(2,1)}), bf16[16,336,128]{2,1,0:T(8,128)(2,1)S(1)}, u32[]{:S(2)}, u32[]{:S(2)}) async-start(bf16[16,336,128]{2,1,0:T(8,128)(2,1)} %bitcast.16), calls=%async_computation | async-start | bytes 2752512 | tf_op jit(solution)/shard_map/all_to_all | solution.py:398
  10.3 0.0 copy-start.1
  10.5 0.1 dynamic-slice_bitcast_fusion
  10.5 3.3 %collective-permute-start = (bf16[128,384]{1,0:T(8,128)(2,1)S(1)}, bf16[128,384]{1,0:T(8,128)(2,1)S(1)}, u32[]{:S(2)}, u32[]{:S(2)}) collective-permute-start(bf16[128,384]{1,0:T(8,128)(2,1)S(1)} %get-tuple-element.47), channel_id=1, source_target_pairs={{0,128},{128,256},{256,384},{384,0},{1,129},{129,257},{257,385},{3... | collective-permute-start | bytes 294920 | tf_op jit(solution)/shard_map/ppermute | solution.py:404
  13.8 4.3 %collective-permute-start.1 = (bf16[128,384]{1,0:T(8,128)(2,1)S(1)}, bf16[128,384]{1,0:T(8,128)(2,1)S(1)}, u32[]{:S(2)}, u32[]{:S(2)}) collective-permute-start(bf16[128,384]{1,0:T(8,128)(2,1)S(1)} %get-tuple-element.46), channel_id=1, source_target_pairs={{0,256},{128,384},{256,0},{384,128},{1,257},{129,385},{257,1},{385... | collective-permute-start | bytes 294920 | tf_op jit(solution)/shard_map/ppermute | solution.py:404
  18.1 3.2 %collective-permute-start.2 = (bf16[128,384]{1,0:T(8,128)(2,1)S(1)}, bf16[128,384]{1,0:T(8,128)(2,1)S(1)}, u32[]{:S(2)}, u32[]{:S(2)}) collective-permute-start(bf16[128,384]{1,0:T(8,128)(2,1)S(1)} %get-tuple-element.45), channel_id=1, source_target_pairs={{0,384},{128,0},{256,128},{384,256},{1,385},{129,1},{257,129},{385... | collective-permute-start | bytes 294920 | tf_op jit(solution)/shard_map/ppermute | solution.py:404
  21.4 6.4 %all-to-all-done.recv = bf16[16,336,128]{2,1,0:T(8,128)(2,1)S(1)} async-done(((bf16[16,336,128]{2,1,0:T(8,128)(2,1)}), bf16[16,336,128]{2,1,0:T(8,128)(2,1)S(1)}, u32[]{:S(2)}, u32[]{:S(2)}) %all-to-all-start) | async-done | bytes 1376288 | tf_op jit(solution)/shard_map/all_to_all | solution.py:398
  27.7 2.1 %select.9 = (bf16[8,432,128]{2,1,0:T(8,128)(2,1)}, bf16[16,144,128]{2,1,0:T(8,128)(2,1)S(1)}) custom-call(s32[4,24]{1,0:T(4,128)S(1)} %copy-done.1, bf16[16,336,128]{2,1,0:T(8,128)(2,1)S(1)} %all-to-all-done.recv), custom_call_target="tpu_custom_call" | custom-call | tf_op jit(solution)/shard_map/select/pallas_call | solution.py:406
  29.9 3.2 %collective-permute-done.1.q2 = bf16[128,384]{1,0:T(8,128)(2,1)S(1)} collective-permute-done((bf16[128,384]{1,0:T(8,128)(2,1)S(1)}, bf16[128,384]{1,0:T(8,128)(2,1)S(1)}, u32[]{:S(2)}, u32[]{:S(2)}) %collective-permute-start.1) | collective-permute-done | bytes 98336 | tf_op jit(solution)/shard_map/ppermute | solution.py:404
  33.1 5.5 %all-to-all-start.1 = ((bf16[8,432,128]{2,1,0:T(8,128)(2,1)}), bf16[8,432,128]{2,1,0:T(8,128)(2,1)S(1)}, u32[]{:S(2)}, u32[]{:S(2)}) async-start(bf16[8,432,128]{2,1,0:T(8,128)(2,1)} %get-tuple-element.30), calls=%async_computation.1 | async-start | bytes 1769472 | tf_op jit(solution)/shard_map/all_to_all | solution.py:426
  38.6 3.0 %collective-permute-start.3 = (bf16[2,2,4,144,128]{4,3,2,1,0:T(8,128)(2,1)S(1)}, bf16[2,2,4,144,128]{4,3,2,1,0:T(8,128)(2,1)S(1)}, u32[]{:S(2)}, u32[]{:S(2)}) collective-permute-start(bf16[2,2,4,144,128]{4,3,2,1,0:T(8,128)(2,1)S(1)} %bitcast.14), channel_id=1, source_target_pairs={{0,2},{2,0},{1,3},{3,1},{4,6},{6,4},{5,7},{7,5},{8,10},{10,8},{9,1... | collective-permute-start | bytes 1769480 | tf_op jit(solution)/shard_map/ppermute | solution.py:425
  41.6 1.6 %collective-permute-done.3.other = bf16[2,2,4,144,128]{4,3,2,1,0:T(8,128)(2,1)S(1)} collective-permute-done((bf16[2,2,4,144,128]{4,3,2,1,0:T(8,128)(2,1)S(1)}, bf16[2,2,4,144,128]{4,3,2,1,0:T(8,128)(2,1)S(1)}, u32[]{:S(2)}, u32[]{:S(2)}) %collective-permute-start.3) | collective-permute-done | bytes 589856 | tf_op jit(solution)/shard_map/ppermute | solution.py:425
  43.2 5.0 %attend_new.1 = (f32[8,1024]{1,0:T(8,128)S(1)}, f32[4,128,256]{2,1,0:T(8,128)S(1)}, f32[8,128]{1,0:T(8,128)S(1)}) custom-call(bf16[128,384]{1,0:T(8,128)(2,1)S(1)} %get-tuple-element.37.q0, bf16[128,384]{1,0:T(8,128)(2,1)S(1)} %collective-permute-done.q1, bf16[128,384]{1,0:T(8,128)(2,1)S(1)} %collective-permute-done.1.q2, ...), custom_call_target="tpu_custom_call" | custom-call | flops 3000000000 | bytes 5000000 | tf_op jit(solution)/shard_map/attend_new/pallas_call | solution.py:429
  48.2 0.0 copy-start.3
  48.2 1.9 %all-to-all-done.1 = bf16[8,432,128]{2,1,0:T(8,128)(2,1)S(1)} async-done(((bf16[8,432,128]{2,1,0:T(8,128)(2,1)}), bf16[8,432,128]{2,1,0:T(8,128)(2,1)S(1)}, u32[]{:S(2)}, u32[]{:S(2)}) %all-to-all-start.1) | async-done | bytes 884768 | tf_op jit(solution)/shard_map/all_to_all | solution.py:426
  50.1 4.4 %collective-permute-start.4 = (bf16[2,2,2,432,128]{4,3,2,1,0:T(8,128)(2,1)S(1)}, bf16[2,2,2,432,128]{4,3,2,1,0:T(8,128)(2,1)S(1)}, u32[]{:S(2)}, u32[]{:S(2)}) collective-permute-start(bf16[2,2,2,432,128]{4,3,2,1,0:T(8,128)(2,1)S(1)} %bitcast.12), channel_id=1, source_target_pairs={{0,2},{2,0},{1,3},{3,1},{4,6},{6,4},{5,7},{7,5},{8,10},{10,8},{9,1... | collective-permute-start | bytes 2654216 | tf_op jit(solution)/shard_map/ppermute | solution.py:449
  54.5 1.1 %prepare.1.joint = bf16[1024,640]{1,0:T(8,128)(2,1)S(1)} custom-call(bf16[128,384]{1,0:T(8,128)(2,1)S(1)} %get-tuple-element.37.q0, bf16[128,384]{1,0:T(8,128)(2,1)S(1)} %collective-permute-done.q1, bf16[128,384]{1,0:T(8,128)(2,1)S(1)} %collective-permute-done.1.q2, bf16[128,384]{1,0:T(8,128)(2,1)S(1)} %collective-permute-done.2.q3, ...), custom_call_target="tpu_custom_call" | custom-call | flops 200000000 | bytes 2000000 | tf_op jit(solution)/shard_map/prepare/pallas_call | solution.py:450
  55.6 0.9 %collective-permute-done.4.other = bf16[2,2,2,432,128]{4,3,2,1,0:T(8,128)(2,1)S(1)} collective-permute-done((bf16[2,2,2,432,128]{4,3,2,1,0:T(8,128)(2,1)S(1)}, bf16[2,2,2,432,128]{4,3,2,1,0:T(8,128)(2,1)S(1)}, u32[]{:S(2)}, u32[]{:S(2)}) %collective-permute-start.4) | collective-permute-done | bytes 884768 | tf_op jit(solution)/shard_map/ppermute | solution.py:449
  56.5 6.5 %attend_cached.1 = bf16[4,128,256]{2,1,0:T(8,128)(2,1)S(1)} custom-call(s32[4]{0:T(128)S(1)} %copy-done.3, bf16[1024,640]{1,0:T(8,128)(2,1)S(1)} %prepare.1.joint, bf16[2,512,128]{2,1,0:T(8,128)(2,1)S(1)} %copy-done.2, bf16[2,2,2,432,128]{4,3,2,1,0:T(8,128)(2,1)S(1)} %bitcast.13, bf16[2,2,2,432,128]{4,3,2,1,0:T(8,128)(2,1)S(1)} %collective-permute-done.4.other, ...), custom_call_target="tpu_custom_call" | custom-call | flops 4000000000 | bytes 5000000 | tf_op jit(solution)/shard_map/attend_cached/pallas_call | solution.py:460
  63.0 8.9 %all_to_all.15 = bf16[4,128,256]{2,1,0:T(8,128)(2,1)S(1)} all-to-all(bf16[4,128,256]{2,1,0:T(8,128)(2,1)S(1)} %attend_cached.1), channel_id=1, replica_groups=mesh['y'=4,'xh'=2,'zh'=8,'zp'=2,'core'=2,'xl'=2] {'y'}, dimensions={0} | all-to-all | bytes 524288 | tf_op jit(solution)/shard_map/all_to_all | solution.py:472
  71.9 0.7 copy.14
  (12 shorter events, 0.1 us)
Async XLA Ops:
  2.6 7.8 %copy-start.4 = (bf16[4,128,256]{2,1,0:T(8,128)(2,1)S(1)}, bf16[4,128,256]{2,1,0:T(8,128)(2,1)}, u32[]{:S(2)}) copy-start(bf16[4,128,256]{2,1,0:T(8,128)(2,1)} %param.11) | copy-start | bytes 786436
  2.6 7.8 %copy-start.5 = (bf16[4,128,128]{2,1,0:T(8,128)(2,1)S(1)}, bf16[4,128,128]{2,1,0:T(8,128)(2,1)}, u32[]{:S(2)}) copy-start(bf16[4,128,128]{2,1,0:T(8,128)(2,1)} %param.12) | copy-start | bytes 393220
  2.6 25.1 %all-to-all-start = ((bf16[16,336,128]{2,1,0:T(8,128)(2,1)}), bf16[16,336,128]{2,1,0:T(8,128)(2,1)S(1)}, u32[]{:S(2)}, u32[]{:S(2)}) async-start(bf16[16,336,128]{2,1,0:T(8,128)(2,1)} %bitcast.16), calls=%async_computation | async-start | bytes 2752512 | tf_op jit(solution)/shard_map/all_to_all | solution.py:398
  10.3 17.4 %copy-start.1 = (s32[4,24]{1,0:T(4,128)S(1)}, s32[4,24]{1,0:T(4,128)}, u32[]{:S(2)}) copy-start(s32[4,24]{1,0:T(4,128)} %owner.3) | copy-start | bytes 1156
  10.5 19.3 %collective-permute-start = (bf16[128,384]{1,0:T(8,128)(2,1)S(1)}, bf16[128,384]{1,0:T(8,128)(2,1)S(1)}, u32[]{:S(2)}, u32[]{:S(2)}) collective-permute-start(bf16[128,384]{1,0:T(8,128)(2,1)S(1)} %get-tuple-element.47), channel_id=1, source_target_pairs={{0,128},{128,256},{256,384},{384,0},{1,129},{129,257},{257,385},{3... | collective-permute-start | bytes 294920 | tf_op jit(solution)/shard_map/ppermute | solution.py:404
  13.8 19.2 %collective-permute-start.1 = (bf16[128,384]{1,0:T(8,128)(2,1)S(1)}, bf16[128,384]{1,0:T(8,128)(2,1)S(1)}, u32[]{:S(2)}, u32[]{:S(2)}) collective-permute-start(bf16[128,384]{1,0:T(8,128)(2,1)S(1)} %get-tuple-element.46), channel_id=1, source_target_pairs={{0,256},{128,384},{256,0},{384,128},{1,257},{129,385},{257,1},{385... | collective-permute-start | bytes 294920 | tf_op jit(solution)/shard_map/ppermute | solution.py:404
  18.1 25.1 %copy-start = (bf16[2,128,512]{2,1,0:T(8,128)(2,1)S(1)}, bf16[2,128,512]{2,1,0:T(8,128)(2,1)}, u32[]{:S(2)}) copy-start(bf16[2,128,512]{2,1,0:T(8,128)(2,1)} %key_up.3) | copy-start | bytes 786436
  18.1 25.0 %copy-start.2 = (bf16[2,512,128]{2,1,0:T(8,128)(2,1)S(1)}, bf16[2,512,128]{2,1,0:T(8,128)(2,1)}, u32[]{:S(2)}) copy-start(bf16[2,512,128]{2,1,0:T(8,128)(2,1)} %value_up.3) | copy-start | bytes 786436
  18.1 14.9 %collective-permute-start.2 = (bf16[128,384]{1,0:T(8,128)(2,1)S(1)}, bf16[128,384]{1,0:T(8,128)(2,1)S(1)}, u32[]{:S(2)}, u32[]{:S(2)}) collective-permute-start(bf16[128,384]{1,0:T(8,128)(2,1)S(1)} %get-tuple-element.45), channel_id=1, source_target_pairs={{0,384},{128,0},{256,128},{384,256},{1,385},{129,1},{257,129},{385... | collective-permute-start | bytes 294920 | tf_op jit(solution)/shard_map/ppermute | solution.py:404
  33.1 17.0 %all-to-all-start.1 = ((bf16[8,432,128]{2,1,0:T(8,128)(2,1)}), bf16[8,432,128]{2,1,0:T(8,128)(2,1)S(1)}, u32[]{:S(2)}, u32[]{:S(2)}) async-start(bf16[8,432,128]{2,1,0:T(8,128)(2,1)} %get-tuple-element.30), calls=%async_computation.1 | async-start | bytes 1769472 | tf_op jit(solution)/shard_map/all_to_all | solution.py:426
  38.6 4.6 %collective-permute-start.3 = (bf16[2,2,4,144,128]{4,3,2,1,0:T(8,128)(2,1)S(1)}, bf16[2,2,4,144,128]{4,3,2,1,0:T(8,128)(2,1)S(1)}, u32[]{:S(2)}, u32[]{:S(2)}) collective-permute-start(bf16[2,2,4,144,128]{4,3,2,1,0:T(8,128)(2,1)S(1)} %bitcast.14), channel_id=1, source_target_pairs={{0,2},{2,0},{1,3},{3,1},{4,6},{6,4},{5,7},{7,5},{8,10},{10,8},{9,1... | collective-permute-start | bytes 1769480 | tf_op jit(solution)/shard_map/ppermute | solution.py:425
  48.2 8.4 %copy-start.3 = (s32[4]{0:T(128)S(1)}, s32[4]{0:T(128)}, u32[]{:S(2)}) copy-start(s32[4]{0:T(128)} %cached_len.1) | copy-start | bytes 52
  50.1 6.4 %collective-permute-start.4 = (bf16[2,2,2,432,128]{4,3,2,1,0:T(8,128)(2,1)S(1)}, bf16[2,2,2,432,128]{4,3,2,1,0:T(8,128)(2,1)S(1)}, u32[]{:S(2)}, u32[]{:S(2)}) collective-permute-start(bf16[2,2,2,432,128]{4,3,2,1,0:T(8,128)(2,1)S(1)} %bitcast.12), channel_id=1, source_target_pairs={{0,2},{2,0},{1,3},{3,1},{4,6},{6,4},{5,7},{7,5},{8,10},{10,8},{9,1... | collective-permute-start | bytes 2654216 | tf_op jit(solution)/shard_map/ppermute | solution.py:449

commit v6 on v5

--- a/solution.py
+++ b/solution.py
@@ -291,44 +291,53 @@
     core, seq = coords("core", "y")
     span = PICK_LAT // 4
     pad = jnp.zeros((span, 64), bf16)
-    for x in range(4):
-        for i, ref in enumerate((own, other)):
-            for zp in range(2):
-                for e in range(4):
-                    start = (e * 4 + x) * span
-                    keys[start : start + span, (2 * i + zp) * LANES : (2 * i + zp + 1) * LANES] = ref[
-                        zp, x % 2, x // 2, e * span : (e + 1) * span, :
-                    ]
-        packed = [
+    packed = [
+        [
             jnp.concatenate([ref[zp, x % 2, x // 2, PICK_LAT:PICK_ROWS, :] for zp in range(2)], axis=0)
             for ref in (own, other)
         ]
-        for e in range(4):
-            start = (e * 4 + x) * span
-            lanes = slice(32 * e, 32 * e + 32)
-            keys[start : start + span, 512:640] = jnp.concatenate(
-                [packed[0][:, lanes], packed[1][:, lanes], pad], axis=1
-            )
-    count = 16 * span
-    index = lax.broadcasted_iota(jnp.int32, (1, count), 1)
+        for x in range(4)
+    ]
+    rows, count = 4 * TOK, 8 * span
+
+    def assemble(half):
+        for e in (2 * half, 2 * half + 1):
+            for x in range(4):
+                start = (e * 4 + x) * span
+                for i, ref in enumerate((own, other)):
+                    for zp in range(2):
+                        keys[start : start + span, (2 * i + zp) * LANES : (2 * i + zp + 1) * LANES] = ref[
+                            zp, x % 2, x // 2, e * span : (e + 1) * span, :
+                        ]
+                lanes = slice(32 * e, 32 * e + 32)
+                keys[start : start + span, 512:640] = jnp.concatenate(
+                    [packed[x][0][:, lanes], packed[x][1][:, lanes], pad], axis=1
+                )
+
+    length = cached_len[seq]
+    index = lax.broadcasted_iota(jnp.int32, (1, 2 * count), 1)
     rest = index % span
     position = (index // (4 * span) * (BLOCKS // 4) + rest // PIECE) * 64
     position = position + index // span % 4 * PIECE + rest % PIECE
-    length = cached_len[seq]
     bias = jnp.where(position < length, 0.0, NEG).astype(f32)
-    rows = 4 * TOK
-    for group in range(2):
-        at = slice(group * rows, (group + 1) * rows)
-        scores = dot_t(joint[at, :], keys[...]) + bias
-        state = jnp.concatenate([stats[:, at]] * 16, axis=0).T
+
+    def score(group, half):
+        q = joint[group * rows : (group + 1) * rows, :]
+        at = slice(half * count, (half + 1) * count)
+        return dot_t(q, keys[at, :]) + bias[:, at]
+
+    def soften(group, scores):
+        state = jnp.concatenate([stats[:, group * rows : (group + 1) * rows]] * 16, axis=0).T
         before, denom_before = state[:, 0:1], state[:, 1:2]
-        top = jnp.maximum(before, jnp.max(scores, -1, keepdims=True))
+        top = functools.reduce(jnp.maximum, [before] + [jnp.max(s, -1, keepdims=True) for s in scores])
         factor = jnp.exp2((before - top) * EXP_SCALE) * denom_before
-        expo = jnp.exp2((scores - top) * EXP_SCALE)
-        denom = factor + jnp.sum(expo, -1, keepdims=True)
-        total = dot(expo.astype(bf16), keys[:, 0:512])
-        share = factor / denom
-        mixed = (total / denom).astype(bf16)
+        expo = [jnp.exp2((s - top) * EXP_SCALE) for s in scores]
+        denom = functools.reduce(jnp.add, [factor] + [jnp.sum(e, -1, keepdims=True) for e in expo])
+        weights = jnp.concatenate([e.astype(bf16) for e in expo], axis=1)
+        return weights, denom, factor / denom
+
+    def finish(group, weights, denom, share):
+        mixed = (dot(weights, keys[:, 0:512]) / denom).astype(bf16)
         for c in range(2):
             chunk = group * 2 + c
             for h in range(2):
@@ -336,6 +345,16 @@
                 cols = slice(h * 128, (h + 1) * 128)
                 fresh = project(mixed[tok], value_up, core, h)
                 out[chunk, :, cols] = (fresh + new_part[chunk, :, cols] * share[tok]).astype(bf16)
+
+    assemble(0)
+    first = [score(0, 0)]
+    assemble(1)
+    first.append(score(0, 1))
+    second = [score(1, 0), score(1, 1)]
+    first = soften(0, first)
+    second = soften(1, second)
+    finish(0, *first)
+    finish(1, *second)
 
 
 def smem():

time: 73.4 us -> 72.5 us (0.988)
  Pallas kernels: 17.2 us -> 16.4 us
    pallas_call x1, Pallas kernels: 6.46 us -> 5.6 us  [on_device(): pl.pallas_call(cached_kernel, out_shape=shape((4, TOK, 256)), in_specs=[s...]
where the time goes in v6:
time: 72.5 us; the launch traced here: 71.8 us
  starting transfers between devices  31.4 us (43%)
  Pallas kernels  16.4 us (23%)
  waiting for transfers between devices  14 us (19%)
  blocking collectives  8.91 us (12%)
  local copies, waits for them, and re-layouts  0.85 us (1%)
    ppermute x3, starting transfers between devices, on_device(): part = lax.ppermute(part, 'y', [(i, (i + k) % 4) for i in range(4)])  10.8 us
    all_to_all x1, blocking collectives, on_device(): return lax.all_to_all(mixed, 'y', 0, 0)  8.91 us
    all_to_all x1, starting transfers between devices, on_device(): recv = lax.all_to_all(send.reshape(16, MSG_ROWS, LANES), PLANE, 0, 0)  7.73 us
    all_to_all x1, waiting for transfers between devices, on_device(): recv = lax.all_to_all(send.reshape(16, MSG_ROWS, LANES), PLANE, 0, 0)  6.37 us
    pallas_call x1, Pallas kernels, on_device(): pl.pallas_call(cached_kernel, out_shape=shape((4, TOK, 256)), in_specs=[s...  5.6 us
    all_to_all x1, starting transfers between devices, on_device(): lax.all_to_all(picked, SPREAD, 0, 0).reshape(2, 2, 2, PICK_ROWS, LANES)  5.54 us
    pallas_call x1, Pallas kernels, on_device(): pl.pallas_call(new_kernel, out_shape=(shape((8, rows), f32), shape((4, TO...  4.97 us
    ppermute x1, starting transfers between devices, on_device(): cache_other = lax.ppermute(cache_own, 'core', swap)  4.39 us
  transfers between devices with their start and end apart: 7, of which 5 were waited for; matrix products, arithmetic and copies ran while one was open for 0% of the time, Pallas kernels for 11%

profile of v6, /device:TPU:1, one launch (start us, length us, event | category | flops | bytes accessed | tf_op | source)
XLA Modules:
  0.0 71.8 jit_solution(10029424673403371493)
XLA Ops:
  0.0 2.6 %pack.1 = bf16[4,4,336,128]{3,2,1,0:T(8,128)(2,1)} custom-call(s32[4,24]{1,0:T(4,128)} %owner.3, s32[4,24]{1,0:T(4,128)} %slot.1, bf16[32,64,512]{2,1,0:T(8,128)(2,1)} %cache_latent.1, bf16[32,64,64]{2,1,0:T(8,128)(2,1)} %cache_rope.1, bf16[4,128,512]{2,1,0:T(8,128)(2,1)} %new_latent.1, bf16[4,64,128]{2,1,0:T(8,128)(2,1)} %bitcast.17), custom_call_target="tpu_custom_call" | custom-call | tf_op jit(solution)/shard_map/pack/pallas_call | solution.py:394
  2.6 0.0 copy-start.4
  2.6 0.0 copy-start.5
  2.6 7.7 %all-to-all-start = ((bf16[16,336,128]{2,1,0:T(8,128)(2,1)}), bf16[16,336,128]{2,1,0:T(8,128)(2,1)S(1)}, u32[]{:S(2)}, u32[]{:S(2)}) async-start(bf16[16,336,128]{2,1,0:T(8,128)(2,1)} %bitcast.16), calls=%async_computation | async-start | bytes 2752512 | tf_op jit(solution)/shard_map/all_to_all | solution.py:417
  10.3 0.0 copy-start.1
  10.5 0.1 dynamic-slice_bitcast_fusion
  10.5 3.3 %collective-permute-start = (bf16[128,384]{1,0:T(8,128)(2,1)S(1)}, bf16[128,384]{1,0:T(8,128)(2,1)S(1)}, u32[]{:S(2)}, u32[]{:S(2)}) collective-permute-start(bf16[128,384]{1,0:T(8,128)(2,1)S(1)} %get-tuple-element.47), channel_id=1, source_target_pairs={{0,128},{128,256},{256,384},{384,0},{1,129},{129,257},{257,385},{3... | collective-permute-start | bytes 294920 | tf_op jit(solution)/shard_map/ppermute | solution.py:423
  13.8 4.3 %collective-permute-start.1 = (bf16[128,384]{1,0:T(8,128)(2,1)S(1)}, bf16[128,384]{1,0:T(8,128)(2,1)S(1)}, u32[]{:S(2)}, u32[]{:S(2)}) collective-permute-start(bf16[128,384]{1,0:T(8,128)(2,1)S(1)} %get-tuple-element.46), channel_id=1, source_target_pairs={{0,256},{128,384},{256,0},{384,128},{1,257},{129,385},{257,1},{385... | collective-permute-start | bytes 294920 | tf_op jit(solution)/shard_map/ppermute | solution.py:423
  18.1 3.2 %collective-permute-start.2 = (bf16[128,384]{1,0:T(8,128)(2,1)S(1)}, bf16[128,384]{1,0:T(8,128)(2,1)S(1)}, u32[]{:S(2)}, u32[]{:S(2)}) collective-permute-start(bf16[128,384]{1,0:T(8,128)(2,1)S(1)} %get-tuple-element.45), channel_id=1, source_target_pairs={{0,384},{128,0},{256,128},{384,256},{1,385},{129,1},{257,129},{385... | collective-permute-start | bytes 294920 | tf_op jit(solution)/shard_map/ppermute | solution.py:423
  21.4 6.4 %all-to-all-done.recv = bf16[16,336,128]{2,1,0:T(8,128)(2,1)S(1)} async-done(((bf16[16,336,128]{2,1,0:T(8,128)(2,1)}), bf16[16,336,128]{2,1,0:T(8,128)(2,1)S(1)}, u32[]{:S(2)}, u32[]{:S(2)}) %all-to-all-start) | async-done | bytes 1376288 | tf_op jit(solution)/shard_map/all_to_all | solution.py:417
  27.7 2.1 %select.9 = (bf16[8,432,128]{2,1,0:T(8,128)(2,1)}, bf16[16,144,128]{2,1,0:T(8,128)(2,1)S(1)}) custom-call(s32[4,24]{1,0:T(4,128)S(1)} %copy-done.1, bf16[16,336,128]{2,1,0:T(8,128)(2,1)S(1)} %all-to-all-done.recv), custom_call_target="tpu_custom_call" | custom-call | tf_op jit(solution)/shard_map/select/pallas_call | solution.py:425
  29.9 3.2 %collective-permute-done.1.q2 = bf16[128,384]{1,0:T(8,128)(2,1)S(1)} collective-permute-done((bf16[128,384]{1,0:T(8,128)(2,1)S(1)}, bf16[128,384]{1,0:T(8,128)(2,1)S(1)}, u32[]{:S(2)}, u32[]{:S(2)}) %collective-permute-start.1) | collective-permute-done | bytes 98336 | tf_op jit(solution)/shard_map/ppermute | solution.py:423
  33.1 5.5 %all-to-all-start.1 = ((bf16[8,432,128]{2,1,0:T(8,128)(2,1)}), bf16[8,432,128]{2,1,0:T(8,128)(2,1)S(1)}, u32[]{:S(2)}, u32[]{:S(2)}) async-start(bf16[8,432,128]{2,1,0:T(8,128)(2,1)} %get-tuple-element.30), calls=%async_computation.1 | async-start | bytes 1769472 | tf_op jit(solution)/shard_map/all_to_all | solution.py:445
  38.6 3.0 %collective-permute-start.3 = (bf16[2,2,4,144,128]{4,3,2,1,0:T(8,128)(2,1)S(1)}, bf16[2,2,4,144,128]{4,3,2,1,0:T(8,128)(2,1)S(1)}, u32[]{:S(2)}, u32[]{:S(2)}) collective-permute-start(bf16[2,2,4,144,128]{4,3,2,1,0:T(8,128)(2,1)S(1)} %bitcast.14), channel_id=1, source_target_pairs={{0,2},{2,0},{1,3},{3,1},{4,6},{6,4},{5,7},{7,5},{8,10},{10,8},{9,1... | collective-permute-start | bytes 1769480 | tf_op jit(solution)/shard_map/ppermute | solution.py:444
  41.6 1.6 %collective-permute-done.3.other = bf16[2,2,4,144,128]{4,3,2,1,0:T(8,128)(2,1)S(1)} collective-permute-done((bf16[2,2,4,144,128]{4,3,2,1,0:T(8,128)(2,1)S(1)}, bf16[2,2,4,144,128]{4,3,2,1,0:T(8,128)(2,1)S(1)}, u32[]{:S(2)}, u32[]{:S(2)}) %collective-permute-start.3) | collective-permute-done | bytes 589856 | tf_op jit(solution)/shard_map/ppermute | solution.py:444
  43.2 5.0 %attend_new.1 = (f32[8,1024]{1,0:T(8,128)S(1)}, f32[4,128,256]{2,1,0:T(8,128)S(1)}, f32[8,128]{1,0:T(8,128)S(1)}) custom-call(bf16[128,384]{1,0:T(8,128)(2,1)S(1)} %get-tuple-element.37.q0, bf16[128,384]{1,0:T(8,128)(2,1)S(1)} %collective-permute-done.q1, bf16[128,384]{1,0:T(8,128)(2,1)S(1)} %collective-permute-done.1.q2, ...), custom_call_target="tpu_custom_call" | custom-call | flops 3000000000 | bytes 5000000 | tf_op jit(solution)/shard_map/attend_new/pallas_call | solution.py:448
  48.2 0.0 copy-start.3
  48.2 1.9 %all-to-all-done.1 = bf16[8,432,128]{2,1,0:T(8,128)(2,1)S(1)} async-done(((bf16[8,432,128]{2,1,0:T(8,128)(2,1)}), bf16[8,432,128]{2,1,0:T(8,128)(2,1)S(1)}, u32[]{:S(2)}, u32[]{:S(2)}) %all-to-all-start.1) | async-done | bytes 884768 | tf_op jit(solution)/shard_map/all_to_all | solution.py:445
  50.1 4.4 %collective-permute-start.4 = (bf16[2,2,2,432,128]{4,3,2,1,0:T(8,128)(2,1)S(1)}, bf16[2,2,2,432,128]{4,3,2,1,0:T(8,128)(2,1)S(1)}, u32[]{:S(2)}, u32[]{:S(2)}) collective-permute-start(bf16[2,2,2,432,128]{4,3,2,1,0:T(8,128)(2,1)S(1)} %bitcast.12), channel_id=1, source_target_pairs={{0,2},{2,0},{1,3},{3,1},{4,6},{6,4},{5,7},{7,5},{8,10},{10,8},{9,1... | collective-permute-start | bytes 2654216 | tf_op jit(solution)/shard_map/ppermute | solution.py:468
  54.5 1.1 %prepare.1.joint = bf16[1024,640]{1,0:T(8,128)(2,1)S(1)} custom-call(bf16[128,384]{1,0:T(8,128)(2,1)S(1)} %get-tuple-element.37.q0, bf16[128,384]{1,0:T(8,128)(2,1)S(1)} %collective-permute-done.q1, bf16[128,384]{1,0:T(8,128)(2,1)S(1)} %collective-permute-done.1.q2, bf16[128,384]{1,0:T(8,128)(2,1)S(1)} %collective-permute-done.2.q3, ...), custom_call_target="tpu_custom_call" | custom-call | flops 200000000 | bytes 2000000 | tf_op jit(solution)/shard_map/prepare/pallas_call | solution.py:469
  55.6 0.9 %collective-permute-done.4.other = bf16[2,2,2,432,128]{4,3,2,1,0:T(8,128)(2,1)S(1)} collective-permute-done((bf16[2,2,2,432,128]{4,3,2,1,0:T(8,128)(2,1)S(1)}, bf16[2,2,2,432,128]{4,3,2,1,0:T(8,128)(2,1)S(1)}, u32[]{:S(2)}, u32[]{:S(2)}) %collective-permute-start.4) | collective-permute-done | bytes 884768 | tf_op jit(solution)/shard_map/ppermute | solution.py:468
  56.5 5.6 %attend_cached.1 = bf16[4,128,256]{2,1,0:T(8,128)(2,1)S(1)} custom-call(s32[4]{0:T(128)S(1)} %copy-done.3, bf16[1024,640]{1,0:T(8,128)(2,1)S(1)} %prepare.1.joint, bf16[2,512,128]{2,1,0:T(8,128)(2,1)S(1)} %copy-done.2, bf16[2,2,2,432,128]{4,3,2,1,0:T(8,128)(2,1)S(1)} %bitcast.13, bf16[2,2,2,432,128]{4,3,2,1,0:T(8,128)(2,1)S(1)} %collective-permute-done.4.other, ...), custom_call_target="tpu_custom_call" | custom-call | flops 4000000000 | bytes 5000000 | tf_op jit(solution)/shard_map/attend_cached/pallas_call | solution.py:479
  62.1 8.9 %all_to_all.15 = bf16[4,128,256]{2,1,0:T(8,128)(2,1)S(1)} all-to-all(bf16[4,128,256]{2,1,0:T(8,128)(2,1)S(1)} %attend_cached.1), channel_id=1, replica_groups=mesh['y'=4,'xh'=2,'zh'=8,'zp'=2,'core'=2,'xl'=2] {'y'}, dimensions={0} | all-to-all | bytes 524288 | tf_op jit(solution)/shard_map/all_to_all | solution.py:491
  71.1 0.7 copy.14
  (12 shorter events, 0.1 us)
Async XLA Ops:
  2.6 7.8 %copy-start.4 = (bf16[4,128,256]{2,1,0:T(8,128)(2,1)S(1)}, bf16[4,128,256]{2,1,0:T(8,128)(2,1)}, u32[]{:S(2)}) copy-start(bf16[4,128,256]{2,1,0:T(8,128)(2,1)} %param.11) | copy-start | bytes 786436
  2.6 7.8 %copy-start.5 = (bf16[4,128,128]{2,1,0:T(8,128)(2,1)S(1)}, bf16[4,128,128]{2,1,0:T(8,128)(2,1)}, u32[]{:S(2)}) copy-start(bf16[4,128,128]{2,1,0:T(8,128)(2,1)} %param.12) | copy-start | bytes 393220
  2.6 25.1 %all-to-all-start = ((bf16[16,336,128]{2,1,0:T(8,128)(2,1)}), bf16[16,336,128]{2,1,0:T(8,128)(2,1)S(1)}, u32[]{:S(2)}, u32[]{:S(2)}) async-start(bf16[16,336,128]{2,1,0:T(8,128)(2,1)} %bitcast.16), calls=%async_computation | async-start | bytes 2752512 | tf_op jit(solution)/shard_map/all_to_all | solution.py:417
  10.3 17.4 %copy-start.1 = (s32[4,24]{1,0:T(4,128)S(1)}, s32[4,24]{1,0:T(4,128)}, u32[]{:S(2)}) copy-start(s32[4,24]{1,0:T(4,128)} %owner.3) | copy-start | bytes 1156
  10.5 19.3 %collective-permute-start = (bf16[128,384]{1,0:T(8,128)(2,1)S(1)}, bf16[128,384]{1,0:T(8,128)(2,1)S(1)}, u32[]{:S(2)}, u32[]{:S(2)}) collective-permute-start(bf16[128,384]{1,0:T(8,128)(2,1)S(1)} %get-tuple-element.47), channel_id=1, source_target_pairs={{0,128},{128,256},{256,384},{384,0},{1,129},{129,257},{257,385},{3... | collective-permute-start | bytes 294920 | tf_op jit(solution)/shard_map/ppermute | solution.py:423
  13.8 19.2 %collective-permute-start.1 = (bf16[128,384]{1,0:T(8,128)(2,1)S(1)}, bf16[128,384]{1,0:T(8,128)(2,1)S(1)}, u32[]{:S(2)}, u32[]{:S(2)}) collective-permute-start(bf16[128,384]{1,0:T(8,128)(2,1)S(1)} %get-tuple-element.46), channel_id=1, source_target_pairs={{0,256},{128,384},{256,0},{384,128},{1,257},{129,385},{257,1},{385... | collective-permute-start | bytes 294920 | tf_op jit(solution)/shard_map/ppermute | solution.py:423
  18.1 25.1 %copy-start = (bf16[2,128,512]{2,1,0:T(8,128)(2,1)S(1)}, bf16[2,128,512]{2,1,0:T(8,128)(2,1)}, u32[]{:S(2)}) copy-start(bf16[2,128,512]{2,1,0:T(8,128)(2,1)} %key_up.3) | copy-start | bytes 786436
  18.1 25.0 %copy-start.2 = (bf16[2,512,128]{2,1,0:T(8,128)(2,1)S(1)}, bf16[2,512,128]{2,1,0:T(8,128)(2,1)}, u32[]{:S(2)}) copy-start(bf16[2,512,128]{2,1,0:T(8,128)(2,1)} %value_up.3) | copy-start | bytes 786436
  18.1 14.9 %collective-permute-start.2 = (bf16[128,384]{1,0:T(8,128)(2,1)S(1)}, bf16[128,384]{1,0:T(8,128)(2,1)S(1)}, u32[]{:S(2)}, u32[]{:S(2)}) collective-permute-start(bf16[128,384]{1,0:T(8,128)(2,1)S(1)} %get-tuple-element.45), channel_id=1, source_target_pairs={{0,384},{128,0},{256,128},{384,256},{1,385},{129,1},{257,129},{385... | collective-permute-start | bytes 294920 | tf_op jit(solution)/shard_map/ppermute | solution.py:423
  33.1 17.0 %all-to-all-start.1 = ((bf16[8,432,128]{2,1,0:T(8,128)(2,1)}), bf16[8,432,128]{2,1,0:T(8,128)(2,1)S(1)}, u32[]{:S(2)}, u32[]{:S(2)}) async-start(bf16[8,432,128]{2,1,0:T(8,128)(2,1)} %get-tuple-element.30), calls=%async_computation.1 | async-start | bytes 1769472 | tf_op jit(solution)/shard_map/all_to_all | solution.py:445
  38.6 4.6 %collective-permute-start.3 = (bf16[2,2,4,144,128]{4,3,2,1,0:T(8,128)(2,1)S(1)}, bf16[2,2,4,144,128]{4,3,2,1,0:T(8,128)(2,1)S(1)}, u32[]{:S(2)}, u32[]{:S(2)}) collective-permute-start(bf16[2,2,4,144,128]{4,3,2,1,0:T(8,128)(2,1)S(1)} %bitcast.14), channel_id=1, source_target_pairs={{0,2},{2,0},{1,3},{3,1},{4,6},{6,4},{5,7},{7,5},{8,10},{10,8},{9,1... | collective-permute-start | bytes 1769480 | tf_op jit(solution)/shard_map/ppermute | solution.py:444
  48.2 8.4 %copy-start.3 = (s32[4]{0:T(128)S(1)}, s32[4]{0:T(128)}, u32[]{:S(2)}) copy-start(s32[4]{0:T(128)} %cached_len.1) | copy-start | bytes 52
  50.1 6.4 %collective-permute-start.4 = (bf16[2,2,2,432,128]{4,3,2,1,0:T(8,128)(2,1)S(1)}, bf16[2,2,2,432,128]{4,3,2,1,0:T(8,128)(2,1)S(1)}, u32[]{:S(2)}, u32[]{:S(2)}) collective-permute-start(bf16[2,2,2,432,128]{4,3,2,1,0:T(8,128)(2,1)S(1)} %bitcast.12), channel_id=1, source_target_pairs={{0,2},{2,0},{1,3},{3,1},{4,6},{6,4},{5,7},{7,5},{8,10},{10,8},{9,1... | collective-permute-start | bytes 2654216 | tf_op jit(solution)/shard_map/ppermute | solution.py:468

commit v7 on v6

--- a/solution.py
+++ b/solution.py
@@ -109,6 +109,12 @@
     for r in range(CAP):
         for x in range(4):
             cached_part[x, r * PIECE : (r + 1) * PIECE, :] = lat[blocks[r], x * PIECE : (x + 1) * PIECE, :]
+    for s in range(SEQS):
+        c = pltpu.make_async_copy(
+            cached_part.at[:, pl.ds(0, LAT_ROWS), :], out.at[:, s, pl.ds(0, LAT_ROWS), :], out_sems.at[4 + s]
+        )
+        c.start()
+        out_copies.append(c)
     for m in range((CAP + 3) // 4):
         quarter = []
         for r in range(4 * m, 4 * m + 4):
@@ -120,7 +126,11 @@
                 x * PIECE : (x + 1) * PIECE, :
             ]
     for s in range(SEQS):
-        c = pltpu.make_async_copy(cached_part, out.at[:, s, pl.ds(0, NEW_AT), :], out_sems.at[4 + s])
+        c = pltpu.make_async_copy(
+            cached_part.at[:, pl.ds(LAT_ROWS, ROPE_ROWS), :],
+            out.at[:, s, pl.ds(LAT_ROWS, ROPE_ROWS), :],
+            out_sems.at[8 + s],
+        )
         c.start()
         out_copies.append(c)
     for c in out_copies:
@@ -249,26 +259,35 @@
     col_tok = col // 32 * 64 + col % 32
     lane = lax.broadcasted_iota(jnp.int32, (rows, LANES), 1)
     causal = [jnp.where(col_tok + 32 * half <= row_tok, 0.0, NEG).astype(f32) for half in range(2)]
-    for chunk in range(4):
+    def score(chunk):
         q = load_query(joint, chunk * rows, rows)
         scores = []
         for part in range(chunk + 1):
             for half in range(2):
                 s = dot_t(q[half], keys[part, half].reshape(TOK, 640))
-                if part == chunk:
-                    s = s + causal[half]
-                scores.append(s)
+                scores.append(s + causal[half] if part == chunk else s)
+        return scores
+
+    def soften(chunk, scores):
         top = functools.reduce(jnp.maximum, [jnp.max(s, -1, keepdims=True) for s in scores])
         expo = [jnp.exp2((s - top) * EXP_SCALE) for s in scores]
         denom = functools.reduce(jnp.add, [jnp.sum(e, -1, keepdims=True) for e in expo])
-        weights = jnp.concatenate([e.astype(bf16) for e in expo], axis=1)
+        stats_out[:, chunk * rows : (chunk + 1) * rows] = jnp.where(lane == 0, top, denom).T[0:8]
+        return jnp.concatenate([e.astype(bf16) for e in expo], axis=1), denom
+
+    def finish(chunk, weights, denom):
         total = dot(weights, keys[0 : chunk + 1, :, :, :, 0:512].reshape((chunk + 1) * rows, 512))
-        stats_out[:, chunk * rows : (chunk + 1) * rows] = jnp.where(lane == 0, top, denom).T[0:8]
         mixed = (total / denom).astype(bf16)
         for h in range(2):
             part_out[chunk, :, h * 128 : (h + 1) * 128] = project(
                 mixed[h * TOK : (h + 1) * TOK], value_up, core, h
             )
+
+    order = (3, 2, 1, 0)
+    scores = {chunk: score(chunk) for chunk in order}
+    softened = {chunk: soften(chunk, scores[chunk]) for chunk in order}
+    for chunk in order:
+        finish(chunk, *softened[chunk])
 
 
 def prepare_kernel(q0, q1, q2, q3, key_up, joint, query, sems):
@@ -408,7 +427,7 @@
             pltpu.VMEM((4, NEW_AT, LANES), bf16),
             pltpu.VMEM((SEQS, NEW_ROWS, LANES), bf16),
             pltpu.SemaphoreType.DMA((6,)),
-            pltpu.SemaphoreType.DMA((8,)),
+            pltpu.SemaphoreType.DMA((12,)),
         ],
         compiler_params=params(63),
         name="pack",

time: 72.5 us -> 72.4 us (level)
  Pallas kernels: 16.4 us -> 15.5 us
  waiting for transfers between devices: 14 us -> 14.8 us
    all_to_all x1, waiting for transfers between devices: 1.94 us -> 2.7 us  [on_device(): lax.all_to_all(picked, SPREAD, 0, 0).reshape(2, 2, 2, PICK_ROWS, LANES)]
    pallas_call x1, Pallas kernels: 4.97 us -> 4.21 us  [on_device(): pl.pallas_call(new_kernel, out_shape=(shape((8, rows), f32), shape((4, TO...]
  transfers between devices with their start and end apart: 7 -> 7, of which waited for: 5 -> 5; matrix products, arithmetic and copies ran while one was open for 0% -> 0% of each run, Pallas kernels for 11% -> 10%
where the time goes in v7:
time: 72.4 us; the launch traced here: 71.6 us
  starting transfers between devices  31.4 us (43%)
  Pallas kernels  15.5 us (21%)
  waiting for transfers between devices  14.8 us (20%)
  blocking collectives  8.9 us (12%)
  local copies, waits for them, and re-layouts  0.85 us (1%)
    ppermute x3, starting transfers between devices, on_device(): part = lax.ppermute(part, 'y', [(i, (i + k) % 4) for i in range(4)])  10.8 us
    all_to_all x1, blocking collectives, on_device(): return lax.all_to_all(mixed, 'y', 0, 0)  8.9 us
    all_to_all x1, starting transfers between devices, on_device(): recv = lax.all_to_all(send.reshape(16, MSG_ROWS, LANES), PLANE, 0, 0)  7.73 us
    all_to_all x1, waiting for transfers between devices, on_device(): recv = lax.all_to_all(send.reshape(16, MSG_ROWS, LANES), PLANE, 0, 0)  6.37 us
    pallas_call x1, Pallas kernels, on_device(): pl.pallas_call(cached_kernel, out_shape=shape((4, TOK, 256)), in_specs=[s...  5.6 us
    all_to_all x1, starting transfers between devices, on_device(): lax.all_to_all(picked, SPREAD, 0, 0).reshape(2, 2, 2, PICK_ROWS, LANES)  5.54 us
    ppermute x1, starting transfers between devices, on_device(): cache_other = lax.ppermute(cache_own, 'core', swap)  4.39 us
    pallas_call x1, Pallas kernels, on_device(): pl.pallas_call(new_kernel, out_shape=(shape((8, rows), f32), shape((4, TO...  4.21 us
  transfers between devices with their start and end apart: 7, of which 5 were waited for; matrix products, arithmetic and copies ran while one was open for 0% of the time, Pallas kernels for 10%

profile of v7, /device:TPU:1, one launch (start us, length us, event | category | flops | bytes accessed | tf_op | source)
XLA Modules:
  0.0 71.6 jit_solution(1406596723227325071)
XLA Ops:
  0.0 2.5 %pack.1 = bf16[4,4,336,128]{3,2,1,0:T(8,128)(2,1)} custom-call(s32[4,24]{1,0:T(4,128)} %owner.3, s32[4,24]{1,0:T(4,128)} %slot.1, bf16[32,64,512]{2,1,0:T(8,128)(2,1)} %cache_latent.1, bf16[32,64,64]{2,1,0:T(8,128)(2,1)} %cache_rope.1, bf16[4,128,512]{2,1,0:T(8,128)(2,1)} %new_latent.1, bf16[4,64,128]{2,1,0:T(8,128)(2,1)} %bitcast.17), custom_call_target="tpu_custom_call" | custom-call | tf_op jit(solution)/shard_map/pack/pallas_call | solution.py:413
  2.5 0.0 copy-start.4
  2.5 7.7 %all-to-all-start = ((bf16[16,336,128]{2,1,0:T(8,128)(2,1)}), bf16[16,336,128]{2,1,0:T(8,128)(2,1)S(1)}, u32[]{:S(2)}, u32[]{:S(2)}) async-start(bf16[16,336,128]{2,1,0:T(8,128)(2,1)} %bitcast.16), calls=%async_computation | async-start | bytes 2752512 | tf_op jit(solution)/shard_map/all_to_all | solution.py:436
  10.2 0.0 copy-start.1
  10.4 0.1 dynamic-slice_bitcast_fusion
  10.4 3.3 %collective-permute-start = (bf16[128,384]{1,0:T(8,128)(2,1)S(1)}, bf16[128,384]{1,0:T(8,128)(2,1)S(1)}, u32[]{:S(2)}, u32[]{:S(2)}) collective-permute-start(bf16[128,384]{1,0:T(8,128)(2,1)S(1)} %get-tuple-element.47), channel_id=1, source_target_pairs={{0,128},{128,256},{256,384},{384,0},{1,129},{129,257},{257,385},{3... | collective-permute-start | bytes 294920 | tf_op jit(solution)/shard_map/ppermute | solution.py:442
  13.7 4.3 %collective-permute-start.1 = (bf16[128,384]{1,0:T(8,128)(2,1)S(1)}, bf16[128,384]{1,0:T(8,128)(2,1)S(1)}, u32[]{:S(2)}, u32[]{:S(2)}) collective-permute-start(bf16[128,384]{1,0:T(8,128)(2,1)S(1)} %get-tuple-element.46), channel_id=1, source_target_pairs={{0,256},{128,384},{256,0},{384,128},{1,257},{129,385},{257,1},{385... | collective-permute-start | bytes 294920 | tf_op jit(solution)/shard_map/ppermute | solution.py:442
  18.0 0.0 copy-start
  18.0 3.2 %collective-permute-start.2 = (bf16[128,384]{1,0:T(8,128)(2,1)S(1)}, bf16[128,384]{1,0:T(8,128)(2,1)S(1)}, u32[]{:S(2)}, u32[]{:S(2)}) collective-permute-start(bf16[128,384]{1,0:T(8,128)(2,1)S(1)} %get-tuple-element.45), channel_id=1, source_target_pairs={{0,384},{128,0},{256,128},{384,256},{1,385},{129,1},{257,129},{385... | collective-permute-start | bytes 294920 | tf_op jit(solution)/shard_map/ppermute | solution.py:442
  21.3 6.4 %all-to-all-done.recv = bf16[16,336,128]{2,1,0:T(8,128)(2,1)S(1)} async-done(((bf16[16,336,128]{2,1,0:T(8,128)(2,1)}), bf16[16,336,128]{2,1,0:T(8,128)(2,1)S(1)}, u32[]{:S(2)}, u32[]{:S(2)}) %all-to-all-start) | async-done | bytes 1376288 | tf_op jit(solution)/shard_map/all_to_all | solution.py:436
  27.6 2.1 %select.9 = (bf16[8,432,128]{2,1,0:T(8,128)(2,1)}, bf16[16,144,128]{2,1,0:T(8,128)(2,1)S(1)}) custom-call(s32[4,24]{1,0:T(4,128)S(1)} %copy-done.1, bf16[16,336,128]{2,1,0:T(8,128)(2,1)S(1)} %all-to-all-done.recv), custom_call_target="tpu_custom_call" | custom-call | tf_op jit(solution)/shard_map/select/pallas_call | solution.py:444
  29.7 3.2 %collective-permute-done.1.q2 = bf16[128,384]{1,0:T(8,128)(2,1)S(1)} collective-permute-done((bf16[128,384]{1,0:T(8,128)(2,1)S(1)}, bf16[128,384]{1,0:T(8,128)(2,1)S(1)}, u32[]{:S(2)}, u32[]{:S(2)}) %collective-permute-start.1) | collective-permute-done | bytes 98336 | tf_op jit(solution)/shard_map/ppermute | solution.py:442
  32.9 5.5 %all-to-all-start.1 = ((bf16[8,432,128]{2,1,0:T(8,128)(2,1)}), bf16[8,432,128]{2,1,0:T(8,128)(2,1)S(1)}, u32[]{:S(2)}, u32[]{:S(2)}) async-start(bf16[8,432,128]{2,1,0:T(8,128)(2,1)} %get-tuple-element.30), calls=%async_computation.1 | async-start | bytes 1769472 | tf_op jit(solution)/shard_map/all_to_all | solution.py:464
  38.5 3.0 %collective-permute-start.3 = (bf16[2,2,4,144,128]{4,3,2,1,0:T(8,128)(2,1)S(1)}, bf16[2,2,4,144,128]{4,3,2,1,0:T(8,128)(2,1)S(1)}, u32[]{:S(2)}, u32[]{:S(2)}) collective-permute-start(bf16[2,2,4,144,128]{4,3,2,1,0:T(8,128)(2,1)S(1)} %bitcast.14), channel_id=1, source_target_pairs={{0,2},{2,0},{1,3},{3,1},{4,6},{6,4},{5,7},{7,5},{8,10},{10,8},{9,1... | collective-permute-start | bytes 1769480 | tf_op jit(solution)/shard_map/ppermute | solution.py:463
  41.4 1.6 %collective-permute-done.3.other = bf16[2,2,4,144,128]{4,3,2,1,0:T(8,128)(2,1)S(1)} collective-permute-done((bf16[2,2,4,144,128]{4,3,2,1,0:T(8,128)(2,1)S(1)}, bf16[2,2,4,144,128]{4,3,2,1,0:T(8,128)(2,1)S(1)}, u32[]{:S(2)}, u32[]{:S(2)}) %collective-permute-start.3) | collective-permute-done | bytes 589856 | tf_op jit(solution)/shard_map/ppermute | solution.py:463
  43.1 4.2 %attend_new.1 = (f32[8,1024]{1,0:T(8,128)S(1)}, f32[4,128,256]{2,1,0:T(8,128)S(1)}, f32[8,128]{1,0:T(8,128)S(1)}) custom-call(bf16[128,384]{1,0:T(8,128)(2,1)S(1)} %get-tuple-element.37.q0, bf16[128,384]{1,0:T(8,128)(2,1)S(1)} %collective-permute-done.q1, bf16[128,384]{1,0:T(8,128)(2,1)S(1)} %collective-permute-done.1.q2, ...), custom_call_target="tpu_custom_call" | custom-call | flops 3000000000 | bytes 5000000 | tf_op jit(solution)/shard_map/attend_new/pallas_call | solution.py:467
  47.3 0.0 copy-start.3
  47.3 2.7 %all-to-all-done.1 = bf16[8,432,128]{2,1,0:T(8,128)(2,1)S(1)} async-done(((bf16[8,432,128]{2,1,0:T(8,128)(2,1)}), bf16[8,432,128]{2,1,0:T(8,128)(2,1)S(1)}, u32[]{:S(2)}, u32[]{:S(2)}) %all-to-all-start.1) | async-done | bytes 884768 | tf_op jit(solution)/shard_map/all_to_all | solution.py:464
  50.0 4.4 %collective-permute-start.4 = (bf16[2,2,2,432,128]{4,3,2,1,0:T(8,128)(2,1)S(1)}, bf16[2,2,2,432,128]{4,3,2,1,0:T(8,128)(2,1)S(1)}, u32[]{:S(2)}, u32[]{:S(2)}) collective-permute-start(bf16[2,2,2,432,128]{4,3,2,1,0:T(8,128)(2,1)S(1)} %bitcast.12), channel_id=1, source_target_pairs={{0,2},{2,0},{1,3},{3,1},{4,6},{6,4},{5,7},{7,5},{8,10},{10,8},{9,1... | collective-permute-start | bytes 2654216 | tf_op jit(solution)/shard_map/ppermute | solution.py:487
  54.4 1.1 %prepare.1.joint = bf16[1024,640]{1,0:T(8,128)(2,1)S(1)} custom-call(bf16[128,384]{1,0:T(8,128)(2,1)S(1)} %get-tuple-element.37.q0, bf16[128,384]{1,0:T(8,128)(2,1)S(1)} %collective-permute-done.q1, bf16[128,384]{1,0:T(8,128)(2,1)S(1)} %collective-permute-done.1.q2, bf16[128,384]{1,0:T(8,128)(2,1)S(1)} %collective-permute-done.2.q3, ...), custom_call_target="tpu_custom_call" | custom-call | flops 200000000 | bytes 2000000 | tf_op jit(solution)/shard_map/prepare/pallas_call | solution.py:488
  55.5 0.9 %collective-permute-done.4.other = bf16[2,2,2,432,128]{4,3,2,1,0:T(8,128)(2,1)S(1)} collective-permute-done((bf16[2,2,2,432,128]{4,3,2,1,0:T(8,128)(2,1)S(1)}, bf16[2,2,2,432,128]{4,3,2,1,0:T(8,128)(2,1)S(1)}, u32[]{:S(2)}, u32[]{:S(2)}) %collective-permute-start.4) | collective-permute-done | bytes 884768 | tf_op jit(solution)/shard_map/ppermute | solution.py:487
  56.4 5.6 %attend_cached.1 = bf16[4,128,256]{2,1,0:T(8,128)(2,1)S(1)} custom-call(s32[4]{0:T(128)S(1)} %copy-done.3, bf16[1024,640]{1,0:T(8,128)(2,1)S(1)} %prepare.1.joint, bf16[2,512,128]{2,1,0:T(8,128)(2,1)S(1)} %copy-done.2, bf16[2,2,2,432,128]{4,3,2,1,0:T(8,128)(2,1)S(1)} %bitcast.13, bf16[2,2,2,432,128]{4,3,2,1,0:T(8,128)(2,1)S(1)} %collective-permute-done.4.other, ...), custom_call_target="tpu_custom_call" | custom-call | flops 4000000000 | bytes 5000000 | tf_op jit(solution)/shard_map/attend_cached/pallas_call | solution.py:498
  62.0 8.9 %all_to_all.15 = bf16[4,128,256]{2,1,0:T(8,128)(2,1)S(1)} all-to-all(bf16[4,128,256]{2,1,0:T(8,128)(2,1)S(1)} %attend_cached.1), channel_id=1, replica_groups=mesh['y'=4,'xh'=2,'zh'=8,'zp'=2,'core'=2,'xl'=2] {'y'}, dimensions={0} | all-to-all | bytes 524288 | tf_op jit(solution)/shard_map/all_to_all | solution.py:510
  70.9 0.7 copy.14
  (12 shorter events, 0.1 us)
Async XLA Ops:
  2.5 7.8 %copy-start.4 = (bf16[4,128,256]{2,1,0:T(8,128)(2,1)S(1)}, bf16[4,128,256]{2,1,0:T(8,128)(2,1)}, u32[]{:S(2)}) copy-start(bf16[4,128,256]{2,1,0:T(8,128)(2,1)} %param.11) | copy-start | bytes 786436
  2.5 7.8 %copy-start.5 = (bf16[4,128,128]{2,1,0:T(8,128)(2,1)S(1)}, bf16[4,128,128]{2,1,0:T(8,128)(2,1)}, u32[]{:S(2)}) copy-start(bf16[4,128,128]{2,1,0:T(8,128)(2,1)} %param.12) | copy-start | bytes 393220
  2.5 25.1 %all-to-all-start = ((bf16[16,336,128]{2,1,0:T(8,128)(2,1)}), bf16[16,336,128]{2,1,0:T(8,128)(2,1)S(1)}, u32[]{:S(2)}, u32[]{:S(2)}) async-start(bf16[16,336,128]{2,1,0:T(8,128)(2,1)} %bitcast.16), calls=%async_computation | async-start | bytes 2752512 | tf_op jit(solution)/shard_map/all_to_all | solution.py:436
  10.2 17.4 %copy-start.1 = (s32[4,24]{1,0:T(4,128)S(1)}, s32[4,24]{1,0:T(4,128)}, u32[]{:S(2)}) copy-start(s32[4,24]{1,0:T(4,128)} %owner.3) | copy-start | bytes 1156
  10.4 19.3 %collective-permute-start = (bf16[128,384]{1,0:T(8,128)(2,1)S(1)}, bf16[128,384]{1,0:T(8,128)(2,1)S(1)}, u32[]{:S(2)}, u32[]{:S(2)}) collective-permute-start(bf16[128,384]{1,0:T(8,128)(2,1)S(1)} %get-tuple-element.47), channel_id=1, source_target_pairs={{0,128},{128,256},{256,384},{384,0},{1,129},{129,257},{257,385},{3... | collective-permute-start | bytes 294920 | tf_op jit(solution)/shard_map/ppermute | solution.py:442
  13.7 19.2 %collective-permute-start.1 = (bf16[128,384]{1,0:T(8,128)(2,1)S(1)}, bf16[128,384]{1,0:T(8,128)(2,1)S(1)}, u32[]{:S(2)}, u32[]{:S(2)}) collective-permute-start(bf16[128,384]{1,0:T(8,128)(2,1)S(1)} %get-tuple-element.46), channel_id=1, source_target_pairs={{0,256},{128,384},{256,0},{384,128},{1,257},{129,385},{257,1},{385... | collective-permute-start | bytes 294920 | tf_op jit(solution)/shard_map/ppermute | solution.py:442
  18.0 25.1 %copy-start = (bf16[2,128,512]{2,1,0:T(8,128)(2,1)S(1)}, bf16[2,128,512]{2,1,0:T(8,128)(2,1)}, u32[]{:S(2)}) copy-start(bf16[2,128,512]{2,1,0:T(8,128)(2,1)} %key_up.3) | copy-start | bytes 786436
  18.0 25.0 %copy-start.2 = (bf16[2,512,128]{2,1,0:T(8,128)(2,1)S(1)}, bf16[2,512,128]{2,1,0:T(8,128)(2,1)}, u32[]{:S(2)}) copy-start(bf16[2,512,128]{2,1,0:T(8,128)(2,1)} %value_up.3) | copy-start | bytes 786436
  18.0 14.9 %collective-permute-start.2 = (bf16[128,384]{1,0:T(8,128)(2,1)S(1)}, bf16[128,384]{1,0:T(8,128)(2,1)S(1)}, u32[]{:S(2)}, u32[]{:S(2)}) collective-permute-start(bf16[128,384]{1,0:T(8,128)(2,1)S(1)} %get-tuple-element.45), channel_id=1, source_target_pairs={{0,384},{128,0},{256,128},{384,256},{1,385},{129,1},{257,129},{385... | collective-permute-start | bytes 294920 | tf_op jit(solution)/shard_map/ppermute | solution.py:442
  32.9 17.0 %all-to-all-start.1 = ((bf16[8,432,128]{2,1,0:T(8,128)(2,1)}), bf16[8,432,128]{2,1,0:T(8,128)(2,1)S(1)}, u32[]{:S(2)}, u32[]{:S(2)}) async-start(bf16[8,432,128]{2,1,0:T(8,128)(2,1)} %get-tuple-element.30), calls=%async_computation.1 | async-start | bytes 1769472 | tf_op jit(solution)/shard_map/all_to_all | solution.py:464
  38.5 4.6 %collective-permute-start.3 = (bf16[2,2,4,144,128]{4,3,2,1,0:T(8,128)(2,1)S(1)}, bf16[2,2,4,144,128]{4,3,2,1,0:T(8,128)(2,1)S(1)}, u32[]{:S(2)}, u32[]{:S(2)}) collective-permute-start(bf16[2,2,4,144,128]{4,3,2,1,0:T(8,128)(2,1)S(1)} %bitcast.14), channel_id=1, source_target_pairs={{0,2},{2,0},{1,3},{3,1},{4,6},{6,4},{5,7},{7,5},{8,10},{10,8},{9,1... | collective-permute-start | bytes 1769480 | tf_op jit(solution)/shard_map/ppermute | solution.py:463
  47.3 9.1 %copy-start.3 = (s32[4]{0:T(128)S(1)}, s32[4]{0:T(128)}, u32[]{:S(2)}) copy-start(s32[4]{0:T(128)} %cached_len.1) | copy-start | bytes 52
  50.0 6.4 %collective-permute-start.4 = (bf16[2,2,2,432,128]{4,3,2,1,0:T(8,128)(2,1)S(1)}, bf16[2,2,2,432,128]{4,3,2,1,0:T(8,128)(2,1)S(1)}, u32[]{:S(2)}, u32[]{:S(2)}) collective-permute-start(bf16[2,2,2,432,128]{4,3,2,1,0:T(8,128)(2,1)S(1)} %bitcast.12), channel_id=1, source_target_pairs={{0,2},{2,0},{1,3},{3,1},{4,6},{6,4},{5,7},{7,5},{8,10},{10,8},{9,1... | collective-permute-start | bytes 2654216 | tf_op jit(solution)/shard_map/ppermute | solution.py:487

commit v8 on v7

--- a/solution.py
+++ b/solution.py
@@ -12,7 +12,7 @@
 LOG2E = 1.4426950408889634
 EXP_SCALE = 192.0 ** (-0.5) * LOG2E
 HOLDER = ("y", "xh", "xl")
-PLANE = ("xh", "xl", "y")
+PLANE = ("y", "xl", "xh")
 SPREAD = ("zp", "xl", "xh")
 CAP = 9
 PIECE = 16
@@ -98,7 +98,7 @@
         new_part[s, 64:128, :] = nlat[s, :, LANES : 2 * LANES]
         new_part[s, 128:144, :] = jnp.concatenate([nrope[s, low, :], nrope[s, high, :]], axis=1)
     out_copies = [
-        pltpu.make_async_copy(new_part, out.at[x, :, pl.ds(NEW_AT, NEW_ROWS), :], out_sems.at[x])
+        pltpu.make_async_copy(new_part, out.at[:, x, pl.ds(NEW_AT, NEW_ROWS), :], out_sems.at[x])
         for x in range(4)
     ]
     for c in out_copies:
@@ -106,12 +106,13 @@
     for c in pool_copies:
         c.wait()
     blocks = [slots[r] for r in range(CAP)]
+    flipped = (0, 2, 1, 3)
     for r in range(CAP):
         for x in range(4):
-            cached_part[x, r * PIECE : (r + 1) * PIECE, :] = lat[blocks[r], x * PIECE : (x + 1) * PIECE, :]
+            cached_part[flipped[x], r * PIECE : (r + 1) * PIECE, :] = lat[blocks[r], x * PIECE : (x + 1) * PIECE, :]
     for s in range(SEQS):
         c = pltpu.make_async_copy(
-            cached_part.at[:, pl.ds(0, LAT_ROWS), :], out.at[:, s, pl.ds(0, LAT_ROWS), :], out_sems.at[4 + s]
+            cached_part.at[:, pl.ds(0, LAT_ROWS), :], out.at[s, :, pl.ds(0, LAT_ROWS), :], out_sems.at[4 + s]
         )
         c.start()
         out_copies.append(c)
@@ -122,13 +123,13 @@
             quarter.append(jnp.where(core == 0, whole[:, 0:32], whole[:, 32:64]))
         both = jnp.concatenate(quarter, axis=1)
         for x in range(4):
-            cached_part[x, LAT_ROWS + m * PIECE : LAT_ROWS + (m + 1) * PIECE, :] = both[
+            cached_part[flipped[x], LAT_ROWS + m * PIECE : LAT_ROWS + (m + 1) * PIECE, :] = both[
                 x * PIECE : (x + 1) * PIECE, :
             ]
     for s in range(SEQS):
         c = pltpu.make_async_copy(
             cached_part.at[:, pl.ds(LAT_ROWS, ROPE_ROWS), :],
-            out.at[:, s, pl.ds(LAT_ROWS, ROPE_ROWS), :],
+            out.at[s, :, pl.ds(LAT_ROWS, ROPE_ROWS), :],
             out_sems.at[8 + s],
         )
         c.start()
@@ -161,7 +162,7 @@
         rank = counts[h]
         counts[h] = rank + 1
         ranks.append(jnp.minimum(rank, CAP - 1))
-        sources.append((h & 3) * 4 + (h >> 2))
+        sources.append((h >> 2) * 4 + (h & 1) * 2 + ((h >> 1) & 1))
     arrive.wait()
     for j in range(BLOCKS):
         rows = pl.ds(pl.multiple_of(ranks[j] * PIECE, PIECE), PIECE)
@@ -247,8 +248,8 @@
                     for tile in range(2):
                         at = tile * 64 + half * 32
                         col = (2 * i + tile) * LANES
-                        keys[y, half, part, :, col : col + LANES] = ref[part // 2, part % 2, y, at : at + 32, :]
-                    keys[y, half, part, rope_rows, 512:640] = ref[part // 2, part % 2, y, 128:144, :]
+                        keys[y, half, part, :, col : col + LANES] = ref[y, part % 2, part // 2, at : at + 32, :]
+                    keys[y, half, part, rope_rows, 512:640] = ref[y, part % 2, part // 2, 128:144, :]
     for c in query_copies:
         c.wait()
     for chunk in range(4):
@@ -412,7 +413,7 @@
     y = lax.axis_index("y")
     send = pl.pallas_call(
         pack_kernel,
-        out_shape=shape((4, SEQS, MSG_ROWS, LANES)),
+        out_shape=shape((SEQS, 4, MSG_ROWS, LANES)),
         in_specs=[anywhere()] * 6,
         out_specs=anywhere(),
         scratch_shapes=[
@@ -459,7 +460,7 @@
     )(block_owner, recv)
     picked, new_own, *queries = lax.optimization_barrier((picked, new_own, *queries))
     swap = [(0, 1), (1, 0)]
-    new_own = new_own.reshape(2, 2, 4, NEW_ROWS, LANES)
+    new_own = new_own.reshape(4, 2, 2, NEW_ROWS, LANES)
     new_other = lax.ppermute(new_own, "core", swap)
     cache_own = lax.all_to_all(picked, SPREAD, 0, 0).reshape(2, 2, 2, PICK_ROWS, LANES)
 

time: 72.4 us -> 72.2 us (level)
  waiting for transfers between devices: 14.8 us -> 15.6 us
    all_to_all x1, waiting for transfers between devices: 2.7 us -> 4.43 us  [on_device(): lax.all_to_all(picked, SPREAD, 0, 0).reshape(2, 2, 2, PICK_ROWS, LANES)]
    ppermute x1, starting transfers between devices: 4.39 us -> 2.94 us  [on_device(): cache_other = lax.ppermute(cache_own, 'core', swap)]
    all_to_all x1, starting transfers between devices: 5.54 us -> 6.73 us  [on_device(): lax.all_to_all(picked, SPREAD, 0, 0).reshape(2, 2, 2, PICK_ROWS, LANES)]
    all_to_all x1, waiting for transfers between devices: 6.37 us -> 5.24 us  [on_device(): recv = lax.all_to_all(send.reshape(16, MSG_ROWS, LANES), PLANE, 0, 0)]
  transfers between devices with their start and end apart: 7 -> 7, of which waited for: 5 -> 6; matrix products, arithmetic and copies ran while one was open for 0% -> 0% of each run, Pallas kernels for 10% -> 10%
where the time goes in v8:
time: 72.2 us; the launch traced here: 71.8 us
  starting transfers between devices  30.9 us (43%)
  waiting for transfers between devices  15.6 us (22%)
  Pallas kernels  15.5 us (21%)
  blocking collectives  8.81 us (12%)
  local copies, waits for them, and re-layouts  0.85 us (1%)
    ppermute x3, starting transfers between devices, on_device(): part = lax.ppermute(part, 'y', [(i, (i + k) % 4) for i in range(4)])  10.8 us
    all_to_all x1, blocking collectives, on_device(): return lax.all_to_all(mixed, 'y', 0, 0)  8.81 us
    all_to_all x1, starting transfers between devices, on_device(): recv = lax.all_to_all(send.reshape(16, MSG_ROWS, LANES), PLANE, 0, 0)  7.73 us
    all_to_all x1, starting transfers between devices, on_device(): lax.all_to_all(picked, SPREAD, 0, 0).reshape(2, 2, 2, PICK_ROWS, LANES)  6.73 us
    pallas_call x1, Pallas kernels, on_device(): pl.pallas_call(cached_kernel, out_shape=shape((4, TOK, 256)), in_specs=[s...  5.6 us
    all_to_all x1, waiting for transfers between devices, on_device(): recv = lax.all_to_all(send.reshape(16, MSG_ROWS, LANES), PLANE, 0, 0)  5.24 us
    all_to_all x1, waiting for transfers between devices, on_device(): lax.all_to_all(picked, SPREAD, 0, 0).reshape(2, 2, 2, PICK_ROWS, LANES)  4.43 us
    pallas_call x1, Pallas kernels, on_device(): pl.pallas_call(new_kernel, out_shape=(shape((8, rows), f32), shape((4, TO...  4.2 us
  transfers between devices with their start and end apart: 7, of which 6 were waited for; matrix products, arithmetic and copies ran while one was open for 0% of the time, Pallas kernels for 10%

profile of v8, /device:TPU:1, one launch (start us, length us, event | category | flops | bytes accessed | tf_op | source)
XLA Modules:
  0.0 71.8 jit_solution(16686028409072266884)
XLA Ops:
  0.0 2.5 %pack.1 = bf16[4,4,336,128]{3,2,1,0:T(8,128)(2,1)} custom-call(s32[4,24]{1,0:T(4,128)} %owner.3, s32[4,24]{1,0:T(4,128)} %slot.1, bf16[32,64,512]{2,1,0:T(8,128)(2,1)} %cache_latent.1, bf16[32,64,64]{2,1,0:T(8,128)(2,1)} %cache_rope.1, bf16[4,128,512]{2,1,0:T(8,128)(2,1)} %new_latent.1, bf16[4,64,128]{2,1,0:T(8,128)(2,1)} %bitcast.17), custom_call_target="tpu_custom_call" | custom-call | tf_op jit(solution)/shard_map/pack/pallas_call | solution.py:414
  2.5 0.0 copy-start.4
  2.5 7.7 %all-to-all-start = ((bf16[16,336,128]{2,1,0:T(8,128)(2,1)}), bf16[16,336,128]{2,1,0:T(8,128)(2,1)S(1)}, u32[]{:S(2)}, u32[]{:S(2)}) async-start(bf16[16,336,128]{2,1,0:T(8,128)(2,1)} %bitcast.16), calls=%async_computation | async-start | bytes 2752512 | tf_op jit(solution)/shard_map/all_to_all | solution.py:437
  10.2 0.0 copy-start.1
  10.4 0.1 dynamic-slice_bitcast_fusion
  10.4 3.3 %collective-permute-start = (bf16[128,384]{1,0:T(8,128)(2,1)S(1)}, bf16[128,384]{1,0:T(8,128)(2,1)S(1)}, u32[]{:S(2)}, u32[]{:S(2)}) collective-permute-start(bf16[128,384]{1,0:T(8,128)(2,1)S(1)} %get-tuple-element.47), channel_id=1, source_target_pairs={{0,128},{128,256},{256,384},{384,0},{1,129},{129,257},{257,385},{3... | collective-permute-start | bytes 294920 | tf_op jit(solution)/shard_map/ppermute | solution.py:443
  13.7 4.3 %collective-permute-start.1 = (bf16[128,384]{1,0:T(8,128)(2,1)S(1)}, bf16[128,384]{1,0:T(8,128)(2,1)S(1)}, u32[]{:S(2)}, u32[]{:S(2)}) collective-permute-start(bf16[128,384]{1,0:T(8,128)(2,1)S(1)} %get-tuple-element.46), channel_id=1, source_target_pairs={{0,256},{128,384},{256,0},{384,128},{1,257},{129,385},{257,1},{385... | collective-permute-start | bytes 294920 | tf_op jit(solution)/shard_map/ppermute | solution.py:443
  18.0 0.0 copy-start.2
  18.0 3.2 %collective-permute-start.2 = (bf16[128,384]{1,0:T(8,128)(2,1)S(1)}, bf16[128,384]{1,0:T(8,128)(2,1)S(1)}, u32[]{:S(2)}, u32[]{:S(2)}) collective-permute-start(bf16[128,384]{1,0:T(8,128)(2,1)S(1)} %get-tuple-element.45), channel_id=1, source_target_pairs={{0,384},{128,0},{256,128},{384,256},{1,385},{129,1},{257,129},{385... | collective-permute-start | bytes 294920 | tf_op jit(solution)/shard_map/ppermute | solution.py:443
  21.3 5.2 %all-to-all-done.recv = bf16[16,336,128]{2,1,0:T(8,128)(2,1)S(1)} async-done(((bf16[16,336,128]{2,1,0:T(8,128)(2,1)}), bf16[16,336,128]{2,1,0:T(8,128)(2,1)S(1)}, u32[]{:S(2)}, u32[]{:S(2)}) %all-to-all-start) | async-done | bytes 1376288 | tf_op jit(solution)/shard_map/all_to_all | solution.py:437
  26.5 2.1 %select.9 = (bf16[8,432,128]{2,1,0:T(8,128)(2,1)}, bf16[16,144,128]{2,1,0:T(8,128)(2,1)S(1)}) custom-call(s32[4,24]{1,0:T(4,128)S(1)} %copy-done.1, bf16[16,336,128]{2,1,0:T(8,128)(2,1)S(1)} %all-to-all-done.recv), custom_call_target="tpu_custom_call" | custom-call | tf_op jit(solution)/shard_map/select/pallas_call | solution.py:445
  28.6 0.2 collective-permute-done.q1
  28.8 3.1 %collective-permute-done.1.q2 = bf16[128,384]{1,0:T(8,128)(2,1)S(1)} collective-permute-done((bf16[128,384]{1,0:T(8,128)(2,1)S(1)}, bf16[128,384]{1,0:T(8,128)(2,1)S(1)}, u32[]{:S(2)}, u32[]{:S(2)}) %collective-permute-start.1) | collective-permute-done | bytes 98336 | tf_op jit(solution)/shard_map/ppermute | solution.py:443
  32.0 6.7 %all-to-all-start.1 = ((bf16[8,432,128]{2,1,0:T(8,128)(2,1)}), bf16[8,432,128]{2,1,0:T(8,128)(2,1)S(1)}, u32[]{:S(2)}, u32[]{:S(2)}) async-start(bf16[8,432,128]{2,1,0:T(8,128)(2,1)} %get-tuple-element.30), calls=%async_computation.1 | async-start | bytes 1769472 | tf_op jit(solution)/shard_map/all_to_all | solution.py:465
  38.7 2.7 %collective-permute-start.3 = (bf16[4,2,2,144,128]{4,3,2,1,0:T(8,128)(2,1)S(1)}, bf16[4,2,2,144,128]{4,3,2,1,0:T(8,128)(2,1)S(1)}, u32[]{:S(2)}, u32[]{:S(2)}) collective-permute-start(bf16[4,2,2,144,128]{4,3,2,1,0:T(8,128)(2,1)S(1)} %bitcast.14), channel_id=1, source_target_pairs={{0,2},{2,0},{1,3},{3,1},{4,6},{6,4},{5,7},{7,5},{8,10},{10,8},{9,1... | collective-permute-start | bytes 1769480 | tf_op jit(solution)/shard_map/ppermute | solution.py:464
  41.4 1.6 %collective-permute-done.3.other = bf16[4,2,2,144,128]{4,3,2,1,0:T(8,128)(2,1)S(1)} collective-permute-done((bf16[4,2,2,144,128]{4,3,2,1,0:T(8,128)(2,1)S(1)}, bf16[4,2,2,144,128]{4,3,2,1,0:T(8,128)(2,1)S(1)}, u32[]{:S(2)}, u32[]{:S(2)}) %collective-permute-start.3) | collective-permute-done | bytes 589856 | tf_op jit(solution)/shard_map/ppermute | solution.py:464
  43.0 4.2 %attend_new.1 = (f32[8,1024]{1,0:T(8,128)S(1)}, f32[4,128,256]{2,1,0:T(8,128)S(1)}, f32[8,128]{1,0:T(8,128)S(1)}) custom-call(bf16[128,384]{1,0:T(8,128)(2,1)S(1)} %get-tuple-element.37.q0, bf16[128,384]{1,0:T(8,128)(2,1)S(1)} %collective-permute-done.q1, bf16[128,384]{1,0:T(8,128)(2,1)S(1)} %collective-permute-done.1.q2, ...), custom_call_target="tpu_custom_call" | custom-call | flops 3000000000 | bytes 5000000 | tf_op jit(solution)/shard_map/attend_new/pallas_call | solution.py:468
  47.2 4.4 %all-to-all-done.1 = bf16[8,432,128]{2,1,0:T(8,128)(2,1)S(1)} async-done(((bf16[8,432,128]{2,1,0:T(8,128)(2,1)}), bf16[8,432,128]{2,1,0:T(8,128)(2,1)S(1)}, u32[]{:S(2)}, u32[]{:S(2)}) %all-to-all-start.1) | async-done | bytes 884768 | tf_op jit(solution)/shard_map/all_to_all | solution.py:465
  51.7 2.9 %collective-permute-start.4 = (bf16[2,2,2,432,128]{4,3,2,1,0:T(8,128)(2,1)S(1)}, bf16[2,2,2,432,128]{4,3,2,1,0:T(8,128)(2,1)S(1)}, u32[]{:S(2)}, u32[]{:S(2)}) collective-permute-start(bf16[2,2,2,432,128]{4,3,2,1,0:T(8,128)(2,1)S(1)} %bitcast.12), channel_id=1, source_target_pairs={{0,2},{2,0},{1,3},{3,1},{4,6},{6,4},{5,7},{7,5},{8,10},{10,8},{9,1... | collective-permute-start | bytes 2654216 | tf_op jit(solution)/shard_map/ppermute | solution.py:488
  54.6 1.1 %prepare.1.joint = bf16[1024,640]{1,0:T(8,128)(2,1)S(1)} custom-call(bf16[128,384]{1,0:T(8,128)(2,1)S(1)} %get-tuple-element.37.q0, bf16[128,384]{1,0:T(8,128)(2,1)S(1)} %collective-permute-done.q1, bf16[128,384]{1,0:T(8,128)(2,1)S(1)} %collective-permute-done.1.q2, bf16[128,384]{1,0:T(8,128)(2,1)S(1)} %collective-permute-done.2.q3, ...), custom_call_target="tpu_custom_call" | custom-call | flops 200000000 | bytes 2000000 | tf_op jit(solution)/shard_map/prepare/pallas_call | solution.py:489
  55.8 0.9 %collective-permute-done.4.other = bf16[2,2,2,432,128]{4,3,2,1,0:T(8,128)(2,1)S(1)} collective-permute-done((bf16[2,2,2,432,128]{4,3,2,1,0:T(8,128)(2,1)S(1)}, bf16[2,2,2,432,128]{4,3,2,1,0:T(8,128)(2,1)S(1)}, u32[]{:S(2)}, u32[]{:S(2)}) %collective-permute-start.4) | collective-permute-done | bytes 884768 | tf_op jit(solution)/shard_map/ppermute | solution.py:488
  56.7 5.6 %attend_cached.1 = bf16[4,128,256]{2,1,0:T(8,128)(2,1)S(1)} custom-call(s32[4]{0:T(128)S(1)} %copy-done.3, bf16[1024,640]{1,0:T(8,128)(2,1)S(1)} %prepare.1.joint, bf16[2,512,128]{2,1,0:T(8,128)(2,1)S(1)} %copy-done.2, bf16[2,2,2,432,128]{4,3,2,1,0:T(8,128)(2,1)S(1)} %bitcast.13, bf16[2,2,2,432,128]{4,3,2,1,0:T(8,128)(2,1)S(1)} %collective-permute-done.4.other, ...), custom_call_target="tpu_custom_call" | custom-call | flops 4000000000 | bytes 5000000 | tf_op jit(solution)/shard_map/attend_cached/pallas_call | solution.py:499
  62.3 8.8 %all_to_all.15 = bf16[4,128,256]{2,1,0:T(8,128)(2,1)S(1)} all-to-all(bf16[4,128,256]{2,1,0:T(8,128)(2,1)S(1)} %attend_cached.1), channel_id=1, replica_groups=mesh['y'=4,'xh'=2,'zh'=8,'zp'=2,'core'=2,'xl'=2] {'y'}, dimensions={0} | all-to-all | bytes 524288 | tf_op jit(solution)/shard_map/all_to_all | solution.py:511
  71.1 0.7 copy.14
  (12 shorter events, 0.1 us)
Async XLA Ops:
  2.5 7.8 %copy-start.4 = (bf16[4,128,256]{2,1,0:T(8,128)(2,1)S(1)}, bf16[4,128,256]{2,1,0:T(8,128)(2,1)}, u32[]{:S(2)}) copy-start(bf16[4,128,256]{2,1,0:T(8,128)(2,1)} %param.11) | copy-start | bytes 786436
  2.5 7.8 %copy-start.5 = (bf16[4,128,128]{2,1,0:T(8,128)(2,1)S(1)}, bf16[4,128,128]{2,1,0:T(8,128)(2,1)}, u32[]{:S(2)}) copy-start(bf16[4,128,128]{2,1,0:T(8,128)(2,1)} %param.12) | copy-start | bytes 393220
  2.5 24.0 %all-to-all-start = ((bf16[16,336,128]{2,1,0:T(8,128)(2,1)}), bf16[16,336,128]{2,1,0:T(8,128)(2,1)S(1)}, u32[]{:S(2)}, u32[]{:S(2)}) async-start(bf16[16,336,128]{2,1,0:T(8,128)(2,1)} %bitcast.16), calls=%async_computation | async-start | bytes 2752512 | tf_op jit(solution)/shard_map/all_to_all | solution.py:437
  10.2 16.3 %copy-start.1 = (s32[4,24]{1,0:T(4,128)S(1)}, s32[4,24]{1,0:T(4,128)}, u32[]{:S(2)}) copy-start(s32[4,24]{1,0:T(4,128)} %owner.3) | copy-start | bytes 1156
  10.4 18.4 %collective-permute-start = (bf16[128,384]{1,0:T(8,128)(2,1)S(1)}, bf16[128,384]{1,0:T(8,128)(2,1)S(1)}, u32[]{:S(2)}, u32[]{:S(2)}) collective-permute-start(bf16[128,384]{1,0:T(8,128)(2,1)S(1)} %get-tuple-element.47), channel_id=1, source_target_pairs={{0,128},{128,256},{256,384},{384,0},{1,129},{129,257},{257,385},{3... | collective-permute-start | bytes 294920 | tf_op jit(solution)/shard_map/ppermute | solution.py:443
  13.7 18.3 %collective-permute-start.1 = (bf16[128,384]{1,0:T(8,128)(2,1)S(1)}, bf16[128,384]{1,0:T(8,128)(2,1)S(1)}, u32[]{:S(2)}, u32[]{:S(2)}) collective-permute-start(bf16[128,384]{1,0:T(8,128)(2,1)S(1)} %get-tuple-element.46), channel_id=1, source_target_pairs={{0,256},{128,384},{256,0},{384,128},{1,257},{129,385},{257,1},{385... | collective-permute-start | bytes 294920 | tf_op jit(solution)/shard_map/ppermute | solution.py:443
  18.0 25.0 %copy-start = (bf16[2,128,512]{2,1,0:T(8,128)(2,1)S(1)}, bf16[2,128,512]{2,1,0:T(8,128)(2,1)}, u32[]{:S(2)}) copy-start(bf16[2,128,512]{2,1,0:T(8,128)(2,1)} %key_up.3) | copy-start | bytes 786436
  18.0 25.0 %copy-start.2 = (bf16[2,512,128]{2,1,0:T(8,128)(2,1)S(1)}, bf16[2,512,128]{2,1,0:T(8,128)(2,1)}, u32[]{:S(2)}) copy-start(bf16[2,512,128]{2,1,0:T(8,128)(2,1)} %value_up.3) | copy-start | bytes 786436
  18.0 14.0 %collective-permute-start.2 = (bf16[128,384]{1,0:T(8,128)(2,1)S(1)}, bf16[128,384]{1,0:T(8,128)(2,1)S(1)}, u32[]{:S(2)}, u32[]{:S(2)}) collective-permute-start(bf16[128,384]{1,0:T(8,128)(2,1)S(1)} %get-tuple-element.45), channel_id=1, source_target_pairs={{0,384},{128,0},{256,128},{384,256},{1,385},{129,1},{257,129},{385... | collective-permute-start | bytes 294920 | tf_op jit(solution)/shard_map/ppermute | solution.py:443
  32.0 19.7 %all-to-all-start.1 = ((bf16[8,432,128]{2,1,0:T(8,128)(2,1)}), bf16[8,432,128]{2,1,0:T(8,128)(2,1)S(1)}, u32[]{:S(2)}, u32[]{:S(2)}) async-start(bf16[8,432,128]{2,1,0:T(8,128)(2,1)} %get-tuple-element.30), calls=%async_computation.1 | async-start | bytes 1769472 | tf_op jit(solution)/shard_map/all_to_all | solution.py:465
  38.7 4.3 %collective-permute-start.3 = (bf16[4,2,2,144,128]{4,3,2,1,0:T(8,128)(2,1)S(1)}, bf16[4,2,2,144,128]{4,3,2,1,0:T(8,128)(2,1)S(1)}, u32[]{:S(2)}, u32[]{:S(2)}) collective-permute-start(bf16[4,2,2,144,128]{4,3,2,1,0:T(8,128)(2,1)S(1)} %bitcast.14), channel_id=1, source_target_pairs={{0,2},{2,0},{1,3},{3,1},{4,6},{6,4},{5,7},{7,5},{8,10},{10,8},{9,1... | collective-permute-start | bytes 1769480 | tf_op jit(solution)/shard_map/ppermute | solution.py:464
  47.2 9.4 %copy-start.3 = (s32[4]{0:T(128)S(1)}, s32[4]{0:T(128)}, u32[]{:S(2)}) copy-start(s32[4]{0:T(128)} %cached_len.1) | copy-start | bytes 52
  51.7 5.0 %collective-permute-start.4 = (bf16[2,2,2,432,128]{4,3,2,1,0:T(8,128)(2,1)S(1)}, bf16[2,2,2,432,128]{4,3,2,1,0:T(8,128)(2,1)S(1)}, u32[]{:S(2)}, u32[]{:S(2)}) collective-permute-start(bf16[2,2,2,432,128]{4,3,2,1,0:T(8,128)(2,1)S(1)} %bitcast.12), channel_id=1, source_target_pairs={{0,2},{2,0},{1,3},{3,1},{4,6},{6,4},{5,7},{7,5},{8,10},{10,8},{9,1... | collective-permute-start | bytes 2654216 | tf_op jit(solution)/shard_map/ppermute | solution.py:488

commit v9 on v8

--- a/solution.py
+++ b/solution.py
@@ -145,7 +145,6 @@
     new_copy = pltpu.make_async_copy(
         recv.at[:, pl.ds(NEW_AT, NEW_ROWS), :], new_out, sems.at[1]
     )
-    new_copy.start()
     for h in range(16):
         counts[h] = 0
 
@@ -164,6 +163,7 @@
         ranks.append(jnp.minimum(rank, CAP - 1))
         sources.append((h >> 2) * 4 + (h & 1) * 2 + ((h >> 1) & 1))
     arrive.wait()
+    new_copy.start()
     for j in range(BLOCKS):
         rows = pl.ds(pl.multiple_of(ranks[j] * PIECE, PIECE), PIECE)
         picked[j * PIECE : (j + 1) * PIECE, :] = cached[sources[j], rows, :]

time: 72.2 us -> 72.2 us (level)
  no operation moved by 1% of the time
where the time goes in v9:
time: 72.2 us; the launch traced here: 71.8 us
  starting transfers between devices  30.9 us (43%)
  waiting for transfers between devices  15.6 us (22%)
  Pallas kernels  15.5 us (21%)
  blocking collectives  8.81 us (12%)
  local copies, waits for them, and re-layouts  0.85 us (1%)
    ppermute x3, starting transfers between devices, on_device(): part = lax.ppermute(part, 'y', [(i, (i + k) % 4) for i in range(4)])  10.8 us
    all_to_all x1, blocking collectives, on_device(): return lax.all_to_all(mixed, 'y', 0, 0)  8.81 us
    all_to_all x1, starting transfers between devices, on_device(): recv = lax.all_to_all(send.reshape(16, MSG_ROWS, LANES), PLANE, 0, 0)  7.73 us
    all_to_all x1, starting transfers between devices, on_device(): lax.all_to_all(picked, SPREAD, 0, 0).reshape(2, 2, 2, PICK_ROWS, LANES)  6.73 us
    pallas_call x1, Pallas kernels, on_device(): pl.pallas_call(cached_kernel, out_shape=shape((4, TOK, 256)), in_specs=[s...  5.6 us
    all_to_all x1, waiting for transfers between devices, on_device(): recv = lax.all_to_all(send.reshape(16, MSG_ROWS, LANES), PLANE, 0, 0)  5.24 us
    all_to_all x1, waiting for transfers between devices, on_device(): lax.all_to_all(picked, SPREAD, 0, 0).reshape(2, 2, 2, PICK_ROWS, LANES)  4.43 us
    pallas_call x1, Pallas kernels, on_device(): pl.pallas_call(new_kernel, out_shape=(shape((8, rows), f32), shape((4, TO...  4.2 us
  transfers between devices with their start and end apart: 7, of which 6 were waited for; matrix products, arithmetic and copies ran while one was open for 0% of the time, Pallas kernels for 10%

profile of v9, /device:TPU:1, one launch (start us, length us, event | category | flops | bytes accessed | tf_op | source)
XLA Modules:
  0.0 71.8 jit_solution(7527935862223540226)
XLA Ops:
  0.0 2.5 %pack.1 = bf16[4,4,336,128]{3,2,1,0:T(8,128)(2,1)} custom-call(s32[4,24]{1,0:T(4,128)} %owner.3, s32[4,24]{1,0:T(4,128)} %slot.1, bf16[32,64,512]{2,1,0:T(8,128)(2,1)} %cache_latent.1, bf16[32,64,64]{2,1,0:T(8,128)(2,1)} %cache_rope.1, bf16[4,128,512]{2,1,0:T(8,128)(2,1)} %new_latent.1, bf16[4,64,128]{2,1,0:T(8,128)(2,1)} %bitcast.17), custom_call_target="tpu_custom_call" | custom-call | tf_op jit(solution)/shard_map/pack/pallas_call | solution.py:414
  2.5 0.0 copy-start.4
  2.5 7.7 %all-to-all-start = ((bf16[16,336,128]{2,1,0:T(8,128)(2,1)}), bf16[16,336,128]{2,1,0:T(8,128)(2,1)S(1)}, u32[]{:S(2)}, u32[]{:S(2)}) async-start(bf16[16,336,128]{2,1,0:T(8,128)(2,1)} %bitcast.16), calls=%async_computation | async-start | bytes 2752512 | tf_op jit(solution)/shard_map/all_to_all | solution.py:437
  10.2 0.0 copy-start.1
  10.4 0.1 dynamic-slice_bitcast_fusion
  10.4 3.3 %collective-permute-start = (bf16[128,384]{1,0:T(8,128)(2,1)S(1)}, bf16[128,384]{1,0:T(8,128)(2,1)S(1)}, u32[]{:S(2)}, u32[]{:S(2)}) collective-permute-start(bf16[128,384]{1,0:T(8,128)(2,1)S(1)} %get-tuple-element.47), channel_id=1, source_target_pairs={{0,128},{128,256},{256,384},{384,0},{1,129},{129,257},{257,385},{3... | collective-permute-start | bytes 294920 | tf_op jit(solution)/shard_map/ppermute | solution.py:443
  13.7 4.3 %collective-permute-start.1 = (bf16[128,384]{1,0:T(8,128)(2,1)S(1)}, bf16[128,384]{1,0:T(8,128)(2,1)S(1)}, u32[]{:S(2)}, u32[]{:S(2)}) collective-permute-start(bf16[128,384]{1,0:T(8,128)(2,1)S(1)} %get-tuple-element.46), channel_id=1, source_target_pairs={{0,256},{128,384},{256,0},{384,128},{1,257},{129,385},{257,1},{385... | collective-permute-start | bytes 294920 | tf_op jit(solution)/shard_map/ppermute | solution.py:443
  18.0 0.0 copy-start.2
  18.0 3.2 %collective-permute-start.2 = (bf16[128,384]{1,0:T(8,128)(2,1)S(1)}, bf16[128,384]{1,0:T(8,128)(2,1)S(1)}, u32[]{:S(2)}, u32[]{:S(2)}) collective-permute-start(bf16[128,384]{1,0:T(8,128)(2,1)S(1)} %get-tuple-element.45), channel_id=1, source_target_pairs={{0,384},{128,0},{256,128},{384,256},{1,385},{129,1},{257,129},{385... | collective-permute-start | bytes 294920 | tf_op jit(solution)/shard_map/ppermute | solution.py:443
  21.3 5.2 %all-to-all-done.recv = bf16[16,336,128]{2,1,0:T(8,128)(2,1)S(1)} async-done(((bf16[16,336,128]{2,1,0:T(8,128)(2,1)}), bf16[16,336,128]{2,1,0:T(8,128)(2,1)S(1)}, u32[]{:S(2)}, u32[]{:S(2)}) %all-to-all-start) | async-done | bytes 1376288 | tf_op jit(solution)/shard_map/all_to_all | solution.py:437
  26.5 2.1 %select.9 = (bf16[8,432,128]{2,1,0:T(8,128)(2,1)}, bf16[16,144,128]{2,1,0:T(8,128)(2,1)S(1)}) custom-call(s32[4,24]{1,0:T(4,128)S(1)} %copy-done.1, bf16[16,336,128]{2,1,0:T(8,128)(2,1)S(1)} %all-to-all-done.recv), custom_call_target="tpu_custom_call" | custom-call | tf_op jit(solution)/shard_map/select/pallas_call | solution.py:445
  28.6 0.2 collective-permute-done.q1
  28.8 3.1 %collective-permute-done.1.q2 = bf16[128,384]{1,0:T(8,128)(2,1)S(1)} collective-permute-done((bf16[128,384]{1,0:T(8,128)(2,1)S(1)}, bf16[128,384]{1,0:T(8,128)(2,1)S(1)}, u32[]{:S(2)}, u32[]{:S(2)}) %collective-permute-start.1) | collective-permute-done | bytes 98336 | tf_op jit(solution)/shard_map/ppermute | solution.py:443
  32.0 6.7 %all-to-all-start.1 = ((bf16[8,432,128]{2,1,0:T(8,128)(2,1)}), bf16[8,432,128]{2,1,0:T(8,128)(2,1)S(1)}, u32[]{:S(2)}, u32[]{:S(2)}) async-start(bf16[8,432,128]{2,1,0:T(8,128)(2,1)} %get-tuple-element.30), calls=%async_computation.1 | async-start | bytes 1769472 | tf_op jit(solution)/shard_map/all_to_all | solution.py:465
  38.7 2.7 %collective-permute-start.3 = (bf16[4,2,2,144,128]{4,3,2,1,0:T(8,128)(2,1)S(1)}, bf16[4,2,2,144,128]{4,3,2,1,0:T(8,128)(2,1)S(1)}, u32[]{:S(2)}, u32[]{:S(2)}) collective-permute-start(bf16[4,2,2,144,128]{4,3,2,1,0:T(8,128)(2,1)S(1)} %bitcast.14), channel_id=1, source_target_pairs={{0,2},{2,0},{1,3},{3,1},{4,6},{6,4},{5,7},{7,5},{8,10},{10,8},{9,1... | collective-permute-start | bytes 1769480 | tf_op jit(solution)/shard_map/ppermute | solution.py:464
  41.4 1.6 %collective-permute-done.3.other = bf16[4,2,2,144,128]{4,3,2,1,0:T(8,128)(2,1)S(1)} collective-permute-done((bf16[4,2,2,144,128]{4,3,2,1,0:T(8,128)(2,1)S(1)}, bf16[4,2,2,144,128]{4,3,2,1,0:T(8,128)(2,1)S(1)}, u32[]{:S(2)}, u32[]{:S(2)}) %collective-permute-start.3) | collective-permute-done | bytes 589856 | tf_op jit(solution)/shard_map/ppermute | solution.py:464
  43.0 4.2 %attend_new.1 = (f32[8,1024]{1,0:T(8,128)S(1)}, f32[4,128,256]{2,1,0:T(8,128)S(1)}, f32[8,128]{1,0:T(8,128)S(1)}) custom-call(bf16[128,384]{1,0:T(8,128)(2,1)S(1)} %get-tuple-element.37.q0, bf16[128,384]{1,0:T(8,128)(2,1)S(1)} %collective-permute-done.q1, bf16[128,384]{1,0:T(8,128)(2,1)S(1)} %collective-permute-done.1.q2, ...), custom_call_target="tpu_custom_call" | custom-call | flops 3000000000 | bytes 5000000 | tf_op jit(solution)/shard_map/attend_new/pallas_call | solution.py:468
  47.2 4.4 %all-to-all-done.1 = bf16[8,432,128]{2,1,0:T(8,128)(2,1)S(1)} async-done(((bf16[8,432,128]{2,1,0:T(8,128)(2,1)}), bf16[8,432,128]{2,1,0:T(8,128)(2,1)S(1)}, u32[]{:S(2)}, u32[]{:S(2)}) %all-to-all-start.1) | async-done | bytes 884768 | tf_op jit(solution)/shard_map/all_to_all | solution.py:465
  51.7 2.9 %collective-permute-start.4 = (bf16[2,2,2,432,128]{4,3,2,1,0:T(8,128)(2,1)S(1)}, bf16[2,2,2,432,128]{4,3,2,1,0:T(8,128)(2,1)S(1)}, u32[]{:S(2)}, u32[]{:S(2)}) collective-permute-start(bf16[2,2,2,432,128]{4,3,2,1,0:T(8,128)(2,1)S(1)} %bitcast.12), channel_id=1, source_target_pairs={{0,2},{2,0},{1,3},{3,1},{4,6},{6,4},{5,7},{7,5},{8,10},{10,8},{9,1... | collective-permute-start | bytes 2654216 | tf_op jit(solution)/shard_map/ppermute | solution.py:488
  54.6 1.1 %prepare.1.joint = bf16[1024,640]{1,0:T(8,128)(2,1)S(1)} custom-call(bf16[128,384]{1,0:T(8,128)(2,1)S(1)} %get-tuple-element.37.q0, bf16[128,384]{1,0:T(8,128)(2,1)S(1)} %collective-permute-done.q1, bf16[128,384]{1,0:T(8,128)(2,1)S(1)} %collective-permute-done.1.q2, bf16[128,384]{1,0:T(8,128)(2,1)S(1)} %collective-permute-done.2.q3, ...), custom_call_target="tpu_custom_call" | custom-call | flops 200000000 | bytes 2000000 | tf_op jit(solution)/shard_map/prepare/pallas_call | solution.py:489
  55.8 0.9 %collective-permute-done.4.other = bf16[2,2,2,432,128]{4,3,2,1,0:T(8,128)(2,1)S(1)} collective-permute-done((bf16[2,2,2,432,128]{4,3,2,1,0:T(8,128)(2,1)S(1)}, bf16[2,2,2,432,128]{4,3,2,1,0:T(8,128)(2,1)S(1)}, u32[]{:S(2)}, u32[]{:S(2)}) %collective-permute-start.4) | collective-permute-done | bytes 884768 | tf_op jit(solution)/shard_map/ppermute | solution.py:488
  56.7 5.6 %attend_cached.1 = bf16[4,128,256]{2,1,0:T(8,128)(2,1)S(1)} custom-call(s32[4]{0:T(128)S(1)} %copy-done.3, bf16[1024,640]{1,0:T(8,128)(2,1)S(1)} %prepare.1.joint, bf16[2,512,128]{2,1,0:T(8,128)(2,1)S(1)} %copy-done.2, bf16[2,2,2,432,128]{4,3,2,1,0:T(8,128)(2,1)S(1)} %bitcast.13, bf16[2,2,2,432,128]{4,3,2,1,0:T(8,128)(2,1)S(1)} %collective-permute-done.4.other, ...), custom_call_target="tpu_custom_call" | custom-call | flops 4000000000 | bytes 5000000 | tf_op jit(solution)/shard_map/attend_cached/pallas_call | solution.py:499
  62.3 8.8 %all_to_all.15 = bf16[4,128,256]{2,1,0:T(8,128)(2,1)S(1)} all-to-all(bf16[4,128,256]{2,1,0:T(8,128)(2,1)S(1)} %attend_cached.1), channel_id=1, replica_groups=mesh['y'=4,'xh'=2,'zh'=8,'zp'=2,'core'=2,'xl'=2] {'y'}, dimensions={0} | all-to-all | bytes 524288 | tf_op jit(solution)/shard_map/all_to_all | solution.py:511
  71.1 0.7 copy.14
  (12 shorter events, 0.1 us)
Async XLA Ops:
  2.5 7.8 %copy-start.4 = (bf16[4,128,256]{2,1,0:T(8,128)(2,1)S(1)}, bf16[4,128,256]{2,1,0:T(8,128)(2,1)}, u32[]{:S(2)}) copy-start(bf16[4,128,256]{2,1,0:T(8,128)(2,1)} %param.11) | copy-start | bytes 786436
  2.5 7.8 %copy-start.5 = (bf16[4,128,128]{2,1,0:T(8,128)(2,1)S(1)}, bf16[4,128,128]{2,1,0:T(8,128)(2,1)}, u32[]{:S(2)}) copy-start(bf16[4,128,128]{2,1,0:T(8,128)(2,1)} %param.12) | copy-start | bytes 393220
  2.5 24.0 %all-to-all-start = ((bf16[16,336,128]{2,1,0:T(8,128)(2,1)}), bf16[16,336,128]{2,1,0:T(8,128)(2,1)S(1)}, u32[]{:S(2)}, u32[]{:S(2)}) async-start(bf16[16,336,128]{2,1,0:T(8,128)(2,1)} %bitcast.16), calls=%async_computation | async-start | bytes 2752512 | tf_op jit(solution)/shard_map/all_to_all | solution.py:437
  10.2 16.3 %copy-start.1 = (s32[4,24]{1,0:T(4,128)S(1)}, s32[4,24]{1,0:T(4,128)}, u32[]{:S(2)}) copy-start(s32[4,24]{1,0:T(4,128)} %owner.3) | copy-start | bytes 1156
  10.4 18.4 %collective-permute-start = (bf16[128,384]{1,0:T(8,128)(2,1)S(1)}, bf16[128,384]{1,0:T(8,128)(2,1)S(1)}, u32[]{:S(2)}, u32[]{:S(2)}) collective-permute-start(bf16[128,384]{1,0:T(8,128)(2,1)S(1)} %get-tuple-element.47), channel_id=1, source_target_pairs={{0,128},{128,256},{256,384},{384,0},{1,129},{129,257},{257,385},{3... | collective-permute-start | bytes 294920 | tf_op jit(solution)/shard_map/ppermute | solution.py:443
  13.7 18.3 %collective-permute-start.1 = (bf16[128,384]{1,0:T(8,128)(2,1)S(1)}, bf16[128,384]{1,0:T(8,128)(2,1)S(1)}, u32[]{:S(2)}, u32[]{:S(2)}) collective-permute-start(bf16[128,384]{1,0:T(8,128)(2,1)S(1)} %get-tuple-element.46), channel_id=1, source_target_pairs={{0,256},{128,384},{256,0},{384,128},{1,257},{129,385},{257,1},{385... | collective-permute-start | bytes 294920 | tf_op jit(solution)/shard_map/ppermute | solution.py:443
  18.0 25.0 %copy-start = (bf16[2,128,512]{2,1,0:T(8,128)(2,1)S(1)}, bf16[2,128,512]{2,1,0:T(8,128)(2,1)}, u32[]{:S(2)}) copy-start(bf16[2,128,512]{2,1,0:T(8,128)(2,1)} %key_up.3) | copy-start | bytes 786436
  18.0 25.0 %copy-start.2 = (bf16[2,512,128]{2,1,0:T(8,128)(2,1)S(1)}, bf16[2,512,128]{2,1,0:T(8,128)(2,1)}, u32[]{:S(2)}) copy-start(bf16[2,512,128]{2,1,0:T(8,128)(2,1)} %value_up.3) | copy-start | bytes 786436
  18.0 14.0 %collective-permute-start.2 = (bf16[128,384]{1,0:T(8,128)(2,1)S(1)}, bf16[128,384]{1,0:T(8,128)(2,1)S(1)}, u32[]{:S(2)}, u32[]{:S(2)}) collective-permute-start(bf16[128,384]{1,0:T(8,128)(2,1)S(1)} %get-tuple-element.45), channel_id=1, source_target_pairs={{0,384},{128,0},{256,128},{384,256},{1,385},{129,1},{257,129},{385... | collective-permute-start | bytes 294920 | tf_op jit(solution)/shard_map/ppermute | solution.py:443
  32.0 19.7 %all-to-all-start.1 = ((bf16[8,432,128]{2,1,0:T(8,128)(2,1)}), bf16[8,432,128]{2,1,0:T(8,128)(2,1)S(1)}, u32[]{:S(2)}, u32[]{:S(2)}) async-start(bf16[8,432,128]{2,1,0:T(8,128)(2,1)} %get-tuple-element.30), calls=%async_computation.1 | async-start | bytes 1769472 | tf_op jit(solution)/shard_map/all_to_all | solution.py:465
  38.7 4.3 %collective-permute-start.3 = (bf16[4,2,2,144,128]{4,3,2,1,0:T(8,128)(2,1)S(1)}, bf16[4,2,2,144,128]{4,3,2,1,0:T(8,128)(2,1)S(1)}, u32[]{:S(2)}, u32[]{:S(2)}) collective-permute-start(bf16[4,2,2,144,128]{4,3,2,1,0:T(8,128)(2,1)S(1)} %bitcast.14), channel_id=1, source_target_pairs={{0,2},{2,0},{1,3},{3,1},{4,6},{6,4},{5,7},{7,5},{8,10},{10,8},{9,1... | collective-permute-start | bytes 1769480 | tf_op jit(solution)/shard_map/ppermute | solution.py:464
  47.2 9.4 %copy-start.3 = (s32[4]{0:T(128)S(1)}, s32[4]{0:T(128)}, u32[]{:S(2)}) copy-start(s32[4]{0:T(128)} %cached_len.1) | copy-start | bytes 52
  51.7 5.0 %collective-permute-start.4 = (bf16[2,2,2,432,128]{4,3,2,1,0:T(8,128)(2,1)S(1)}, bf16[2,2,2,432,128]{4,3,2,1,0:T(8,128)(2,1)S(1)}, u32[]{:S(2)}, u32[]{:S(2)}) collective-permute-start(bf16[2,2,2,432,128]{4,3,2,1,0:T(8,128)(2,1)S(1)} %bitcast.12), channel_id=1, source_target_pairs={{0,2},{2,0},{1,3},{3,1},{4,6},{6,4},{5,7},{7,5},{8,10},{10,8},{9,1... | collective-permute-start | bytes 2654216 | tf_op jit(solution)/shard_map/ppermute | solution.py:488
